TPU v7x, 32 devices: a whole 2x2x4 slice. The times are simulated.
32 devices in a mesh: row: 4 (over y, x), col: 8 (over z, core).
Axes of the slice: x: 2, y: 2, z: 4, core: 2. Of those that a mesh axis runs over, the one named last changes fastest.
Arguments:
- tokens: bfloat16 [512, 6144], P('row', 'col'), may hold values from -6 to 6
- w_query: bfloat16 [6144, 1024], P('row', 'col'), may hold values from -0.078125 to 0.078125
- w_key: bfloat16 [6144, 1024], P('row', 'col'), may hold values from -0.078125 to 0.078125
- w_value: bfloat16 [6144, 1024], P('row', 'col'), may hold values from -0.078125 to 0.078125
- w_out: bfloat16 [1024, 6144], P('row', 'col'), may hold values from -0.1875 to 0.1875
- key_cache: bfloat16 [8192, 1024], P('row', 'col'), may hold values from -6 to 6
- value_cache: bfloat16 [8192, 1024], P('row', 'col'), may hold values from -6 to 6
- query_gain: float32 [128], replicated, may hold values from 1 to 2.5
- key_gain: float32 [128], replicated, may hold values from 1 to 2.5
- out_gate: float32 [6144], P('col'), may hold values from 0.5 to 2
- cotangent: bfloat16 [512, 6144], P('row', 'col'), may hold values from -6 to 6
Outputs:
- layer_out: bfloat16 [512, 6144], P('row', 'col')
- attention_cotangent: bfloat16 [512, 1024], P('row', 'col')
All inputs are finite; a program needn't handle non-finite values.
Results may differ from a plain program's by a relative error of at most 0.012.
Values may be sent and summed in bfloat16 or wider, within the bound.
No kernel may reach another device: no remote copies, remote signals or barrier semaphores. Data moves between devices by JAX's collectives and lax.ppermute only.
A program may use at most 64 MiB of HBM per device.

v0:
```python
import jax
import jax.numpy as jnp
from jax import lax
from jax.sharding import PartitionSpec as P

epsilon = 1e-06


def norm_heads(values, gain):
    wide = values.astype(jnp.float32)
    mean_square = jnp.mean(wide * wide, axis=-1, keepdims=True)
    return (wide * lax.rsqrt(mean_square + epsilon) * gain).astype(jnp.bfloat16)


def body(
    tokens,
    w_query,
    w_key,
    w_value,
    w_out,
    key_cache,
    value_cache,
    query_gain,
    key_gain,
    out_gate,
    cotangent,
):
    tok_rows = tokens.shape[0]
    head_size = query_gain.shape[0]
    local_width = w_query.shape[1]
    heads_here = local_width // head_size
    scale = head_size ** (-0.5)
    features_whole = lax.all_gather(tokens, "col", axis=1, tiled=True)
    pieces = (
        lax.all_gather(w_query, "row", axis=0, tiled=True),
        lax.all_gather(w_key, "row", axis=0, tiled=True),
        lax.all_gather(w_value, "row", axis=0, tiled=True),
    )
    proj_query, proj_key, proj_value = tuple(
        (jnp.dot(features_whole, piece, preferred_element_type=jnp.float32) for piece in pieces)
    )
    query_norm = norm_heads(
        proj_query.astype(jnp.bfloat16).reshape(tok_rows, heads_here, head_size), query_gain
    ).reshape(tok_rows, local_width)
    keys_local = jnp.concatenate([key_cache, proj_key.astype(jnp.bfloat16)], axis=0)
    key_norm = norm_heads(keys_local.reshape(-1, heads_here, head_size), key_gain)
    values_local = jnp.concatenate([value_cache, proj_value.astype(jnp.bfloat16)], axis=0).reshape(
        -1, heads_here, head_size
    )
    queries = lax.all_gather(query_norm, "row", axis=0, tiled=True)
    total_rows = queries.shape[0]
    block_rows = min(512, total_rows)
    query_blocks = queries.reshape(total_rows // block_rows, block_rows, heads_here, head_size)

    def attend(query_block):
        scores = (
            jnp.einsum("qhd,khd->hqk", query_block, key_norm, preferred_element_type=jnp.float32)
            * scale
        )
        weights = jnp.exp(scores)
        sums_here = jnp.sum(weights, axis=2)
        numerators = jnp.einsum(
            "hqk,khd->qhd",
            weights.astype(jnp.bfloat16),
            values_local,
            preferred_element_type=jnp.float32,
        )
        return (numerators, sums_here.T)

    numerators, sums_local = lax.map(attend, query_blocks)
    numerators = numerators.reshape(total_rows, local_width)
    sums_local = sums_local.reshape(total_rows, heads_here)
    numer_mine, sums_mine = (
        lax.psum_scatter(numerators, "row", scatter_dimension=0, tiled=True),
        lax.psum_scatter(sums_local, "row", scatter_dimension=0, tiled=True),
    )
    attention = (
        (numer_mine.reshape(tok_rows, heads_here, head_size) / sums_mine[:, :, None])
        .astype(jnp.bfloat16)
        .reshape(tok_rows, local_width)
    )
    attention_whole = lax.all_gather(attention, "col", axis=1, tiled=True)
    scaled = (cotangent.astype(jnp.float32) * out_gate).astype(jnp.bfloat16)
    contract_last = (((1,), (1,)), ((), ()))
    output_whole = lax.all_gather(w_out, "row", axis=0, tiled=True)
    branch = jnp.dot(attention_whole, output_whole, preferred_element_type=jnp.float32)
    head_rows = lax.all_to_all(output_whole, "col", split_axis=0, concat_axis=1, tiled=True)
    scaled_whole = lax.all_gather(scaled, "col", axis=1, tiled=True)
    attention_cotangent = lax.dot_general(
        scaled_whole, head_rows, contract_last, preferred_element_type=jnp.float32
    ).astype(jnp.bfloat16)
    layer_out = (tokens.astype(jnp.float32) + out_gate * branch).astype(jnp.bfloat16)
    return (layer_out, attention_cotangent)


def solution(mesh):
    placed = (
        P("row", "col"),
        P("row", "col"),
        P("row", "col"),
        P("row", "col"),
        P("row", "col"),
        P("row", "col"),
        P("row", "col"),
        P(),
        P(),
        P("col"),
        P("row", "col"),
    )
    return jax.shard_map(
        body,
        mesh=mesh,
        in_specs=placed,
        out_specs=(P("row", "col"), P("row", "col")),
        check_vma=False,
    )
```

profile of v0, /device:TPU:0, one launch (start us, length us, event | category | flops | bytes accessed | tf_op | source)
XLA Modules:
  0.0 258.2 jit_solution(3797672866346747954)
XLA Ops:
  7.2 0.0 all-gather.11.cloned.1.call-start
  7.2 0.7 all-gather.11.cloned.1.call-update
  7.9 0.0 all-gather.7.cloned.1.call-start
  7.9 0.7 all-gather.7.cloned.1.call-update
  8.6 0.0 all-gather.13.cloned.1.call-start
  8.7 0.7 all-gather.13.cloned.1.call-update
  9.4 0.0 all-gather.9.cloned.1.call-start
  9.4 0.5 all-gather.9.cloned.1.call-update
  10.0 0.0 all-gather.15.cloned.1.call-start
  10.0 0.5 all-gather.15.cloned.1.call-update
  10.5 0.0 copy-start.8
  10.6 0.0 reduce-scatter.7.cloned.1.call-start
  10.6 32.9 %all-gather.11.cloned.1.call-done = bf16[6144,128]{1,0:T(8,128)(2,1)} async-done(((bf16[1536,128]{1,0:T(8,128)(2,1)}), bf16[6144,128]{1,0:T(8,128)(2,1)}) %all-gather.11.cloned.1.call-update) | async-done | bytes 1572880 | tf_op jit(solution)/shard_map/all_gather | solution.py:35
  43.5 26.7 %all-gather.7.cloned.1.call-done = bf16[128,6144]{1,0:T(8,128)(2,1)} async-done(((bf16[128,768]{1,0:T(8,128)(2,1)}), bf16[128,6144]{1,0:T(8,128)(2,1)}) %all-gather.7.cloned.1.call-update) | async-done | bytes 1572880 | tf_op jit(solution)/shard_map/all_gather | solution.py:33
  70.2 2.7 %multiply_reduce_fusion.1 = (f32[128]{0:T(128)S(1)}, f32[128,128]{0,1:T(8,128)S(1)}) fusion(bf16[128,6144]{1,0:T(8,128)(2,1)} %all-gather.7.cloned.1.call-done, bf16[6144,128]{1,0:T(8,128)(2,1)} %all-gather.11.cloned.1.call-done), kind=kOutput, calls=%fused_computation.26 | convolution fusion | flops 201392000 | bytes 3211776 | tf_op jit(solution)/shard_map/dot_general | solution.py:40
  73.0 0.0 copy-done.8
  73.0 0.1 multiply_convert_fusion.3
  73.1 8.4 %all_gather.27 = bf16[512,128]{0,1:T(8,128)(2,1)S(1)} all-gather(bf16[128,128]{0,1:T(8,128)(2,1)S(1)} %multiply_convert_fusion.3), channel_id=1, replica_groups=mesh['row'=4,'col'=8] {'row'}, dimensions={0}, use_global_device_ids=true | all-gather | bytes 163840 | tf_op jit(solution)/shard_map/all_gather | solution.py:50
  81.5 21.1 %all-gather.13.cloned.1.call-done = bf16[6144,128]{1,0:T(8,128)(2,1)} async-done(((bf16[1536,128]{1,0:T(8,128)(2,1)}), bf16[6144,128]{1,0:T(8,128)(2,1)}) %all-gather.13.cloned.1.call-update) | async-done | bytes 1572880 | tf_op jit(solution)/shard_map/all_gather | solution.py:36
  102.6 0.0 copy-done
  102.6 2.0 convolution_convert_fusion.1
  104.6 0.4 multiply_reduce_fusion
  105.0 0.0 copy-done.9
  105.0 2.6 fusion.19
  107.6 0.8 copy.15
  108.4 0.0 reduce-scatter.7.cloned.1.call-update
  108.4 0.0 copy-start.5
  108.4 0.0 reduce-scatter.5.cloned.1.call-start
  108.5 26.8 %all-gather.9.cloned.1.call-done = bf16[6144,128]{1,0:T(8,128)(2,1)} async-done(((bf16[1536,128]{1,0:T(8,128)(2,1)}), bf16[6144,128]{1,0:T(8,128)(2,1)}) %all-gather.9.cloned.1.call-update) | async-done | bytes 1572880 | tf_op jit(solution)/shard_map/all_gather | solution.py:37
  135.3 2.1 convolution_convert_fusion.3
  137.5 1.6 fusion.5
  139.0 0.0 reduce-scatter.5.cloned.1.call-update
  139.1 29.0 %all-gather.15.cloned.1.call-done = bf16[1024,768]{1,0:T(8,128)(2,1)} async-done(((bf16[256,768]{1,0:T(8,128)(2,1)}), bf16[1024,768]{1,0:T(8,128)(2,1)}) %all-gather.15.cloned.1.call-update) | async-done | bytes 1572880 | tf_op jit(solution)/shard_map/all_gather | solution.py:85
  168.0 4.7 %all-to-all-start = ((bf16[8,128,768]{2,1,0:T(8,128)(2,1)}), bf16[8,128,768]{2,1,0:T(8,128)(2,1)S(1)}, u32[]{:S(2)}, u32[]{:S(2)}) async-start(bf16[8,128,768]{2,1,0:T(8,128)(2,1)} %bitcast.26), calls=%async_computation.1 | async-start | bytes 3145728 | tf_op jit(solution)/shard_map/all_to_all | solution.py:87
  172.8 0.0 all-gather.17.cloned.1.call-start
  172.8 0.7 multiply_convert_fusion.2
  173.6 0.0 all-gather.17.cloned.1.call-update
  173.6 21.2 %reduce-scatter.7.cloned.1.call-done = f32[128,1]{1,0:T(8,128)} async-done(((f32[512,1]{1,0:T(8,128)}), f32[128,1]{1,0:T(8,128)}) %reduce-scatter.7.cloned.1.call-update) | async-done | bytes 528
  194.8 0.9 copy.16
  195.7 26.2 %reduce-scatter.5.cloned.1.call-done = f32[128,128]{0,1:T(8,128)} async-done(((f32[512,128]{0,1:T(8,128)}), f32[128,128]{0,1:T(8,128)}) %reduce-scatter.5.cloned.1.call-update) | async-done | bytes 65552 | tf_op jit(solution)/shard_map/reduce_scatter | solution.py:74
  221.9 0.8 divide_convert_fusion
  222.7 14.7 %all_gather.29 = bf16[128,1024]{0,1:T(8,128)(2,1)S(1)} all-gather(bf16[128,128]{0,1:T(8,128)(2,1)S(1)} %divide_convert_fusion), channel_id=1, replica_groups=mesh['row'=4,'col'=8] {'col'}, dimensions={1}, use_global_device_ids=true | all-gather | bytes 294912 | tf_op jit(solution)/shard_map/all_gather | solution.py:82
  237.4 0.0 copy-done.3
  237.4 1.1 fusion.4
  238.5 0.0 all-to-all-done
  238.5 0.9 copy.14
  239.4 9.4 %all-gather.17.cloned.1.call-done = bf16[128,6144]{1,0:T(8,128)(2,1)} async-done(((bf16[128,768]{1,0:T(8,128)(2,1)}), bf16[128,6144]{1,0:T(8,128)(2,1)}) %all-gather.17.cloned.1.call-update) | async-done | bytes 1572880 | tf_op jit(solution)/shard_map/all_gather | solution.py:88
  248.8 2.6 %convolution_convert_fusion = bf16[128,128]{1,0:T(8,128)(2,1)} fusion(bf16[128,6144]{1,0:T(8,128)(2,1)} %all-gather.17.cloned.1.call-done, bf16[128,6144]{0,1:T(8,128)(2,1)S(1)} %bitcast.28), kind=kOutput, calls=%fused_computation.8 | convolution fusion | flops 201342976 | bytes 3178496 | tf_op jit(solution)/shard_map/dot_general | solution.py:89
  (16 shorter events, 0.0 us)
Async XLA Ops:
  7.2 36.4 %all-gather.11.cloned.1.call-start = ((), (), s32[]{:S(2)}) async-start(), calls=%async_computation.5 | async-start | bytes 1966080 | tf_op jit(solution)/shard_map/all_gather | solution.py:35
  7.9 62.3 %all-gather.7.cloned.1.call-start = ((), (), s32[]{:S(2)}) async-start(), calls=%async_computation.3 | async-start | bytes 1769472 | tf_op jit(solution)/shard_map/all_gather | solution.py:33
  8.6 94.0 %all-gather.13.cloned.1.call-start = ((), (), s32[]{:S(2)}) async-start(), calls=%async_computation.6 | async-start | bytes 1966080 | tf_op jit(solution)/shard_map/all_gather | solution.py:36
  9.4 125.9 %all-gather.9.cloned.1.call-start = ((), (), s32[]{:S(2)}) async-start(), calls=%async_computation.4 | async-start | bytes 1966080 | tf_op jit(solution)/shard_map/all_gather | solution.py:37
  10.0 158.1 %all-gather.15.cloned.1.call-start = ((), (), s32[]{:S(2)}) async-start(), calls=%async_computation.8 | async-start | bytes 1966080 | tf_op jit(solution)/shard_map/all_gather | solution.py:85
  10.5 62.5 %copy-start.8 = (f32[128]{0:T(128)S(1)}, f32[128]{0:T(128)}, u32[]{:S(2)}) copy-start(f32[128]{0:T(128)} %param.18) | copy-start | bytes 1540
  10.6 184.2 %reduce-scatter.7.cloned.1.call-start = ((), (), s32[]{:S(2)}) async-start(), calls=%async_computation.10 | async-start | bytes 327680
  70.2 32.4 %copy-start = (bf16[128,6144]{1,0:T(8,128)(2,1)S(1)}, bf16[128,6144]{1,0:T(8,128)(2,1)}, u32[]{:S(2)}) copy-start(bf16[128,6144]{1,0:T(8,128)(2,1)} %all-gather.7.cloned.1.call-done) | copy-start | bytes 4718596
  81.5 23.1 %copy-start.4 = (bf16[2048,128]{1,0:T(8,128)(2,1)S(1)}, bf16[2048,128]{1,0:T(8,128)(2,1)}, u32[]{:S(2)}) copy-start(bf16[2048,128]{1,0:T(8,128)(2,1)} %param.16) | copy-start | bytes 1572868
  81.5 23.5 %copy-start.9 = (f32[128]{0:T(128)S(1)}, f32[128]{0:T(128)}, u32[]{:S(2)}) copy-start(f32[128]{0:T(128)} %param.19) | copy-start | bytes 1540
  108.4 29.0 %copy-start.5 = (bf16[2048,128]{1,0:T(8,128)(2,1)S(1)}, bf16[2048,128]{1,0:T(8,128)(2,1)}, u32[]{:S(2)}) copy-start(bf16[2048,128]{1,0:T(8,128)(2,1)} %param.17) | copy-start | bytes 1572868
  108.4 113.4 %reduce-scatter.5.cloned.1.call-start = ((), (), s32[]{:S(2)}) async-start(), calls=%async_computation.7 | async-start | bytes 327680 | tf_op jit(solution)/shard_map/reduce_scatter | solution.py:74
  135.3 2.1 copy-start.2
  168.0 4.8 %copy-start.6 = (bf16[128,768]{1,0:T(8,128)(2,1)S(1)}, bf16[128,768]{1,0:T(8,128)(2,1)}, u32[]{:S(2)}) copy-start(bf16[128,768]{1,0:T(8,128)(2,1)} %param.21) | copy-start | bytes 589828
  168.0 4.8 %copy-start.7 = (f32[768]{0:T(1024)S(1)}, f32[768]{0:T(1024)}, u32[]{:S(2)}) copy-start(f32[768]{0:T(1024)} %param.20) | copy-start | bytes 9220
  168.0 69.4 %copy-start.1 = (bf16[1024,768]{1,0:T(8,128)(2,1)S(1)}, bf16[1024,768]{1,0:T(8,128)(2,1)}, u32[]{:S(2)}) copy-start(bf16[1024,768]{1,0:T(8,128)(2,1)} %all-gather.15.cloned.1.call-done) | copy-start | bytes 4718596
  168.0 69.4 %copy-start.3 = (bf16[128,768]{1,0:T(8,128)(2,1)S(1)}, bf16[128,768]{1,0:T(8,128)(2,1)}, u32[]{:S(2)}) copy-start(bf16[128,768]{1,0:T(8,128)(2,1)} %param.11) | copy-start | bytes 589828
  168.0 70.5 %all-to-all-start = ((bf16[8,128,768]{2,1,0:T(8,128)(2,1)}), bf16[8,128,768]{2,1,0:T(8,128)(2,1)S(1)}, u32[]{:S(2)}, u32[]{:S(2)}) async-start(bf16[8,128,768]{2,1,0:T(8,128)(2,1)} %bitcast.26), calls=%async_computation.1 | async-start | bytes 3145728 | tf_op jit(solution)/shard_map/all_to_all | solution.py:87
  172.8 76.0 %all-gather.17.cloned.1.call-start = ((), (), s32[]{:S(2)}) async-start(), calls=%async_computation.9 | async-start | bytes 1769472 | tf_op jit(solution)/shard_map/all_gather | solution.py:88
Sparse Core Ops, SparseCore 0:
  9.8 33.6 all-gather.10
  45.2 25.0 all-gather.6
  72.1 30.4 all-gather.12
  104.3 30.9 all-gather.8
  137.0 30.9 all-gather.14
  170.6 24.0 reduce-scatter.6
  197.7 24.0 reduce-scatter.4
  223.5 25.2 all-gather.16
where the time goes:
time: 259 us; the launch traced here: 258 us
  waiting for transfers between devices  196 us (76%)
  blocking collectives  23.1 us (9%)
  matrix products  14.6 us (6%)
  between operations  14.3 us (6%)
  starting transfers between devices  5.05 us (2%)
  local copies, waits for them, and re-layouts  2.67 us (1%)
    all_gather x1, waiting for transfers between devices, body(): lax.all_gather(w_query, 'row', axis=0, tiled=True)  32.9 us
    all_gather x1, waiting for transfers between devices, body(): output_whole = lax.all_gather(w_out, 'row', axis=0, tiled=True)  29 us
    all_gather x1, waiting for transfers between devices, body(): lax.all_gather(w_value, 'row', axis=0, tiled=True)  26.8 us
    all_gather x1, waiting for transfers between devices, body(): features_whole = lax.all_gather(tokens, 'col', axis=1, tiled=True)  26.7 us
    reduce_scatter x1, waiting for transfers between devices, body(): lax.psum_scatter(numerators, 'row', scatter_dimension=0, tiled=True)  26.2 us
    unnamed x9, waiting for transfers between devices  24.4 us
    all_gather x1, waiting for transfers between devices, body(): lax.all_gather(w_key, 'row', axis=0, tiled=True)  21.1 us
    all_gather x1, blocking collectives, body(): attention_whole = lax.all_gather(attention, 'col', axis=1, tiled=True)  14.7 us
  transfers between devices with their start and end apart: 9, of which 8 were waited for; matrix products, arithmetic and copies ran while one was open for 6% of the time, Pallas kernels for 0%

commit v1 on v0

v1 whole, which is shorter than its diff:
```python
import math

import jax
import jax.numpy as jnp
from jax import lax
from jax.experimental import pallas as pl
from jax.experimental.pallas import tpu as pltpu
from jax.sharding import PartitionSpec as P

epsilon = 1e-06
both = ("row", "col")
f32 = jnp.float32
bf16 = jnp.bfloat16
tail = 16


def size_of(arrays):
    return sum(math.prod(a.shape) * jnp.dtype(a.dtype).itemsize for a in arrays)


def call(kernel, name, operands, outs, scratch=(), flops=0):
    moved = size_of(operands) + size_of(outs)
    held = moved + sum(math.prod(s.shape) * jnp.dtype(s.dtype).itemsize for s in scratch)
    whole = pl.BlockSpec(memory_space=pltpu.VMEM)
    return pl.pallas_call(
        kernel,
        out_shape=list(outs),
        in_specs=[whole] * len(operands),
        out_specs=[whole] * len(outs),
        scratch_shapes=list(scratch),
        compiler_params=pltpu.CompilerParams(vmem_limit_bytes=2 * held + (12 << 20)),
        cost_estimate=pl.CostEstimate(flops=flops, bytes_accessed=moved, transcendentals=0),
        name=name,
    )(*operands)


def dot(a, b):
    return jnp.dot(a, b, preferred_element_type=f32)


def dot_last(a, b):
    return lax.dot_general(a, b, (((1,), (1,)), ((), ())), preferred_element_type=f32)


def normed(wide, gain):
    mean_square = jnp.mean(wide * wide, axis=-1, keepdims=True)
    return wide * lax.rsqrt(mean_square + epsilon) * gain


def solution(mesh):
    R, C = mesh.shape["row"], mesh.shape["col"]
    k = C // R
    assert C == R * k and k == 2 and R & (R - 1) == 0

    def here():
        f, c = lax.axis_index("row"), lax.axis_index("col")
        return f, c // k, c % k

    def route(to):
        return [
            (r * C + z * k + q, (lambda a, b, e: a * C + b * k + e)(*to(r, z, q)))
            for r in range(R)
            for z in range(R)
            for q in range(k)
        ]

    def across_chip(x):
        return lax.ppermute(x, both, route(lambda r, z, q: (r, z, q ^ 1)))

    def over_row(x, s):
        return lax.ppermute(x, both, route(lambda r, z, q: (r ^ s, z, q)))

    def over_z(x, m):
        return lax.ppermute(x, both, route(lambda r, z, q: (r, z ^ m, q)))

    def turned(x, d):
        return lax.ppermute(x, both, route(lambda r, z, q: (z, r ^ d, q)))

    def body(
        tokens,
        w_query,
        w_key,
        w_value,
        w_out,
        key_cache,
        value_cache,
        query_gain,
        key_gain,
        out_gate,
        cotangent,
    ):
        T, F = tokens.shape
        H = query_gain.shape[0]
        cached = key_cache.shape[0]
        wide_out = w_out.shape[1]
        assert w_query.shape == (k * F, H) and w_out.shape == (k * H, wide_out) and T == H
        query_gain = query_gain.reshape(1, H)
        key_gain = key_gain.reshape(1, H)
        out_gate = out_gate.reshape(1, wide_out)
        fold = H ** (-0.5) * math.log2(math.e)

        mine = [turned(tokens, d) for d in range(R)]
        other = [across_chip(x) for x in mine]
        out_rows = [w_out] + [over_row(w_out, s) for s in range(1, R)]

        def prepare(key_ref, value_ref, gain_ref, key_out, value_out):
            key = normed(key_ref[...].astype(f32), gain_ref[...])
            key_out[...] = key.T.astype(bf16)
            value_out[:, :H] = value_ref[...]
            value_out[:, H:] = jnp.ones((cached, H), bf16)

        keys_t, values_one = call(
            prepare,
            "cache",
            (key_cache, value_cache, key_gain),
            [
                jax.ShapeDtypeStruct((H, cached), bf16),
                jax.ShapeDtypeStruct((cached, 2 * H), bf16),
            ],
        )

        def project(*refs):
            mine_refs, other_refs = refs[:R], refs[R : 2 * R]
            wq, wk, wv = refs[2 * R : 2 * R + 3]
            outs = refs[2 * R + 3 : 3 * R + 3]
            held = refs[3 * R + 3]
            f, _, q = here()
            first = pl.ds(pl.multiple_of(q * F, F), F)
            second = pl.ds(pl.multiple_of((1 - q) * F, F), F)
            w_mine = jnp.concatenate([wq[first], wk[first], wv[first]], axis=1)
            w_other = jnp.concatenate([wq[second], wk[second], wv[second]], axis=1)
            for d in range(R):
                part = (dot(mine_refs[d][...], w_mine) + dot(other_refs[d][...], w_other)).astype(bf16)
                for s in range(R):
                    outs[s][d * T : (d + 1) * T, :] = part[:, :H]
                held[d, :T] = part[:, H : 2 * H]
                held[d, T:] = part[:, 2 * H :]
            for s in range(R):
                outs[s][R * T :, :] = held[f ^ s]

        parts = call(
            project,
            "project",
            (*mine, *other, w_query, w_key, w_value),
            [jax.ShapeDtypeStruct(((R + 2) * T, H), bf16)] * R,
            [pltpu.VMEM((R, 2 * T, H), bf16)],
            flops=2 * R * T * k * F * 3 * H,
        )
        parts = [parts[0]] + [over_row(parts[s], s) for s in range(1, R)]

        def attend(*refs):
            part_refs = refs[:R]
            keys_ref, values_ref, query_gain_ref, key_gain_ref = refs[R : R + 4]
            outs = refs[R + 4 : 2 * R + 4]
            query_ref, held = refs[2 * R + 4 :]
            f, z, _ = here()

            def total(rows):
                return sum(ref[rows, :].astype(f32) for ref in part_refs)

            query_ref[...] = normed(total(slice(0, R * T)), query_gain_ref[...] * fold).astype(bf16)
            key_new = normed(total(slice(R * T, (R + 1) * T)), key_gain_ref[...]).astype(bf16)
            value_new = total(slice((R + 1) * T, (R + 2) * T)).astype(bf16)
            value_new = jnp.concatenate([value_new, jnp.ones((T, H), bf16)], axis=1)
            step = min(512, cached)
            eye = lax.broadcasted_iota(jnp.int32, (T, H), 0) == lax.broadcasted_iota(
                jnp.int32, (T, H), 1
            )

            def block(d, carry):
                query = query_ref[pl.ds(pl.multiple_of(d * T, T), T), :]
                weights = jnp.exp2(dot_last(query, key_new)).astype(bf16)
                sums = dot(weights, value_new)
                for j in range(0, cached, step):
                    weights = jnp.exp2(dot(query, keys_ref[:, j : j + step])).astype(bf16)
                    sums = sums + dot(weights, values_ref[j : j + step, :])
                held[d, :T] = sums[:, :H].astype(bf16)
                row = jnp.sum(jnp.where(eye, sums[:, H:], 0.0), axis=0, keepdims=True)
                high = row.astype(bf16).astype(f32)
                low = row - high
                which = lax.broadcasted_iota(jnp.int32, (tail, H), 0)
                held[d, T:] = jnp.where(which == 0, high, jnp.where(which == 1, low, 0.0)).astype(bf16)
                return carry

            lax.fori_loop(0, R, block, 0, unroll=min(R, 4))
            for s in range(R):
                outs[s][...] = held[f ^ z ^ s]

        sums = call(
            attend,
            "attend",
            (*parts, keys_t, values_one, query_gain, key_gain),
            [jax.ShapeDtypeStruct((T + tail, H), bf16)] * R,
            [pltpu.VMEM((R * T, H), bf16), pltpu.VMEM((R, T + tail, H), bf16)],
            flops=4 * R * T * (cached + T) * H,
        )
        sums = [sums[0]] + [over_row(sums[s], s) for s in range(1, R)]

        def gradient(*refs):
            cot_ref, gate_ref = refs[:2]
            rows_refs = refs[2 : 2 + R]
            own_ref, away_ref = refs[2 + R :]
            f, z, q = here()
            scaled = (cot_ref[...].astype(f32) * gate_ref[...]).astype(bf16)
            for s in range(R):
                part = dot_last(scaled, rows_refs[s][...]).astype(bf16)
                even, odd = part[:, :H], part[:, H:]
                m = f ^ s ^ z
                own_ref[m] = jnp.where(q == 0, even, odd)
                away_ref[m] = jnp.where(q == 0, odd, even)

        slots = jax.ShapeDtypeStruct((R, T, H), bf16)
        grad_own, grad_away = call(
            gradient,
            "gradient",
            (cotangent, out_gate, *out_rows),
            [slots, slots],
            flops=2 * T * R * k * H * wide_out,
        )
        grad_away = across_chip(grad_away)

        def finish(*refs):
            sum_refs = refs[:R]
            own_ref, away_ref = refs[R : R + 2]
            outs = refs[R + 2 :]
            numerators = sum(ref[:T, :].astype(f32) for ref in sum_refs)
            row = sum(ref[T : T + 1, :].astype(f32) + ref[T + 1 : T + 2, :].astype(f32) for ref in sum_refs)
            eye = lax.broadcasted_iota(jnp.int32, (T, H), 0) == lax.broadcasted_iota(
                jnp.int32, (T, H), 1
            )
            totals = jnp.sum(jnp.where(eye, row, 0.0), axis=1, keepdims=True)
            attention = (numerators / totals).astype(bf16)
            for m in range(R):
                outs[m][:T] = attention
                outs[m][T:] = (own_ref[m].astype(f32) + away_ref[m].astype(f32)).astype(bf16)

        pairs = call(
            finish,
            "finish",
            (*sums, grad_own, grad_away),
            [jax.ShapeDtypeStruct((2 * T, H), bf16)] * R,
        )
        pairs = [pairs[0]] + [over_z(pairs[m], m) for m in range(1, R)]
        pairs_other = [across_chip(x) for x in pairs]

        def output(*refs):
            mine_refs, other_refs, rows_refs = refs[:R], refs[R : 2 * R], refs[2 * R : 3 * R]
            tokens_ref, gate_ref, layer_ref, grad_ref, held = refs[3 * R :]
            f, z, q = here()
            grad = jnp.zeros((T, H), f32)
            for m in range(R):
                own, away = mine_refs[m][:T], other_refs[m][:T]
                held[z ^ m, :, :H] = jnp.where(q == 0, own, away)
                held[z ^ m, :, H:] = jnp.where(q == 0, away, own)
                grad = grad + mine_refs[m][T:].astype(f32)
            grad_ref[...] = grad.astype(bf16)
            branch = sum(dot(held[f ^ s], rows_refs[s][...]) for s in range(R))
            layer_ref[...] = (tokens_ref[...].astype(f32) + gate_ref[...] * branch).astype(bf16)

        layer_out, attention_cotangent = call(
            output,
            "output",
            (*pairs, *pairs_other, *out_rows, tokens, out_gate),
            [jax.ShapeDtypeStruct((T, wide_out), bf16), jax.ShapeDtypeStruct((T, H), bf16)],
            [pltpu.VMEM((R, T, k * H), bf16)],
            flops=2 * T * R * k * H * wide_out,
        )
        return layer_out, attention_cotangent

    spread = P("row", "col")
    return jax.shard_map(
        body,
        mesh=mesh,
        in_specs=(spread,) * 7 + (P(), P(), P("col"), spread),
        out_specs=(spread, spread),
        check_vma=False,
    )
```

time: 259 us -> 77.7 us (0.30)
  waiting for transfers between devices: 196 us -> 24.5 us
  starting transfers between devices: 5.05 us -> 42.8 us
  blocking collectives: 23.1 us -> 0 us
  matrix products: 14.6 us -> 0 us
  between operations: 14.3 us -> 0.79 us
  Pallas kernels: 0 us -> 5.2 us
    all_gather x6 -> x0, waiting for transfers between devices: 146 us -> none  [the longest x1 32.9 us: body(): lax.all_gather(w_query, 'row', axis=0, tiled=True)]
    ppermute x0 -> x25, starting transfers between devices: none -> 42.8 us  [the longest x9 24.8 us: over_row(): return lax.ppermute(x, both, route(lambda r, z, q: (r ^ s, z, q)))]
    reduce_scatter x1 -> x0, waiting for transfers between devices: 26.2 us -> none  [body(): lax.psum_scatter(numerators, 'row', scatter_dimension=0, tiled=True)]
    ppermute x0 -> x25, waiting for transfers between devices: none -> 24.5 us  [the longest x9 17.6 us: over_row(): return lax.ppermute(x, both, route(lambda r, z, q: (r ^ s, z, q)))]
    unnamed x9 -> x0, waiting for transfers between devices: 24.4 us -> none
    all_gather x2 -> x0, blocking collectives: 23.1 us -> none  [the longest x1 14.7 us: body(): attention_whole = lax.all_gather(attention, 'col', axis=1, tiled=True)]
    dot_general x7 -> x0, matrix products: 14.6 us -> none  [the longest x3 6.82 us: body(): jnp.dot(features_whole, piece, preferred_element_type=jnp.float32)]
    pallas_call x0 -> x6, Pallas kernels: none -> 5.2 us  [call(): pl.pallas_call(kernel, out_shape=list(outs), in_specs=[whole] * len(opera...]
  transfers between devices with their start and end apart: 9 -> 25, of which waited for: 8 -> 11; matrix products, arithmetic and copies ran while one was open for 6% -> 0% of each run, Pallas kernels for 0% -> 5%
where the time goes in v1:
time: 77.7 us; the launch traced here: 77.5 us
  starting transfers between devices  42.8 us (55%)
  waiting for transfers between devices  24.5 us (32%)
  Pallas kernels  5.2 us (7%)
  local copies, waits for them, and re-layouts  4.22 us (5%)
  between operations  0.79 us (1%)
    ppermute x9, starting transfers between devices, over_row(): return lax.ppermute(x, both, route(lambda r, z, q: (r ^ s, z, q)))  24.8 us
    ppermute x9, waiting for transfers between devices, over_row(): return lax.ppermute(x, both, route(lambda r, z, q: (r ^ s, z, q)))  17.6 us
    ppermute x4, starting transfers between devices, turned(): return lax.ppermute(x, both, route(lambda r, z, q: (z, r ^ d, q)))  11.9 us
    pallas_call x6, Pallas kernels, call(): pl.pallas_call(kernel, out_shape=list(outs), in_specs=[whole] * len(opera...  5.2 us
    ppermute x3, starting transfers between devices, over_z(): return lax.ppermute(x, both, route(lambda r, z, q: (r, z ^ m, q)))  4.45 us
    ppermute x3, waiting for transfers between devices, over_z(): return lax.ppermute(x, both, route(lambda r, z, q: (r, z ^ m, q)))  4.28 us
    unnamed x22, local copies, waits for them, and re-layouts  4.22 us
    ppermute x9, waiting for transfers between devices, across_chip(): return lax.ppermute(x, both, route(lambda r, z, q: (r, z, q ^ 1)))  2.46 us
  transfers between devices with their start and end apart: 25, of which 11 were waited for; matrix products, arithmetic and copies ran while one was open for 0% of the time, Pallas kernels for 5%

profile of v1, /device:TPU:0, one launch (start us, length us, event | category | flops | bytes accessed | tf_op | source)
XLA Modules:
  0.0 77.5 jit_solution(9041603618051740980)
XLA Ops:
  0.6 1.7 %collective-permute-start = (bf16[128,768]{1,0:T(8,128)(2,1)}, bf16[128,768]{1,0:T(8,128)(2,1)S(1)}, u32[]{:S(2)}, u32[]{:S(2)}) collective-permute-start(bf16[128,768]{1,0:T(8,128)(2,1)} %refs_12_.1), channel_id=1, source_target_pairs={{0,0},{1,1},{2,8},{3,9},{4,16},{5,17},{6,24},{7,25},{8,2},{9,3},{1... | collective-permute-start | bytes 589832 | tf_op jit(solution)/shard_map/ppermute | solution.py:77
  2.4 4.8 %collective-permute-start.1 = (bf16[128,768]{1,0:T(8,128)(2,1)}, bf16[128,768]{1,0:T(8,128)(2,1)S(1)}, u32[]{:S(2)}, u32[]{:S(2)}) collective-permute-start(bf16[128,768]{1,0:T(8,128)(2,1)} %refs_12_.1), channel_id=1, source_target_pairs={{0,2},{1,3},{2,10},{3,11},{4,18},{5,19},{6,26},{7,27},{8,0},{9,1},... | collective-permute-start | bytes 589832 | tf_op jit(solution)/shard_map/ppermute | solution.py:77
  7.1 3.5 %collective-permute-start.2 = (bf16[128,768]{1,0:T(8,128)(2,1)}, bf16[128,768]{1,0:T(8,128)(2,1)S(1)}, u32[]{:S(2)}, u32[]{:S(2)}) collective-permute-start(bf16[128,768]{1,0:T(8,128)(2,1)} %refs_12_.1), channel_id=1, source_target_pairs={{0,4},{1,5},{2,12},{3,13},{4,20},{5,21},{6,28},{7,29},{8,6},{9,7},... | collective-permute-start | bytes 589832 | tf_op jit(solution)/shard_map/ppermute | solution.py:77
  10.6 1.9 %collective-permute-start.3 = (bf16[128,768]{1,0:T(8,128)(2,1)}, bf16[128,768]{1,0:T(8,128)(2,1)S(1)}, u32[]{:S(2)}, u32[]{:S(2)}) collective-permute-start(bf16[128,768]{1,0:T(8,128)(2,1)} %refs_12_.1), channel_id=1, source_target_pairs={{0,6},{1,7},{2,14},{3,15},{4,22},{5,23},{6,30},{7,31},{8,4},{9,5},... | collective-permute-start | bytes 589832 | tf_op jit(solution)/shard_map/ppermute | solution.py:77
  12.5 0.0 collective-permute-done.refs_0_
  12.6 0.0 collective-permute-start.4
  12.6 0.5 collective-permute-start.5
  13.1 7.0 %collective-permute-start.14 = (bf16[256,768]{1,0:T(8,128)(2,1)}, bf16[256,768]{1,0:T(8,128)(2,1)S(1)}, u32[]{:S(2)}, u32[]{:S(2)}) collective-permute-start(bf16[256,768]{1,0:T(8,128)(2,1)} %refs_8_.3), channel_id=1, source_target_pairs={{0,8},{1,9},{2,10},{3,11},{4,12},{5,13},{6,14},{7,15},{8,0},{9,1},... | collective-permute-start | bytes 1179656 | tf_op jit(solution)/shard_map/ppermute | solution.py:71
  20.0 0.1 collective-permute-done.2.refs_2_
  20.2 8.0 %collective-permute-start.15 = (bf16[256,768]{1,0:T(8,128)(2,1)}, bf16[256,768]{1,0:T(8,128)(2,1)S(1)}, u32[]{:S(2)}, u32[]{:S(2)}) collective-permute-start(bf16[256,768]{1,0:T(8,128)(2,1)} %refs_8_.3), channel_id=1, source_target_pairs={{0,16},{1,17},{2,18},{3,19},{4,20},{5,21},{6,22},{7,23},{8,24},{9,... | collective-permute-start | bytes 1179656 | tf_op jit(solution)/shard_map/ppermute | solution.py:71
  28.1 0.0 collective-permute-done.3.refs_3_
  28.1 1.5 %collective-permute-start.16 = (bf16[256,768]{1,0:T(8,128)(2,1)}, bf16[256,768]{1,0:T(8,128)(2,1)S(1)}, u32[]{:S(2)}, u32[]{:S(2)}) collective-permute-start(bf16[256,768]{1,0:T(8,128)(2,1)} %refs_8_.3), channel_id=1, source_target_pairs={{0,24},{1,25},{2,26},{3,27},{4,28},{5,29},{6,30},{7,31},{8,16},{9,... | collective-permute-start | bytes 1179656 | tf_op jit(solution)/shard_map/ppermute | solution.py:71
  29.6 0.5 collective-permute-start.7
  30.1 0.9 %collective-permute-done.6.refs_6_ = bf16[128,768]{1,0:T(8,128)(2,1)S(1)} collective-permute-done((bf16[128,768]{1,0:T(8,128)(2,1)S(1)}, bf16[128,768]{1,0:T(8,128)(2,1)S(1)}, u32[]{:S(2)}, u32[]{:S(2)}) %collective-permute-start.6) | collective-permute-done | bytes 196640 | tf_op jit(solution)/shard_map/ppermute | solution.py:68
  31.0 0.3 collective-permute-done.7.refs_7_
  31.3 1.0 %copy-done.3 = bf16[1536,128]{1,0:T(8,128)(2,1)S(1)} copy-done((bf16[1536,128]{1,0:T(8,128)(2,1)S(1)}, bf16[1536,128]{1,0:T(8,128)(2,1)}, u32[]{:S(2)}) %copy-start.3) | copy-done | bytes 393240
  32.3 1.0 %copy-done.4 = bf16[1536,128]{1,0:T(8,128)(2,1)S(1)} copy-done((bf16[1536,128]{1,0:T(8,128)(2,1)S(1)}, bf16[1536,128]{1,0:T(8,128)(2,1)}, u32[]{:S(2)}) %copy-start.4) | copy-done | bytes 393240
  33.3 1.0 %copy-done.5 = bf16[1536,128]{1,0:T(8,128)(2,1)S(1)} copy-done((bf16[1536,128]{1,0:T(8,128)(2,1)S(1)}, bf16[1536,128]{1,0:T(8,128)(2,1)}, u32[]{:S(2)}) %copy-start.5) | copy-done | bytes 393240
  34.3 1.0 %project.1 = (bf16[768,128]{1,0:T(8,128)(2,1)S(1)}, bf16[768,128]{1,0:T(8,128)(2,1)S(1)}, bf16[768,128]{1,0:T(8,128)(2,1)S(1)}, bf16[768,128]{1,0:T(8,128)(2,1)S(1)}) custom-call(bf16[128,768]{1,0:T(8,128)(2,1)S(1)} %collective-permute-done.refs_0_, bf16[128,768]{1,0:T(8,128)(2,1)S(1)} %collective-permute-done.1.refs_1_, ...), custom_call_target="tpu_custom_call" | custom-call | flops 603979776 | bytes 3538944 | tf_op jit(solution)/shard_map/project/pallas_call | solution.py:25
  35.3 0.0 copy-start.10
  35.3 1.6 %collective-permute-start.10 = (bf16[768,128]{1,0:T(8,128)(2,1)S(1)}, bf16[768,128]{1,0:T(8,128)(2,1)S(1)}, u32[]{:S(2)}, u32[]{:S(2)}) collective-permute-start(bf16[768,128]{1,0:T(8,128)(2,1)S(1)} %get-tuple-element.21), channel_id=1, source_target_pairs={{0,24},{1,25},{2,26},{3,27},{4,28},{5,29},{6,30},{7,31},{8,16},{9,... | collective-permute-start | bytes 589832 | tf_op jit(solution)/shard_map/ppermute | solution.py:71
  36.9 1.9 %collective-permute-start.8 = (bf16[768,128]{1,0:T(8,128)(2,1)S(1)}, bf16[768,128]{1,0:T(8,128)(2,1)S(1)}, u32[]{:S(2)}, u32[]{:S(2)}) collective-permute-start(bf16[768,128]{1,0:T(8,128)(2,1)S(1)} %get-tuple-element.19), channel_id=1, source_target_pairs={{0,8},{1,9},{2,10},{3,11},{4,12},{5,13},{6,14},{7,15},{8,0},{9,1},... | collective-permute-start | bytes 589832 | tf_op jit(solution)/shard_map/ppermute | solution.py:71
  38.8 1.4 %collective-permute-start.9 = (bf16[768,128]{1,0:T(8,128)(2,1)S(1)}, bf16[768,128]{1,0:T(8,128)(2,1)S(1)}, u32[]{:S(2)}, u32[]{:S(2)}) collective-permute-start(bf16[768,128]{1,0:T(8,128)(2,1)S(1)} %get-tuple-element.20), channel_id=1, source_target_pairs={{0,16},{1,17},{2,18},{3,19},{4,20},{5,21},{6,22},{7,23},{8,24},{9,... | collective-permute-start | bytes 589832 | tf_op jit(solution)/shard_map/ppermute | solution.py:71
  40.2 0.0 copy-start.2
  40.2 10.3 %collective-permute-done.15.refs_4_.refs_10_ = bf16[256,768]{1,0:T(8,128)(2,1)S(1)} collective-permute-done((bf16[256,768]{1,0:T(8,128)(2,1)}, bf16[256,768]{1,0:T(8,128)(2,1)S(1)}, u32[]{:S(2)}, u32[]{:S(2)}) %collective-permute-start.15) | collective-permute-done | bytes 393248 | tf_op jit(solution)/shard_map/ppermute | solution.py:71
  50.5 0.7 gradient.1
  51.2 0.0 copy-start.8
  51.2 0.1 collective-permute-start.17
  51.3 0.5 copy-done.8
  51.9 0.6 cache.1
  52.5 3.6 %collective-permute-done.9.refs_2_ = bf16[768,128]{1,0:T(8,128)(2,1)S(1)} collective-permute-done((bf16[768,128]{1,0:T(8,128)(2,1)S(1)}, bf16[768,128]{1,0:T(8,128)(2,1)S(1)}, u32[]{:S(2)}, u32[]{:S(2)}) %collective-permute-start.9) | collective-permute-done | bytes 196640 | tf_op jit(solution)/shard_map/ppermute | solution.py:71
  56.1 0.7 copy-done.9
  56.7 1.7 %attend.1 = (bf16[144,128]{1,0:T(8,128)(2,1)S(1)}, bf16[144,128]{1,0:T(8,128)(2,1)S(1)}, bf16[144,128]{1,0:T(8,128)(2,1)S(1)}, bf16[144,128]{1,0:T(8,128)(2,1)S(1)}) custom-call(bf16[768,128]{1,0:T(8,128)(2,1)S(1)} %get-tuple-element.18.refs_0_, bf16[768,128]{1,0:T(8,128)(2,1)S(1)} %collective-permute-done.8.refs_1_, ...), custom_call_target="tpu_custom_call" | custom-call | flops 570425344 | bytes 2507776 | tf_op jit(solution)/shard_map/attend/pallas_call | solution.py:25
  58.5 0.7 collective-permute-start.11
  59.2 1.7 %collective-permute-start.12 = (bf16[144,128]{1,0:T(8,128)(2,1)S(1)}, bf16[144,128]{1,0:T(8,128)(2,1)S(1)}, u32[]{:S(2)}, u32[]{:S(2)}) collective-permute-start(bf16[144,128]{1,0:T(8,128)(2,1)S(1)} %get-tuple-element.26), channel_id=1, source_target_pairs={{0,16},{1,17},{2,18},{3,19},{4,20},{5,21},{6,22},{7,23},{8,24},{9,... | collective-permute-start | bytes 110600 | tf_op jit(solution)/shard_map/ppermute | solution.py:71
  60.9 1.2 %collective-permute-start.13 = (bf16[144,128]{1,0:T(8,128)(2,1)S(1)}, bf16[144,128]{1,0:T(8,128)(2,1)S(1)}, u32[]{:S(2)}, u32[]{:S(2)}) collective-permute-start(bf16[144,128]{1,0:T(8,128)(2,1)S(1)} %get-tuple-element.27), channel_id=1, source_target_pairs={{0,24},{1,25},{2,26},{3,27},{4,28},{5,29},{6,30},{7,31},{8,16},{9,... | collective-permute-start | bytes 110600 | tf_op jit(solution)/shard_map/ppermute | solution.py:71
  62.0 0.5 collective-permute-done.11.refs_1_
  62.5 0.6 collective-permute-done.12.refs_2_
  63.1 2.6 %collective-permute-done.13.refs_3_ = bf16[144,128]{1,0:T(8,128)(2,1)S(1)} collective-permute-done((bf16[144,128]{1,0:T(8,128)(2,1)S(1)}, bf16[144,128]{1,0:T(8,128)(2,1)S(1)}, u32[]{:S(2)}, u32[]{:S(2)}) %collective-permute-start.13) | collective-permute-done | bytes 36896 | tf_op jit(solution)/shard_map/ppermute | solution.py:71
  65.7 0.1 finish.1
  65.8 0.5 collective-permute-start.18
  66.4 2.7 %collective-permute-start.19 = (bf16[256,128]{1,0:T(8,128)(2,1)S(1)}, bf16[256,128]{1,0:T(8,128)(2,1)S(1)}, u32[]{:S(2)}, u32[]{:S(2)}) collective-permute-start(bf16[256,128]{1,0:T(8,128)(2,1)S(1)} %get-tuple-element.32), channel_id=1, source_target_pairs={{0,4},{1,5},{2,6},{3,7},{4,0},{5,1},{6,2},{7,3},{8,12},{9,13},{10,... | collective-permute-start | bytes 196616 | tf_op jit(solution)/shard_map/ppermute | solution.py:74
  69.0 1.3 %collective-permute-start.20 = (bf16[256,128]{1,0:T(8,128)(2,1)S(1)}, bf16[256,128]{1,0:T(8,128)(2,1)S(1)}, u32[]{:S(2)}, u32[]{:S(2)}) collective-permute-start(bf16[256,128]{1,0:T(8,128)(2,1)S(1)} %get-tuple-element.33), channel_id=1, source_target_pairs={{0,6},{1,7},{2,4},{3,5},{4,2},{5,3},{6,0},{7,1},{8,14},{9,15},{10,... | collective-permute-start | bytes 196616 | tf_op jit(solution)/shard_map/ppermute | solution.py:74
  70.3 0.5 collective-permute-start.22
  70.8 2.1 %collective-permute-done.19.refs_2_ = bf16[256,128]{1,0:T(8,128)(2,1)S(1)} collective-permute-done((bf16[256,128]{1,0:T(8,128)(2,1)S(1)}, bf16[256,128]{1,0:T(8,128)(2,1)S(1)}, u32[]{:S(2)}, u32[]{:S(2)}) %collective-permute-start.19) | collective-permute-done | bytes 65568 | tf_op jit(solution)/shard_map/ppermute | solution.py:74
  72.9 2.2 %collective-permute-done.20.refs_3_ = bf16[256,128]{1,0:T(8,128)(2,1)S(1)} collective-permute-done((bf16[256,128]{1,0:T(8,128)(2,1)S(1)}, bf16[256,128]{1,0:T(8,128)(2,1)S(1)}, u32[]{:S(2)}, u32[]{:S(2)}) %collective-permute-start.20) | collective-permute-done | bytes 65568 | tf_op jit(solution)/shard_map/ppermute | solution.py:74
  75.1 1.2 %collective-permute-done.24.refs_7_ = bf16[256,128]{1,0:T(8,128)(2,1)S(1)} collective-permute-done((bf16[256,128]{1,0:T(8,128)(2,1)S(1)}, bf16[256,128]{1,0:T(8,128)(2,1)S(1)}, u32[]{:S(2)}, u32[]{:S(2)}) %collective-permute-start.24) | collective-permute-done | bytes 65568 | tf_op jit(solution)/shard_map/ppermute | solution.py:68
  76.4 1.1 %output.1 = (bf16[128,768]{1,0:T(8,128)(2,1)}, bf16[128,128]{1,0:T(8,128)(2,1)}) custom-call(bf16[256,128]{1,0:T(8,128)(2,1)S(1)} %get-tuple-element.30.refs_0_, bf16[256,128]{1,0:T(8,128)(2,1)S(1)} %collective-permute-done.18.refs_1_, bf16[256,128]{1,0:T(8,128)(2,1)S(1)} %collective-permute-done.19.refs_2_, ...), custom_call_target="tpu_custom_call" | custom-call | flops 201326592 | bytes 2526208 | tf_op jit(solution)/shard_map/output/pallas_call | solution.py:25
  (31 shorter events, 0.1 us)
Async XLA Ops:
  0.6 49.9 %copy-start = (bf16[256,768]{1,0:T(8,128)(2,1)S(1)}, bf16[256,768]{1,0:T(8,128)(2,1)}, u32[]{:S(2)}) copy-start(bf16[256,768]{1,0:T(8,128)(2,1)} %refs_8_.3) | copy-start | bytes 1179652
  0.6 11.9 %collective-permute-start = (bf16[128,768]{1,0:T(8,128)(2,1)}, bf16[128,768]{1,0:T(8,128)(2,1)S(1)}, u32[]{:S(2)}, u32[]{:S(2)}) collective-permute-start(bf16[128,768]{1,0:T(8,128)(2,1)} %refs_12_.1), channel_id=1, source_target_pairs={{0,0},{1,1},{2,8},{3,9},{4,16},{5,17},{6,24},{7,25},{8,2},{9,3},{1... | collective-permute-start | bytes 589832 | tf_op jit(solution)/shard_map/ppermute | solution.py:77
  2.4 10.2 %collective-permute-start.1 = (bf16[128,768]{1,0:T(8,128)(2,1)}, bf16[128,768]{1,0:T(8,128)(2,1)S(1)}, u32[]{:S(2)}, u32[]{:S(2)}) collective-permute-start(bf16[128,768]{1,0:T(8,128)(2,1)} %refs_12_.1), channel_id=1, source_target_pairs={{0,2},{1,3},{2,10},{3,11},{4,18},{5,19},{6,26},{7,27},{8,0},{9,1},... | collective-permute-start | bytes 589832 | tf_op jit(solution)/shard_map/ppermute | solution.py:77
  7.1 13.0 %collective-permute-start.2 = (bf16[128,768]{1,0:T(8,128)(2,1)}, bf16[128,768]{1,0:T(8,128)(2,1)S(1)}, u32[]{:S(2)}, u32[]{:S(2)}) collective-permute-start(bf16[128,768]{1,0:T(8,128)(2,1)} %refs_12_.1), channel_id=1, source_target_pairs={{0,4},{1,5},{2,12},{3,13},{4,20},{5,21},{6,28},{7,29},{8,6},{9,7},... | collective-permute-start | bytes 589832 | tf_op jit(solution)/shard_map/ppermute | solution.py:77
  10.6 17.5 %collective-permute-start.3 = (bf16[128,768]{1,0:T(8,128)(2,1)}, bf16[128,768]{1,0:T(8,128)(2,1)S(1)}, u32[]{:S(2)}, u32[]{:S(2)}) collective-permute-start(bf16[128,768]{1,0:T(8,128)(2,1)} %refs_12_.1), channel_id=1, source_target_pairs={{0,6},{1,7},{2,14},{3,15},{4,22},{5,23},{6,30},{7,31},{8,4},{9,5},... | collective-permute-start | bytes 589832 | tf_op jit(solution)/shard_map/ppermute | solution.py:77
  12.6 17.0 %collective-permute-start.4 = (bf16[128,768]{1,0:T(8,128)(2,1)S(1)}, bf16[128,768]{1,0:T(8,128)(2,1)S(1)}, u32[]{:S(2)}, u32[]{:S(2)}) collective-permute-start(bf16[128,768]{1,0:T(8,128)(2,1)S(1)} %collective-permute-done.refs_0_), channel_id=1, source_target_pairs={{0,1},{1,0},{2,3},{3,2},{4,5},{5,4},{6,7},{7,6},{8,9},{9,8},{10,11... | collective-permute-start | bytes 589832 | tf_op jit(solution)/shard_map/ppermute | solution.py:68
  12.6 17.0 %collective-permute-start.5 = (bf16[128,768]{1,0:T(8,128)(2,1)S(1)}, bf16[128,768]{1,0:T(8,128)(2,1)S(1)}, u32[]{:S(2)}, u32[]{:S(2)}) collective-permute-start(bf16[128,768]{1,0:T(8,128)(2,1)S(1)} %collective-permute-done.1.refs_1_), channel_id=1, source_target_pairs={{0,1},{1,0},{2,3},{3,2},{4,5},{5,4},{6,7},{7,6},{8,9},{9,8},{10,11... | collective-permute-start | bytes 589832 | tf_op jit(solution)/shard_map/ppermute | solution.py:68
  13.1 25.7 %collective-permute-start.14 = (bf16[256,768]{1,0:T(8,128)(2,1)}, bf16[256,768]{1,0:T(8,128)(2,1)S(1)}, u32[]{:S(2)}, u32[]{:S(2)}) collective-permute-start(bf16[256,768]{1,0:T(8,128)(2,1)} %refs_8_.3), channel_id=1, source_target_pairs={{0,8},{1,9},{2,10},{3,11},{4,12},{5,13},{6,14},{7,15},{8,0},{9,1},... | collective-permute-start | bytes 1179656 | tf_op jit(solution)/shard_map/ppermute | solution.py:71
  20.2 30.4 %collective-permute-start.15 = (bf16[256,768]{1,0:T(8,128)(2,1)}, bf16[256,768]{1,0:T(8,128)(2,1)S(1)}, u32[]{:S(2)}, u32[]{:S(2)}) collective-permute-start(bf16[256,768]{1,0:T(8,128)(2,1)} %refs_8_.3), channel_id=1, source_target_pairs={{0,16},{1,17},{2,18},{3,19},{4,20},{5,21},{6,22},{7,23},{8,24},{9,... | collective-permute-start | bytes 1179656 | tf_op jit(solution)/shard_map/ppermute | solution.py:71
  28.1 22.4 %collective-permute-start.16 = (bf16[256,768]{1,0:T(8,128)(2,1)}, bf16[256,768]{1,0:T(8,128)(2,1)S(1)}, u32[]{:S(2)}, u32[]{:S(2)}) collective-permute-start(bf16[256,768]{1,0:T(8,128)(2,1)} %refs_8_.3), channel_id=1, source_target_pairs={{0,24},{1,25},{2,26},{3,27},{4,28},{5,29},{6,30},{7,31},{8,16},{9,... | collective-permute-start | bytes 1179656 | tf_op jit(solution)/shard_map/ppermute | solution.py:71
  29.6 1.4 %collective-permute-start.6 = (bf16[128,768]{1,0:T(8,128)(2,1)S(1)}, bf16[128,768]{1,0:T(8,128)(2,1)S(1)}, u32[]{:S(2)}, u32[]{:S(2)}) collective-permute-start(bf16[128,768]{1,0:T(8,128)(2,1)S(1)} %collective-permute-done.2.refs_2_), channel_id=1, source_target_pairs={{0,1},{1,0},{2,3},{3,2},{4,5},{5,4},{6,7},{7,6},{8,9},{9,8},{10,11... | collective-permute-start | bytes 589832 | tf_op jit(solution)/shard_map/ppermute | solution.py:68
  29.6 1.7 %collective-permute-start.7 = (bf16[128,768]{1,0:T(8,128)(2,1)S(1)}, bf16[128,768]{1,0:T(8,128)(2,1)S(1)}, u32[]{:S(2)}, u32[]{:S(2)}) collective-permute-start(bf16[128,768]{1,0:T(8,128)(2,1)S(1)} %collective-permute-done.3.refs_3_), channel_id=1, source_target_pairs={{0,1},{1,0},{2,3},{3,2},{4,5},{5,4},{6,7},{7,6},{8,9},{9,8},{10,11... | collective-permute-start | bytes 589832 | tf_op jit(solution)/shard_map/ppermute | solution.py:68
  31.3 1.0 %copy-start.3 = (bf16[1536,128]{1,0:T(8,128)(2,1)S(1)}, bf16[1536,128]{1,0:T(8,128)(2,1)}, u32[]{:S(2)}) copy-start(bf16[1536,128]{1,0:T(8,128)(2,1)} %refs_8_.2) | copy-start | bytes 1179652
  32.3 1.0 %copy-start.4 = (bf16[1536,128]{1,0:T(8,128)(2,1)S(1)}, bf16[1536,128]{1,0:T(8,128)(2,1)}, u32[]{:S(2)}) copy-start(bf16[1536,128]{1,0:T(8,128)(2,1)} %refs_9_.1) | copy-start | bytes 1179652
  33.3 1.0 %copy-start.5 = (bf16[1536,128]{1,0:T(8,128)(2,1)S(1)}, bf16[1536,128]{1,0:T(8,128)(2,1)}, u32[]{:S(2)}) copy-start(bf16[1536,128]{1,0:T(8,128)(2,1)} %refs_10_.1) | copy-start | bytes 1179652
  34.3 16.2 %copy-start.7 = (bf16[128,768]{1,0:T(8,128)(2,1)S(1)}, bf16[128,768]{1,0:T(8,128)(2,1)}, u32[]{:S(2)}) copy-start(bf16[128,768]{1,0:T(8,128)(2,1)} %refs_0_.1) | copy-start | bytes 589828
  35.3 4.9 %copy-start.10 = (f32[768]{0:T(1024)S(1)}, f32[768]{0:T(1024)}, u32[]{:S(2)}) copy-start(f32[768]{0:T(1024)} %param.20) | copy-start | bytes 9220
  35.3 17.1 %collective-permute-start.10 = (bf16[768,128]{1,0:T(8,128)(2,1)S(1)}, bf16[768,128]{1,0:T(8,128)(2,1)S(1)}, u32[]{:S(2)}, u32[]{:S(2)}) collective-permute-start(bf16[768,128]{1,0:T(8,128)(2,1)S(1)} %get-tuple-element.21), channel_id=1, source_target_pairs={{0,24},{1,25},{2,26},{3,27},{4,28},{5,29},{6,30},{7,31},{8,16},{9,... | collective-permute-start | bytes 589832 | tf_op jit(solution)/shard_map/ppermute | solution.py:71
  36.9 15.6 %collective-permute-start.8 = (bf16[768,128]{1,0:T(8,128)(2,1)S(1)}, bf16[768,128]{1,0:T(8,128)(2,1)S(1)}, u32[]{:S(2)}, u32[]{:S(2)}) collective-permute-start(bf16[768,128]{1,0:T(8,128)(2,1)S(1)} %get-tuple-element.19), channel_id=1, source_target_pairs={{0,8},{1,9},{2,10},{3,11},{4,12},{5,13},{6,14},{7,15},{8,0},{9,1},... | collective-permute-start | bytes 589832 | tf_op jit(solution)/shard_map/ppermute | solution.py:71
  38.8 17.3 %collective-permute-start.9 = (bf16[768,128]{1,0:T(8,128)(2,1)S(1)}, bf16[768,128]{1,0:T(8,128)(2,1)S(1)}, u32[]{:S(2)}, u32[]{:S(2)}) collective-permute-start(bf16[768,128]{1,0:T(8,128)(2,1)S(1)} %get-tuple-element.20), channel_id=1, source_target_pairs={{0,16},{1,17},{2,18},{3,19},{4,20},{5,21},{6,22},{7,23},{8,24},{9,... | collective-permute-start | bytes 589832 | tf_op jit(solution)/shard_map/ppermute | solution.py:71
  40.2 11.1 %copy-start.1 = (bf16[2048,128]{1,0:T(8,128)(2,1)S(1)}, bf16[2048,128]{1,0:T(8,128)(2,1)}, u32[]{:S(2)}) copy-start(bf16[2048,128]{1,0:T(8,128)(2,1)} %key_ref.1) | copy-start | bytes 1572868
  40.2 11.1 %copy-start.2 = (bf16[2048,128]{1,0:T(8,128)(2,1)S(1)}, bf16[2048,128]{1,0:T(8,128)(2,1)}, u32[]{:S(2)}) copy-start(bf16[2048,128]{1,0:T(8,128)(2,1)} %value_ref.1) | copy-start | bytes 1572868
  51.2 0.7 copy-start.8
  51.2 10.8 %collective-permute-start.17 = (bf16[4,128,128]{2,1,0:T(8,128)(2,1)S(1)}, bf16[4,128,128]{2,1,0:T(8,128)(2,1)S(1)}, u32[]{:S(2)}, u32[]{:S(2)}) collective-permute-start(bf16[4,128,128]{2,1,0:T(8,128)(2,1)S(1)} %get-tuple-element.29), channel_id=1, source_target_pairs={{0,1},{1,0},{2,3},{3,2},{4,5},{5,4},{6,7},{7,6},{8,9},{9,8},{10,11... | collective-permute-start | bytes 393224 | tf_op jit(solution)/shard_map/ppermute | solution.py:68
  56.1 0.7 copy-start.9
  58.5 4.0 %collective-permute-start.11 = (bf16[144,128]{1,0:T(8,128)(2,1)S(1)}, bf16[144,128]{1,0:T(8,128)(2,1)S(1)}, u32[]{:S(2)}, u32[]{:S(2)}) collective-permute-start(bf16[144,128]{1,0:T(8,128)(2,1)S(1)} %get-tuple-element.25), channel_id=1, source_target_pairs={{0,8},{1,9},{2,10},{3,11},{4,12},{5,13},{6,14},{7,15},{8,0},{9,1},... | collective-permute-start | bytes 110600 | tf_op jit(solution)/shard_map/ppermute | solution.py:71
  59.2 4.0 %collective-permute-start.12 = (bf16[144,128]{1,0:T(8,128)(2,1)S(1)}, bf16[144,128]{1,0:T(8,128)(2,1)S(1)}, u32[]{:S(2)}, u32[]{:S(2)}) collective-permute-start(bf16[144,128]{1,0:T(8,128)(2,1)S(1)} %get-tuple-element.26), channel_id=1, source_target_pairs={{0,16},{1,17},{2,18},{3,19},{4,20},{5,21},{6,22},{7,23},{8,24},{9,... | collective-permute-start | bytes 110600 | tf_op jit(solution)/shard_map/ppermute | solution.py:71
  60.9 4.9 %collective-permute-start.13 = (bf16[144,128]{1,0:T(8,128)(2,1)S(1)}, bf16[144,128]{1,0:T(8,128)(2,1)S(1)}, u32[]{:S(2)}, u32[]{:S(2)}) collective-permute-start(bf16[144,128]{1,0:T(8,128)(2,1)S(1)} %get-tuple-element.27), channel_id=1, source_target_pairs={{0,24},{1,25},{2,26},{3,27},{4,28},{5,29},{6,30},{7,31},{8,16},{9,... | collective-permute-start | bytes 110600 | tf_op jit(solution)/shard_map/ppermute | solution.py:71
  65.7 10.6 %copy-start.6 = (bf16[128,768]{1,0:T(8,128)(2,1)S(1)}, bf16[128,768]{1,0:T(8,128)(2,1)}, u32[]{:S(2)}) copy-start(bf16[128,768]{1,0:T(8,128)(2,1)} %refs_12_.1) | copy-start | bytes 589828
  65.8 4.5 %collective-permute-start.18 = (bf16[256,128]{1,0:T(8,128)(2,1)S(1)}, bf16[256,128]{1,0:T(8,128)(2,1)S(1)}, u32[]{:S(2)}, u32[]{:S(2)}) collective-permute-start(bf16[256,128]{1,0:T(8,128)(2,1)S(1)} %get-tuple-element.31), channel_id=1, source_target_pairs={{0,2},{1,3},{2,0},{3,1},{4,6},{5,7},{6,4},{7,5},{8,10},{9,11},{10,... | collective-permute-start | bytes 196616 | tf_op jit(solution)/shard_map/ppermute | solution.py:74
  66.4 6.6 %collective-permute-start.19 = (bf16[256,128]{1,0:T(8,128)(2,1)S(1)}, bf16[256,128]{1,0:T(8,128)(2,1)S(1)}, u32[]{:S(2)}, u32[]{:S(2)}) collective-permute-start(bf16[256,128]{1,0:T(8,128)(2,1)S(1)} %get-tuple-element.32), channel_id=1, source_target_pairs={{0,4},{1,5},{2,6},{3,7},{4,0},{5,1},{6,2},{7,3},{8,12},{9,13},{10,... | collective-permute-start | bytes 196616 | tf_op jit(solution)/shard_map/ppermute | solution.py:74
  69.0 6.1 %collective-permute-start.20 = (bf16[256,128]{1,0:T(8,128)(2,1)S(1)}, bf16[256,128]{1,0:T(8,128)(2,1)S(1)}, u32[]{:S(2)}, u32[]{:S(2)}) collective-permute-start(bf16[256,128]{1,0:T(8,128)(2,1)S(1)} %get-tuple-element.33), channel_id=1, source_target_pairs={{0,6},{1,7},{2,4},{3,5},{4,2},{5,3},{6,0},{7,1},{8,14},{9,15},{10,... | collective-permute-start | bytes 196616 | tf_op jit(solution)/shard_map/ppermute | solution.py:74
  70.3 4.8 %collective-permute-start.21 = (bf16[256,128]{1,0:T(8,128)(2,1)S(1)}, bf16[256,128]{1,0:T(8,128)(2,1)S(1)}, u32[]{:S(2)}, u32[]{:S(2)}) collective-permute-start(bf16[256,128]{1,0:T(8,128)(2,1)S(1)} %get-tuple-element.30.refs_0_), channel_id=1, source_target_pairs={{0,1},{1,0},{2,3},{3,2},{4,5},{5,4},{6,7},{7,6},{8,9},{9,8},{10,11... | collective-permute-start | bytes 196616 | tf_op jit(solution)/shard_map/ppermute | solution.py:68
  70.3 4.8 %collective-permute-start.22 = (bf16[256,128]{1,0:T(8,128)(2,1)S(1)}, bf16[256,128]{1,0:T(8,128)(2,1)S(1)}, u32[]{:S(2)}, u32[]{:S(2)}) collective-permute-start(bf16[256,128]{1,0:T(8,128)(2,1)S(1)} %collective-permute-done.18.refs_1_), channel_id=1, source_target_pairs={{0,1},{1,0},{2,3},{3,2},{4,5},{5,4},{6,7},{7,6},{8,9},{9,8},{10,11... | collective-permute-start | bytes 196616 | tf_op jit(solution)/shard_map/ppermute | solution.py:68
  72.9 2.2 %collective-permute-start.23 = (bf16[256,128]{1,0:T(8,128)(2,1)S(1)}, bf16[256,128]{1,0:T(8,128)(2,1)S(1)}, u32[]{:S(2)}, u32[]{:S(2)}) collective-permute-start(bf16[256,128]{1,0:T(8,128)(2,1)S(1)} %collective-permute-done.19.refs_2_), channel_id=1, source_target_pairs={{0,1},{1,0},{2,3},{3,2},{4,5},{5,4},{6,7},{7,6},{8,9},{9,8},{10,11... | collective-permute-start | bytes 196616 | tf_op jit(solution)/shard_map/ppermute | solution.py:68
  75.1 1.3 %collective-permute-start.24 = (bf16[256,128]{1,0:T(8,128)(2,1)S(1)}, bf16[256,128]{1,0:T(8,128)(2,1)S(1)}, u32[]{:S(2)}, u32[]{:S(2)}) collective-permute-start(bf16[256,128]{1,0:T(8,128)(2,1)S(1)} %collective-permute-done.20.refs_3_), channel_id=1, source_target_pairs={{0,1},{1,0},{2,3},{3,2},{4,5},{5,4},{6,7},{7,6},{8,9},{9,8},{10,11... | collective-permute-start | bytes 196616 | tf_op jit(solution)/shard_map/ppermute | solution.py:68

commit v2 on v1

v2 whole, which is shorter than its diff:
```python
import math

import jax
import jax.numpy as jnp
from jax import lax
from jax.experimental import pallas as pl
from jax.experimental.pallas import tpu as pltpu
from jax.sharding import PartitionSpec as P

epsilon = 1e-06
both = ("row", "col")
f32 = jnp.float32
bf16 = jnp.bfloat16
tail = 16


def size_of(arrays):
    return sum(math.prod(a.shape) * jnp.dtype(a.dtype).itemsize for a in arrays)


def call(kernel, name, operands, outs, scratch=(), far=0):
    moved = size_of(operands) + size_of(outs)
    held = moved + size_of(scratch)
    whole = pl.BlockSpec(memory_space=pltpu.VMEM)
    fetched = [pltpu.VMEM(a.shape, a.dtype) for a in operands[:far]]

    def fetch(*refs):
        n = len(operands) + len(outs)
        landed, sems = refs[n : n + far], refs[-1]
        copies = [pltpu.make_async_copy(refs[i], landed[i], sems.at[i]) for i in range(far)]
        for copy in copies:
            copy.start()
        for copy in copies:
            copy.wait()
        kernel(*landed, *refs[far:n], *refs[n + far : -1])

    return pl.pallas_call(
        fetch if far else kernel,
        out_shape=list(outs),
        in_specs=[pl.BlockSpec(memory_space=pl.ANY)] * far + [whole] * (len(operands) - far),
        out_specs=[whole] * len(outs),
        scratch_shapes=[*fetched, *scratch] + ([pltpu.SemaphoreType.DMA((far,))] if far else []),
        compiler_params=pltpu.CompilerParams(vmem_limit_bytes=2 * held + (12 << 20)),
        cost_estimate=pl.CostEstimate(flops=0, bytes_accessed=0, transcendentals=0),
        name=name,
    )(*(pltpu.with_memory_space_constraint(a, pltpu.HBM) for a in operands[:far]), *operands[far:])


def dot(a, b):
    return jnp.dot(a, b, preferred_element_type=f32)


def dot_last(a, b):
    return lax.dot_general(a, b, (((1,), (1,)), ((), ())), preferred_element_type=f32)


def normed(wide, gain):
    mean_square = jnp.mean(wide * wide, axis=-1, keepdims=True)
    return wide * lax.rsqrt(mean_square + epsilon) * gain


def solution(mesh):
    R, C = mesh.shape["row"], mesh.shape["col"]
    k = C // R
    assert C == R * k and k == 2 and R & (R - 1) == 0

    def here():
        f, c = lax.axis_index("row"), lax.axis_index("col")
        return f, c // k, c % k

    def route(to):
        return [
            (r * C + z * k + q, (lambda a, b, e: a * C + b * k + e)(*to(r, z, q)))
            for r in range(R)
            for z in range(R)
            for q in range(k)
        ]

    def across_chip(x):
        return lax.ppermute(x, both, route(lambda r, z, q: (r, z, q ^ 1)))

    def over_row(x, s):
        return lax.ppermute(x, both, route(lambda r, z, q: (r ^ s, z, q)))

    def over_z(x, m):
        return lax.ppermute(x, both, route(lambda r, z, q: (r, z ^ m, q)))

    def turned(x, d):
        return lax.ppermute(x, both, route(lambda r, z, q: (z, r ^ z ^ d, q)))

    def body(
        tokens,
        w_query,
        w_key,
        w_value,
        w_out,
        key_cache,
        value_cache,
        query_gain,
        key_gain,
        out_gate,
        cotangent,
    ):
        T, F = tokens.shape
        H = query_gain.shape[0]
        cached = key_cache.shape[0]
        wide_out = w_out.shape[1]
        assert w_query.shape == (k * F, H) and w_out.shape == (k * H, wide_out) and T == H
        query_gain = query_gain.reshape(1, H)
        key_gain = key_gain.reshape(1, H)
        out_gate = out_gate.reshape(1, wide_out)
        fold = H ** (-0.5) * math.log2(math.e)

        near = [s for s in range(1, R) if s & (s - 1) == 0]
        out_rows = {0: w_out, **{s: over_row(w_out, s) for s in near}}
        order = [d for d in range(R) if d.bit_count() % 2 == 0][::-1]
        mine = {d: turned(tokens, d) for d in order}
        mine.update({d ^ 1: over_z(mine[d], 1) for d in order})
        half = k * H // 2
        for s in range(1, R):
            low = s & -s
            top = s ^ low
            if top in near:
                out_rows[s] = (
                    over_row(out_rows[top][:half], low),
                    over_row(out_rows[low][half:], top),
                )
            elif top:
                out_rows[s] = (over_row(w_out, s),)

        def prepare(key_ref, value_ref, wq, wk, wv, qg, kg, key_out, value_out, weight_out, gain_out):
            key = normed(key_ref[...].astype(f32), kg[...])
            key_out[...] = key.T.astype(bf16)
            value_out[:, :H] = value_ref[...]
            value_out[:, H:] = jnp.ones((cached, H), bf16)
            weight_out[:, :H] = wq[...]
            weight_out[:, H : 2 * H] = wk[...]
            weight_out[:, 2 * H :] = wv[...]
            gain_out[0:1, :] = qg[...] * fold
            gain_out[1:2, :] = kg[...]

        keys_t, values_one, weights, gains = call(
            prepare,
            "prepare",
            (key_cache, value_cache, w_query, w_key, w_value, query_gain, key_gain),
            [
                jax.ShapeDtypeStruct((H, cached), bf16),
                jax.ShapeDtypeStruct((cached, 2 * H), bf16),
                jax.ShapeDtypeStruct((k * F, 3 * H), bf16),
                jax.ShapeDtypeStruct((2, H), f32),
            ],
            far=7,
        )

        def project(*refs):
            mine_refs, other_refs, weight_ref = refs[:R], refs[R : 2 * R], refs[2 * R]
            outs, held = refs[2 * R + 1 : 3 * R + 1], refs[-1]
            f, z, q = here()
            w_mine = weight_ref[pl.ds(pl.multiple_of(q * F, F), F), :]
            w_other = weight_ref[pl.ds(pl.multiple_of((1 - q) * F, F), F), :]
            for d in range(R):
                part = (dot(mine_refs[d][...], w_mine) + dot(other_refs[d][...], w_other)).astype(bf16)
                block = f ^ z ^ d
                rows = pl.ds(pl.multiple_of(block * T, T), T)
                for s in range(R):
                    outs[s][rows, :] = part[:, :H]
                held[block, :T] = part[:, H : 2 * H]
                held[block, T:] = part[:, 2 * H :]
            for s in range(R):
                outs[s][R * T :, :] = held[f ^ s]

        joined = lax.optimization_barrier(
            (
                list(mine.values()),
                [out_rows[s] for s in range(1, R)],
                [keys_t, values_one, weights, gains],
            )
        )
        slots, out_rows = dict(zip(mine, joined[0])), [w_out, *joined[1]]
        slots = [slots[d] for d in range(R)]
        keys_t, values_one, weights, gains = joined[2]
        out_rows = [x if not isinstance(x, tuple) else x[0] if len(x) == 1 else jnp.concatenate(x) for x in out_rows]
        slots_other = [across_chip(x) for x in slots]
        parts = call(
            project,
            "project",
            (*slots, *slots_other, weights),
            [jax.ShapeDtypeStruct(((R + 2) * T, H), bf16)] * R,
            [pltpu.VMEM((R, 2 * T, H), bf16)],
        )
        parts = [parts[0]] + [over_row(parts[s], s) for s in range(1, R)]
        def gradient(*refs):
            cot_ref, gate_ref = refs[:2]
            rows_refs, outs, held = refs[2 : 2 + R], refs[2 + R : 2 + 2 * R], refs[-1]
            f, z, q = here()
            scaled = (cot_ref[...].astype(f32) * gate_ref[...]).astype(bf16)
            for s in range(R):
                part = dot_last(scaled, rows_refs[s][...]).astype(bf16)
                even, odd = part[:, :H], part[:, H:]
                held[f ^ s, :T] = jnp.where(q == 0, even, odd)
                held[f ^ s, T:] = jnp.where(q == 0, odd, even)
            for m in range(R):
                outs[m][...] = held[z ^ m]

        sent = jax.ShapeDtypeStruct((k * T, H), bf16)
        grads = call(
            gradient,
            "gradient",
            (cotangent, out_gate, *out_rows),
            [sent] * R,
            [pltpu.VMEM((R, k * T, H), bf16)],
        )
        grads = [grads[0]] + [over_z(grads[m], m) for m in range(1, R)]

        parts, grads = lax.optimization_barrier((parts, grads))

        def join(*refs):
            own_ref, away_ref = refs[R:]
            both_heads = sum(ref[...].astype(f32) for ref in refs[:R])
            own_ref[...] = both_heads[:T].astype(bf16)
            away_ref[...] = both_heads[T:].astype(bf16)

        grad_own, grad_away = call(join, "join", grads, [jax.ShapeDtypeStruct((T, H), bf16)] * 2)
        grad_away = across_chip(grad_away)

        def attend(*refs):
            part_refs = refs[:R]
            keys_ref, values_ref, gain_ref = refs[R : R + 3]
            outs = refs[R + 3 : 2 * R + 3]
            query_ref, held = refs[2 * R + 3 :]
            f, _, _ = here()

            def total(rows):
                return sum(ref[rows, :].astype(f32) for ref in part_refs)

            query_ref[...] = normed(total(slice(0, R * T)), gain_ref[0:1, :]).astype(bf16)
            key_new = normed(total(slice(R * T, (R + 1) * T)), gain_ref[1:2, :]).astype(bf16)
            value_new = total(slice((R + 1) * T, (R + 2) * T)).astype(bf16)
            value_new = jnp.concatenate([value_new, jnp.ones_like(value_new)], axis=1)
            step = min(512, cached)
            eye = lax.broadcasted_iota(jnp.int32, (T, H), 0) == lax.broadcasted_iota(
                jnp.int32, (T, H), 1
            )

            def block(d, carry):
                query = query_ref[pl.ds(pl.multiple_of(d * T, T), T), :]
                weights = jnp.exp2(dot_last(query, key_new)).astype(bf16)
                sums = dot(weights, value_new)
                for j in range(0, cached, step):
                    weights = jnp.exp2(dot(query, keys_ref[:, j : j + step])).astype(bf16)
                    sums = sums + dot(weights, values_ref[j : j + step, :])
                held[d, :T] = sums[:, :H].astype(bf16)
                row = jnp.sum(jnp.where(eye, sums[:, H:], 0.0), axis=0, keepdims=True)
                high = row.astype(bf16).astype(f32)
                low = row - high
                which = lax.broadcasted_iota(jnp.int32, (tail, H), 0)
                held[d, T:] = jnp.where(which == 0, high, jnp.where(which == 1, low, 0.0)).astype(bf16)
                return carry

            lax.fori_loop(0, R, block, 0, unroll=min(R, 4))
            for s in range(R):
                outs[s][...] = held[f ^ s]

        sums = call(
            attend,
            "attend",
            (*parts, keys_t, values_one, gains),
            [jax.ShapeDtypeStruct((T + tail, H), bf16)] * R,
            [pltpu.VMEM((R * T, H), bf16), pltpu.VMEM((R, T + tail, H), bf16)],
        )
        sums = [sums[0]] + [over_row(sums[s], s) for s in range(1, R)]

        def finish(*refs):
            sum_refs, out = refs[:R], refs[R]
            numerators = sum(ref[:T, :].astype(f32) for ref in sum_refs)
            row = sum(ref[T : T + 1, :].astype(f32) + ref[T + 1 : T + 2, :].astype(f32) for ref in sum_refs)
            eye = lax.broadcasted_iota(jnp.int32, (T, H), 0) == lax.broadcasted_iota(
                jnp.int32, (T, H), 1
            )
            totals = jnp.sum(jnp.where(eye, row, 0.0), axis=1, keepdims=True)
            out[...] = (numerators / totals).astype(bf16)

        (attention,) = call(finish, "finish", sums, [jax.ShapeDtypeStruct((T, H), bf16)])
        heads = {0: attention}
        for bit in near:
            heads.update({m | bit: over_z(heads[m], bit) for m in list(heads)})
        heads = [heads[m] for m in range(R)]
        heads = [heads[0], *lax.optimization_barrier(heads[1:])]
        heads_other = [across_chip(x) for x in heads]

        def output(*refs):
            tokens_ref, gate_ref, own_ref, away_ref = refs[:4]
            mine_refs, other_refs, rows_refs = (refs[i * R + 4 : (i + 1) * R + 4] for i in range(3))
            layer_ref, grad_ref, held = refs[3 * R + 4 :]
            f, z, q = here()
            grad_ref[...] = (own_ref[...].astype(f32) + away_ref[...].astype(f32)).astype(bf16)
            for m in range(R):
                own, away = mine_refs[m][...], other_refs[m][...]
                held[z ^ m, :, :H] = jnp.where(q == 0, own, away)
                held[z ^ m, :, H:] = jnp.where(q == 0, away, own)
            branch = sum(dot(held[f ^ s], rows_refs[s][...]) for s in range(R))
            layer_ref[...] = (tokens_ref[...].astype(f32) + gate_ref[...] * branch).astype(bf16)

        layer_out, attention_cotangent = call(
            output,
            "output",
            (tokens, out_gate, grad_own, grad_away, *heads, *heads_other, *out_rows),
            [jax.ShapeDtypeStruct((T, wide_out), bf16), jax.ShapeDtypeStruct((T, H), bf16)],
            [pltpu.VMEM((R, T, k * H), bf16)],
        )
        return layer_out, attention_cotangent

    spread = P("row", "col")
    return jax.shard_map(
        body,
        mesh=mesh,
        in_specs=(spread,) * 7 + (P(), P(), P("col"), spread),
        out_specs=(spread, spread),
        check_vma=False,
    )
```

time: 77.7 us -> 69.2 us (0.89)
  starting transfers between devices: 42.8 us -> 35.4 us
  local copies, waits for them, and re-layouts: 4.22 us -> 0.08 us
  Pallas kernels: 5.2 us -> 7.2 us
  waiting for transfers between devices: 24.5 us -> 25.5 us
    ppermute x9 -> x10, waiting for transfers between devices: 17.6 us -> 5.3 us  [over_row(): return lax.ppermute(x, both, route(lambda r, z, q: (r ^ s, z, q)))]
    ppermute x9 -> x10, starting transfers between devices: 24.8 us -> 14.9 us  [over_row(): return lax.ppermute(x, both, route(lambda r, z, q: (r ^ s, z, q)))]
    ppermute x3 -> x8, waiting for transfers between devices: 4.28 us -> 11.6 us  [over_z(): return lax.ppermute(x, both, route(lambda r, z, q: (r, z ^ m, q)))]
    ppermute x3 -> x8, starting transfers between devices: 4.45 us -> 11.3 us  [over_z(): return lax.ppermute(x, both, route(lambda r, z, q: (r, z ^ m, q)))]
    ppermute x4 -> x2, waiting for transfers between devices: 0.12 us -> 6.21 us  [turned(): return lax.ppermute(x, both, route(lambda r, z, q: (z, r ^ z ^ d, q)))]
    ppermute x4 -> x2, starting transfers between devices: 11.9 us -> 7.09 us  [turned(): return lax.ppermute(x, both, route(lambda r, z, q: (z, r ^ z ^ d, q)))]
    unnamed x22 -> x9, local copies, waits for them, and re-layouts: 4.22 us -> 0.04 us
    pallas_call x6 -> x7, Pallas kernels: 5.2 us -> 7.2 us  [call(): pl.pallas_call(fetch if far else kernel, out_shape=list(outs), in_specs=[...]
  transfers between devices with their start and end apart: 25 -> 29, of which waited for: 11 -> 18; matrix products, arithmetic and copies ran while one was open for 0% -> 0% of each run, Pallas kernels for 5% -> 5%
where the time goes in v2:
time: 69.2 us; the launch traced here: 69 us
  starting transfers between devices  35.4 us (51%)
  waiting for transfers between devices  25.5 us (37%)
  Pallas kernels  7.2 us (10%)
  between operations  0.8 us (1%)
    ppermute x10, starting transfers between devices, over_row(): return lax.ppermute(x, both, route(lambda r, z, q: (r ^ s, z, q)))  14.9 us
    ppermute x8, waiting for transfers between devices, over_z(): return lax.ppermute(x, both, route(lambda r, z, q: (r, z ^ m, q)))  11.6 us
    ppermute x8, starting transfers between devices, over_z(): return lax.ppermute(x, both, route(lambda r, z, q: (r, z ^ m, q)))  11.3 us
    pallas_call x7, Pallas kernels, call(): pl.pallas_call(fetch if far else kernel, out_shape=list(outs), in_specs=[...  7.2 us
    ppermute x2, starting transfers between devices, turned(): return lax.ppermute(x, both, route(lambda r, z, q: (z, r ^ z ^ d, q)))  7.09 us
    ppermute x2, waiting for transfers between devices, turned(): return lax.ppermute(x, both, route(lambda r, z, q: (z, r ^ z ^ d, q)))  6.21 us
    ppermute x10, waiting for transfers between devices, over_row(): return lax.ppermute(x, both, route(lambda r, z, q: (r ^ s, z, q)))  5.3 us
    ppermute x9, waiting for transfers between devices, across_chip(): return lax.ppermute(x, both, route(lambda r, z, q: (r, z, q ^ 1)))  2.41 us
  transfers between devices with their start and end apart: 29, of which 18 were waited for; matrix products, arithmetic and copies ran while one was open for 0% of the time, Pallas kernels for 5%

profile of v2, /device:TPU:0, one launch (start us, length us, event | category | flops | bytes accessed | tf_op | source)
XLA Modules:
  0.0 69.0 jit_solution(9348805813264144263)
XLA Ops:
  0.6 3.0 %collective-permute-start.5 = (bf16[256,768]{1,0:T(8,128)(2,1)}, bf16[256,768]{1,0:T(8,128)(2,1)S(1)}, u32[]{:S(2)}, u32[]{:S(2)}) collective-permute-start(bf16[256,768]{1,0:T(8,128)(2,1)} %refs_12_.1), channel_id=1, source_target_pairs={{0,16},{1,17},{2,18},{3,19},{4,20},{5,21},{6,22},{7,23},{8,24},{9,... | collective-permute-start | bytes 1179656 | tf_op jit(solution)/shard_map/ppermute | solution.py:83
  3.7 1.5 %collective-permute-start.4 = (bf16[256,768]{1,0:T(8,128)(2,1)}, bf16[256,768]{1,0:T(8,128)(2,1)S(1)}, u32[]{:S(2)}, u32[]{:S(2)}) collective-permute-start(bf16[256,768]{1,0:T(8,128)(2,1)} %refs_12_.1), channel_id=1, source_target_pairs={{0,8},{1,9},{2,10},{3,11},{4,12},{5,13},{6,14},{7,15},{8,0},{9,1},... | collective-permute-start | bytes 1179656 | tf_op jit(solution)/shard_map/ppermute | solution.py:83
  5.2 5.5 %collective-permute-start = (bf16[128,768]{1,0:T(8,128)(2,1)}, bf16[128,768]{1,0:T(8,128)(2,1)S(1)}, u32[]{:S(2)}, u32[]{:S(2)}) collective-permute-start(bf16[128,768]{1,0:T(8,128)(2,1)} %refs_0_.5), channel_id=1, source_target_pairs={{0,6},{1,7},{2,12},{3,13},{4,18},{5,19},{6,24},{7,25},{8,4},{9,5},... | collective-permute-start | bytes 589832 | tf_op jit(solution)/shard_map/ppermute | solution.py:89
  10.7 1.6 %collective-permute-start.1 = (bf16[128,768]{1,0:T(8,128)(2,1)}, bf16[128,768]{1,0:T(8,128)(2,1)S(1)}, u32[]{:S(2)}, u32[]{:S(2)}) collective-permute-start(bf16[128,768]{1,0:T(8,128)(2,1)} %refs_0_.5), channel_id=1, source_target_pairs={{0,0},{1,1},{2,10},{3,11},{4,20},{5,21},{6,30},{7,31},{8,2},{9,3},... | collective-permute-start | bytes 589832 | tf_op jit(solution)/shard_map/ppermute | solution.py:89
  12.2 6.2 %collective-permute-done.refs_3_ = bf16[128,768]{1,0:T(8,128)(2,1)S(1)} collective-permute-done((bf16[128,768]{1,0:T(8,128)(2,1)}, bf16[128,768]{1,0:T(8,128)(2,1)S(1)}, u32[]{:S(2)}, u32[]{:S(2)}) %collective-permute-start) | collective-permute-done | bytes 196640 | tf_op jit(solution)/shard_map/ppermute | solution.py:89
  18.5 2.6 %collective-permute-start.3 = (bf16[128,768]{1,0:T(8,128)(2,1)S(1)}, bf16[128,768]{1,0:T(8,128)(2,1)S(1)}, u32[]{:S(2)}, u32[]{:S(2)}) collective-permute-start(bf16[128,768]{1,0:T(8,128)(2,1)S(1)} %collective-permute-done.1.refs_0_), channel_id=1, source_target_pairs={{0,2},{1,3},{2,0},{3,1},{4,6},{5,7},{6,4},{7,5},{8,10},{9,11},{10,... | collective-permute-start | bytes 589832 | tf_op jit(solution)/shard_map/ppermute | solution.py:86
  21.1 3.2 %collective-permute-start.6 = (bf16[128,768]{1,0:T(8,128)(2,1)S(1)}, bf16[128,768]{1,0:T(8,128)(2,1)S(1)}, u32[]{:S(2)}, u32[]{:S(2)}) collective-permute-start(bf16[128,768]{1,0:T(8,128)(2,1)S(1)} %slice.8), channel_id=1, source_target_pairs={{0,8},{1,9},{2,10},{3,11},{4,12},{5,13},{6,14},{7,15},{8,0},{9,1},... | collective-permute-start | bytes 589832 | tf_op jit(solution)/shard_map/ppermute | solution.py:83
  24.3 0.1 collective-permute-start.7
  24.4 2.5 %prepare.1 = (bf16[128,2048]{1,0:T(8,128)(2,1)S(1)}, bf16[2048,256]{1,0:T(8,128)(2,1)S(1)}, bf16[1536,384]{1,0:T(8,128)(2,1)S(1)}, f32[2,128]{1,0:T(2,128)S(1)}) custom-call(bf16[2048,128]{1,0:T(8,128)(2,1)} %refs_0_.3, bf16[2048,128]{1,0:T(8,128)(2,1)} %refs_1_.1, bf16[1536,128]{1,0:T(8,128)(2,1)} %refs_2_.2, bf16[1536,128]{1,0:T(8,128)(2,1)} %refs_3_.1, ...), custom_call_target="tpu_custom_call" | custom-call | tf_op jit(solution)/shard_map/prepare/pallas_call | solution.py:37
  26.9 1.6 %collective-permute-done.3.refs_1_ = bf16[128,768]{1,0:T(8,128)(2,1)S(1)} collective-permute-done((bf16[128,768]{1,0:T(8,128)(2,1)S(1)}, bf16[128,768]{1,0:T(8,128)(2,1)S(1)}, u32[]{:S(2)}, u32[]{:S(2)}) %collective-permute-start.3) | collective-permute-done | bytes 196640 | tf_op jit(solution)/shard_map/ppermute | solution.py:86
  28.4 1.6 %collective-permute-done.7 = bf16[128,768]{1,0:T(8,128)(2,1)S(1)} collective-permute-done((bf16[128,768]{1,0:T(8,128)(2,1)S(1)}, bf16[128,768]{1,0:T(8,128)(2,1)S(1)}, u32[]{:S(2)}, u32[]{:S(2)}) %collective-permute-start.7) | collective-permute-done | bytes 196640 | tf_op jit(solution)/shard_map/ppermute | solution.py:83
  30.0 0.5 collective-permute-start.9
  30.5 0.5 collective-permute-start.11
  31.1 0.4 collective-permute-done.8.refs_4_
  31.5 0.3 collective-permute-done.9.refs_5_
  31.7 0.3 collective-permute-done.10.refs_6_
  32.0 0.3 collective-permute-done.11.refs_7_
  32.3 1.0 %project.1 = (bf16[768,128]{1,0:T(8,128)(2,1)S(1)}, bf16[768,128]{1,0:T(8,128)(2,1)S(1)}, bf16[768,128]{1,0:T(8,128)(2,1)S(1)}, bf16[768,128]{1,0:T(8,128)(2,1)S(1)}) custom-call(bf16[128,768]{1,0:T(8,128)(2,1)S(1)} %collective-permute-done.1.refs_0_, bf16[128,768]{1,0:T(8,128)(2,1)S(1)} %collective-permute-done.3.refs_1_, ...), custom_call_target="tpu_custom_call" | custom-call | tf_op jit(solution)/shard_map/project/pallas_call | solution.py:37
  33.3 1.5 %collective-permute-start.12 = (bf16[768,128]{1,0:T(8,128)(2,1)S(1)}, bf16[768,128]{1,0:T(8,128)(2,1)S(1)}, u32[]{:S(2)}, u32[]{:S(2)}) collective-permute-start(bf16[768,128]{1,0:T(8,128)(2,1)S(1)} %get-tuple-element.53), channel_id=1, source_target_pairs={{0,8},{1,9},{2,10},{3,11},{4,12},{5,13},{6,14},{7,15},{8,0},{9,1},... | collective-permute-start | bytes 589832 | tf_op jit(solution)/shard_map/ppermute | solution.py:83
  34.8 0.3 collective-permute-start.13
  35.2 1.7 %collective-permute-start.14 = (bf16[768,128]{1,0:T(8,128)(2,1)S(1)}, bf16[768,128]{1,0:T(8,128)(2,1)S(1)}, u32[]{:S(2)}, u32[]{:S(2)}) collective-permute-start(bf16[768,128]{1,0:T(8,128)(2,1)S(1)} %get-tuple-element.55), channel_id=1, source_target_pairs={{0,24},{1,25},{2,26},{3,27},{4,28},{5,29},{6,30},{7,31},{8,16},{9,... | collective-permute-start | bytes 589832 | tf_op jit(solution)/shard_map/ppermute | solution.py:83
  36.9 0.7 gradient.1
  37.6 2.1 %collective-permute-start.15 = (bf16[256,128]{1,0:T(8,128)(2,1)S(1)}, bf16[256,128]{1,0:T(8,128)(2,1)S(1)}, u32[]{:S(2)}, u32[]{:S(2)}) collective-permute-start(bf16[256,128]{1,0:T(8,128)(2,1)S(1)} %get-tuple-element.61), channel_id=1, source_target_pairs={{0,2},{1,3},{2,0},{3,1},{4,6},{5,7},{6,4},{7,5},{8,10},{9,11},{10,... | collective-permute-start | bytes 196616 | tf_op jit(solution)/shard_map/ppermute | solution.py:86
  39.7 0.9 %collective-permute-start.16 = (bf16[256,128]{1,0:T(8,128)(2,1)S(1)}, bf16[256,128]{1,0:T(8,128)(2,1)S(1)}, u32[]{:S(2)}, u32[]{:S(2)}) collective-permute-start(bf16[256,128]{1,0:T(8,128)(2,1)S(1)} %get-tuple-element.62), channel_id=1, source_target_pairs={{0,4},{1,5},{2,6},{3,7},{4,0},{5,1},{6,2},{7,3},{8,12},{9,13},{10,... | collective-permute-start | bytes 196616 | tf_op jit(solution)/shard_map/ppermute | solution.py:86
  40.6 1.3 %collective-permute-done.15.refs_1_ = bf16[256,128]{1,0:T(8,128)(2,1)S(1)} collective-permute-done((bf16[256,128]{1,0:T(8,128)(2,1)S(1)}, bf16[256,128]{1,0:T(8,128)(2,1)S(1)}, u32[]{:S(2)}, u32[]{:S(2)}) %collective-permute-start.15) | collective-permute-done | bytes 65568 | tf_op jit(solution)/shard_map/ppermute | solution.py:86
  42.0 2.3 %collective-permute-start.17 = (bf16[256,128]{1,0:T(8,128)(2,1)S(1)}, bf16[256,128]{1,0:T(8,128)(2,1)S(1)}, u32[]{:S(2)}, u32[]{:S(2)}) collective-permute-start(bf16[256,128]{1,0:T(8,128)(2,1)S(1)} %get-tuple-element.63), channel_id=1, source_target_pairs={{0,6},{1,7},{2,4},{3,5},{4,2},{5,3},{6,0},{7,1},{8,14},{9,15},{10,... | collective-permute-start | bytes 196616 | tf_op jit(solution)/shard_map/ppermute | solution.py:86
  44.2 2.6 %collective-permute-done.16.refs_2_ = bf16[256,128]{1,0:T(8,128)(2,1)S(1)} collective-permute-done((bf16[256,128]{1,0:T(8,128)(2,1)S(1)}, bf16[256,128]{1,0:T(8,128)(2,1)S(1)}, u32[]{:S(2)}, u32[]{:S(2)}) %collective-permute-start.16) | collective-permute-done | bytes 65568 | tf_op jit(solution)/shard_map/ppermute | solution.py:86
  46.8 1.3 %collective-permute-done.17.refs_3_ = bf16[256,128]{1,0:T(8,128)(2,1)S(1)} collective-permute-done((bf16[256,128]{1,0:T(8,128)(2,1)S(1)}, bf16[256,128]{1,0:T(8,128)(2,1)S(1)}, u32[]{:S(2)}, u32[]{:S(2)}) %collective-permute-start.17) | collective-permute-done | bytes 65568 | tf_op jit(solution)/shard_map/ppermute | solution.py:86
  48.1 1.8 %attend.1 = (bf16[144,128]{1,0:T(8,128)(2,1)S(1)}, bf16[144,128]{1,0:T(8,128)(2,1)S(1)}, bf16[144,128]{1,0:T(8,128)(2,1)S(1)}, bf16[144,128]{1,0:T(8,128)(2,1)S(1)}) custom-call(bf16[768,128]{1,0:T(8,128)(2,1)S(1)} %get-tuple-element.70.refs_0_, bf16[768,128]{1,0:T(8,128)(2,1)S(1)} %collective-permute-done.12.refs_1_, ...), custom_call_target="tpu_custom_call" | custom-call | tf_op jit(solution)/shard_map/attend/pallas_call | solution.py:37
  49.9 2.1 %collective-permute-start.19 = (bf16[144,128]{1,0:T(8,128)(2,1)S(1)}, bf16[144,128]{1,0:T(8,128)(2,1)S(1)}, u32[]{:S(2)}, u32[]{:S(2)}) collective-permute-start(bf16[144,128]{1,0:T(8,128)(2,1)S(1)} %get-tuple-element.78), channel_id=1, source_target_pairs={{0,8},{1,9},{2,10},{3,11},{4,12},{5,13},{6,14},{7,15},{8,0},{9,1},... | collective-permute-start | bytes 110600 | tf_op jit(solution)/shard_map/ppermute | solution.py:83
  52.0 0.4 collective-permute-start.20
  52.4 1.1 %collective-permute-start.21 = (bf16[144,128]{1,0:T(8,128)(2,1)S(1)}, bf16[144,128]{1,0:T(8,128)(2,1)S(1)}, u32[]{:S(2)}, u32[]{:S(2)}) collective-permute-start(bf16[144,128]{1,0:T(8,128)(2,1)S(1)} %get-tuple-element.80), channel_id=1, source_target_pairs={{0,24},{1,25},{2,26},{3,27},{4,28},{5,29},{6,30},{7,31},{8,16},{9,... | collective-permute-start | bytes 110600 | tf_op jit(solution)/shard_map/ppermute | solution.py:83
  53.5 0.4 collective-permute-done.19.refs_1_
  54.0 2.0 %collective-permute-done.20.refs_2_ = bf16[144,128]{1,0:T(8,128)(2,1)S(1)} collective-permute-done((bf16[144,128]{1,0:T(8,128)(2,1)S(1)}, bf16[144,128]{1,0:T(8,128)(2,1)S(1)}, u32[]{:S(2)}, u32[]{:S(2)}) %collective-permute-start.20) | collective-permute-done | bytes 36896 | tf_op jit(solution)/shard_map/ppermute | solution.py:83
  56.0 1.3 %collective-permute-done.21.refs_3_ = bf16[144,128]{1,0:T(8,128)(2,1)S(1)} collective-permute-done((bf16[144,128]{1,0:T(8,128)(2,1)S(1)}, bf16[144,128]{1,0:T(8,128)(2,1)S(1)}, u32[]{:S(2)}, u32[]{:S(2)}) %collective-permute-start.21) | collective-permute-done | bytes 36896 | tf_op jit(solution)/shard_map/ppermute | solution.py:83
  57.3 0.1 finish.1.refs_4_
  57.4 0.1 collective-permute-start.22
  57.4 2.7 %collective-permute-start.23 = (bf16[128,128]{1,0:T(8,128)(2,1)S(1)}, bf16[128,128]{1,0:T(8,128)(2,1)S(1)}, u32[]{:S(2)}, u32[]{:S(2)}) collective-permute-start(bf16[128,128]{1,0:T(8,128)(2,1)S(1)} %finish.1.refs_4_), channel_id=1, source_target_pairs={{0,4},{1,5},{2,6},{3,7},{4,0},{5,1},{6,2},{7,3},{8,12},{9,13},{10,... | collective-permute-start | bytes 98312 | tf_op jit(solution)/shard_map/ppermute | solution.py:86
  60.1 1.2 %collective-permute-done.22.refs_5_ = bf16[128,128]{1,0:T(8,128)(2,1)S(1)} collective-permute-done((bf16[128,128]{1,0:T(8,128)(2,1)S(1)}, bf16[128,128]{1,0:T(8,128)(2,1)S(1)}, u32[]{:S(2)}, u32[]{:S(2)}) %collective-permute-start.22) | collective-permute-done | bytes 32800 | tf_op jit(solution)/shard_map/ppermute | solution.py:86
  61.3 0.6 collective-permute-start.24
  62.0 0.1 collective-permute-start.18
  62.1 0.5 collective-permute-start.25
  62.6 3.5 %collective-permute-done.24.refs_7_ = bf16[128,128]{1,0:T(8,128)(2,1)S(1)} collective-permute-done((bf16[128,128]{1,0:T(8,128)(2,1)S(1)}, bf16[128,128]{1,0:T(8,128)(2,1)S(1)}, u32[]{:S(2)}, u32[]{:S(2)}) %collective-permute-start.24) | collective-permute-done | bytes 32800 | tf_op jit(solution)/shard_map/ppermute | solution.py:86
  66.2 0.5 collective-permute-start.27
  66.7 0.7 collective-permute-done.26.refs_9_
  67.4 0.2 collective-permute-done.27.refs_10_
  67.5 0.3 collective-permute-done.28.refs_11_
  67.9 1.1 %output.1 = (bf16[128,768]{1,0:T(8,128)(2,1)}, bf16[128,128]{1,0:T(8,128)(2,1)}) custom-call(bf16[128,768]{1,0:T(8,128)(2,1)S(1)} %copy-done.1, f32[1,768]{1,0:T(1,128)S(1)} %reshape.13.refs_1_, bf16[128,128]{1,0:T(8,128)(2,1)S(1)} %get-tuple-element.68.refs_2_, bf16[128,128]{1,0:T(8,128)(2,1)S(1)} %collective-permute-done.18.refs_3_, ...), custom_call_target="tpu_custom_call" | custom-call | tf_op jit(solution)/shard_map/output/pallas_call | solution.py:37
  (30 shorter events, 0.2 us)
Async XLA Ops:
  0.6 20.5 %collective-permute-start.5 = (bf16[256,768]{1,0:T(8,128)(2,1)}, bf16[256,768]{1,0:T(8,128)(2,1)S(1)}, u32[]{:S(2)}, u32[]{:S(2)}) collective-permute-start(bf16[256,768]{1,0:T(8,128)(2,1)} %refs_12_.1), channel_id=1, source_target_pairs={{0,16},{1,17},{2,18},{3,19},{4,20},{5,21},{6,22},{7,23},{8,24},{9,... | collective-permute-start | bytes 1179656 | tf_op jit(solution)/shard_map/ppermute | solution.py:83
  3.7 20.6 %collective-permute-start.4 = (bf16[256,768]{1,0:T(8,128)(2,1)}, bf16[256,768]{1,0:T(8,128)(2,1)S(1)}, u32[]{:S(2)}, u32[]{:S(2)}) collective-permute-start(bf16[256,768]{1,0:T(8,128)(2,1)} %refs_12_.1), channel_id=1, source_target_pairs={{0,8},{1,9},{2,10},{3,11},{4,12},{5,13},{6,14},{7,15},{8,0},{9,1},... | collective-permute-start | bytes 1179656 | tf_op jit(solution)/shard_map/ppermute | solution.py:83
  5.2 13.3 %collective-permute-start = (bf16[128,768]{1,0:T(8,128)(2,1)}, bf16[128,768]{1,0:T(8,128)(2,1)S(1)}, u32[]{:S(2)}, u32[]{:S(2)}) collective-permute-start(bf16[128,768]{1,0:T(8,128)(2,1)} %refs_0_.5), channel_id=1, source_target_pairs={{0,6},{1,7},{2,12},{3,13},{4,18},{5,19},{6,24},{7,25},{8,4},{9,5},... | collective-permute-start | bytes 589832 | tf_op jit(solution)/shard_map/ppermute | solution.py:89
  10.7 7.8 %collective-permute-start.1 = (bf16[128,768]{1,0:T(8,128)(2,1)}, bf16[128,768]{1,0:T(8,128)(2,1)S(1)}, u32[]{:S(2)}, u32[]{:S(2)}) collective-permute-start(bf16[128,768]{1,0:T(8,128)(2,1)} %refs_0_.5), channel_id=1, source_target_pairs={{0,0},{1,1},{2,10},{3,11},{4,20},{5,21},{6,30},{7,31},{8,2},{9,3},... | collective-permute-start | bytes 589832 | tf_op jit(solution)/shard_map/ppermute | solution.py:89
  18.5 8.4 %collective-permute-start.2 = (bf16[128,768]{1,0:T(8,128)(2,1)S(1)}, bf16[128,768]{1,0:T(8,128)(2,1)S(1)}, u32[]{:S(2)}, u32[]{:S(2)}) collective-permute-start(bf16[128,768]{1,0:T(8,128)(2,1)S(1)} %collective-permute-done.refs_3_), channel_id=1, source_target_pairs={{0,2},{1,3},{2,0},{3,1},{4,6},{5,7},{6,4},{7,5},{8,10},{9,11},{10,... | collective-permute-start | bytes 589832 | tf_op jit(solution)/shard_map/ppermute | solution.py:86
  18.5 10.0 %collective-permute-start.3 = (bf16[128,768]{1,0:T(8,128)(2,1)S(1)}, bf16[128,768]{1,0:T(8,128)(2,1)S(1)}, u32[]{:S(2)}, u32[]{:S(2)}) collective-permute-start(bf16[128,768]{1,0:T(8,128)(2,1)S(1)} %collective-permute-done.1.refs_0_), channel_id=1, source_target_pairs={{0,2},{1,3},{2,0},{3,1},{4,6},{5,7},{6,4},{7,5},{8,10},{9,11},{10,... | collective-permute-start | bytes 589832 | tf_op jit(solution)/shard_map/ppermute | solution.py:86
  21.1 7.3 %collective-permute-start.6 = (bf16[128,768]{1,0:T(8,128)(2,1)S(1)}, bf16[128,768]{1,0:T(8,128)(2,1)S(1)}, u32[]{:S(2)}, u32[]{:S(2)}) collective-permute-start(bf16[128,768]{1,0:T(8,128)(2,1)S(1)} %slice.8), channel_id=1, source_target_pairs={{0,8},{1,9},{2,10},{3,11},{4,12},{5,13},{6,14},{7,15},{8,0},{9,1},... | collective-permute-start | bytes 589832 | tf_op jit(solution)/shard_map/ppermute | solution.py:83
  24.3 6.8 %copy-start.3 = (f32[768]{0:T(1024)S(1)}, f32[768]{0:T(1024)}, u32[]{:S(2)}) copy-start(f32[768]{0:T(1024)} %param.20) | copy-start | bytes 9220
  24.3 5.7 %collective-permute-start.7 = (bf16[128,768]{1,0:T(8,128)(2,1)S(1)}, bf16[128,768]{1,0:T(8,128)(2,1)S(1)}, u32[]{:S(2)}, u32[]{:S(2)}) collective-permute-start(bf16[128,768]{1,0:T(8,128)(2,1)S(1)} %slice.9), channel_id=1, source_target_pairs={{0,16},{1,17},{2,18},{3,19},{4,20},{5,21},{6,22},{7,23},{8,24},{9,... | collective-permute-start | bytes 589832 | tf_op jit(solution)/shard_map/ppermute | solution.py:83
  30.0 1.4 %collective-permute-start.8 = (bf16[128,768]{1,0:T(8,128)(2,1)S(1)}, bf16[128,768]{1,0:T(8,128)(2,1)S(1)}, u32[]{:S(2)}, u32[]{:S(2)}) collective-permute-start(bf16[128,768]{1,0:T(8,128)(2,1)S(1)} %collective-permute-done.1.refs_0_), channel_id=1, source_target_pairs={{0,1},{1,0},{2,3},{3,2},{4,5},{5,4},{6,7},{7,6},{8,9},{9,8},{10,11... | collective-permute-start | bytes 589832 | tf_op jit(solution)/shard_map/ppermute | solution.py:80
  30.0 1.7 %collective-permute-start.9 = (bf16[128,768]{1,0:T(8,128)(2,1)S(1)}, bf16[128,768]{1,0:T(8,128)(2,1)S(1)}, u32[]{:S(2)}, u32[]{:S(2)}) collective-permute-start(bf16[128,768]{1,0:T(8,128)(2,1)S(1)} %collective-permute-done.3.refs_1_), channel_id=1, source_target_pairs={{0,1},{1,0},{2,3},{3,2},{4,5},{5,4},{6,7},{7,6},{8,9},{9,8},{10,11... | collective-permute-start | bytes 589832 | tf_op jit(solution)/shard_map/ppermute | solution.py:80
  30.5 1.5 %collective-permute-start.10 = (bf16[128,768]{1,0:T(8,128)(2,1)S(1)}, bf16[128,768]{1,0:T(8,128)(2,1)S(1)}, u32[]{:S(2)}, u32[]{:S(2)}) collective-permute-start(bf16[128,768]{1,0:T(8,128)(2,1)S(1)} %collective-permute-done.2.refs_2_), channel_id=1, source_target_pairs={{0,1},{1,0},{2,3},{3,2},{4,5},{5,4},{6,7},{7,6},{8,9},{9,8},{10,11... | collective-permute-start | bytes 589832 | tf_op jit(solution)/shard_map/ppermute | solution.py:80
  30.5 1.8 %collective-permute-start.11 = (bf16[128,768]{1,0:T(8,128)(2,1)S(1)}, bf16[128,768]{1,0:T(8,128)(2,1)S(1)}, u32[]{:S(2)}, u32[]{:S(2)}) collective-permute-start(bf16[128,768]{1,0:T(8,128)(2,1)S(1)} %collective-permute-done.refs_3_), channel_id=1, source_target_pairs={{0,1},{1,0},{2,3},{3,2},{4,5},{5,4},{6,7},{7,6},{8,9},{9,8},{10,11... | collective-permute-start | bytes 589832 | tf_op jit(solution)/shard_map/ppermute | solution.py:80
  31.1 5.8 %copy-start = (bf16[256,768]{1,0:T(8,128)(2,1)S(1)}, bf16[256,768]{1,0:T(8,128)(2,1)}, u32[]{:S(2)}) copy-start(bf16[256,768]{1,0:T(8,128)(2,1)} %refs_12_.1) | copy-start | bytes 1179652
  31.1 5.8 %copy-start.2 = (bf16[128,768]{1,0:T(8,128)(2,1)S(1)}, bf16[128,768]{1,0:T(8,128)(2,1)}, u32[]{:S(2)}) copy-start(bf16[128,768]{1,0:T(8,128)(2,1)} %refs_0_.4) | copy-start | bytes 589828
  33.3 14.8 %collective-permute-start.12 = (bf16[768,128]{1,0:T(8,128)(2,1)S(1)}, bf16[768,128]{1,0:T(8,128)(2,1)S(1)}, u32[]{:S(2)}, u32[]{:S(2)}) collective-permute-start(bf16[768,128]{1,0:T(8,128)(2,1)S(1)} %get-tuple-element.53), channel_id=1, source_target_pairs={{0,8},{1,9},{2,10},{3,11},{4,12},{5,13},{6,14},{7,15},{8,0},{9,1},... | collective-permute-start | bytes 589832 | tf_op jit(solution)/shard_map/ppermute | solution.py:83
  34.8 13.3 %collective-permute-start.13 = (bf16[768,128]{1,0:T(8,128)(2,1)S(1)}, bf16[768,128]{1,0:T(8,128)(2,1)S(1)}, u32[]{:S(2)}, u32[]{:S(2)}) collective-permute-start(bf16[768,128]{1,0:T(8,128)(2,1)S(1)} %get-tuple-element.54), channel_id=1, source_target_pairs={{0,16},{1,17},{2,18},{3,19},{4,20},{5,21},{6,22},{7,23},{8,24},{9,... | collective-permute-start | bytes 589832 | tf_op jit(solution)/shard_map/ppermute | solution.py:83
  35.2 12.9 %collective-permute-start.14 = (bf16[768,128]{1,0:T(8,128)(2,1)S(1)}, bf16[768,128]{1,0:T(8,128)(2,1)S(1)}, u32[]{:S(2)}, u32[]{:S(2)}) collective-permute-start(bf16[768,128]{1,0:T(8,128)(2,1)S(1)} %get-tuple-element.55), channel_id=1, source_target_pairs={{0,24},{1,25},{2,26},{3,27},{4,28},{5,29},{6,30},{7,31},{8,16},{9,... | collective-permute-start | bytes 589832 | tf_op jit(solution)/shard_map/ppermute | solution.py:83
  37.6 4.3 %collective-permute-start.15 = (bf16[256,128]{1,0:T(8,128)(2,1)S(1)}, bf16[256,128]{1,0:T(8,128)(2,1)S(1)}, u32[]{:S(2)}, u32[]{:S(2)}) collective-permute-start(bf16[256,128]{1,0:T(8,128)(2,1)S(1)} %get-tuple-element.61), channel_id=1, source_target_pairs={{0,2},{1,3},{2,0},{3,1},{4,6},{5,7},{6,4},{7,5},{8,10},{9,11},{10,... | collective-permute-start | bytes 196616 | tf_op jit(solution)/shard_map/ppermute | solution.py:86
  39.7 7.1 %collective-permute-start.16 = (bf16[256,128]{1,0:T(8,128)(2,1)S(1)}, bf16[256,128]{1,0:T(8,128)(2,1)S(1)}, u32[]{:S(2)}, u32[]{:S(2)}) collective-permute-start(bf16[256,128]{1,0:T(8,128)(2,1)S(1)} %get-tuple-element.62), channel_id=1, source_target_pairs={{0,4},{1,5},{2,6},{3,7},{4,0},{5,1},{6,2},{7,3},{8,12},{9,13},{10,... | collective-permute-start | bytes 196616 | tf_op jit(solution)/shard_map/ppermute | solution.py:86
  42.0 6.2 %collective-permute-start.17 = (bf16[256,128]{1,0:T(8,128)(2,1)S(1)}, bf16[256,128]{1,0:T(8,128)(2,1)S(1)}, u32[]{:S(2)}, u32[]{:S(2)}) collective-permute-start(bf16[256,128]{1,0:T(8,128)(2,1)S(1)} %get-tuple-element.63), channel_id=1, source_target_pairs={{0,6},{1,7},{2,4},{3,5},{4,2},{5,3},{6,0},{7,1},{8,14},{9,15},{10,... | collective-permute-start | bytes 196616 | tf_op jit(solution)/shard_map/ppermute | solution.py:86
  48.1 19.7 %copy-start.1 = (bf16[128,768]{1,0:T(8,128)(2,1)S(1)}, bf16[128,768]{1,0:T(8,128)(2,1)}, u32[]{:S(2)}) copy-start(bf16[128,768]{1,0:T(8,128)(2,1)} %refs_0_.5) | copy-start | bytes 589828
  49.9 4.0 %collective-permute-start.19 = (bf16[144,128]{1,0:T(8,128)(2,1)S(1)}, bf16[144,128]{1,0:T(8,128)(2,1)S(1)}, u32[]{:S(2)}, u32[]{:S(2)}) collective-permute-start(bf16[144,128]{1,0:T(8,128)(2,1)S(1)} %get-tuple-element.78), channel_id=1, source_target_pairs={{0,8},{1,9},{2,10},{3,11},{4,12},{5,13},{6,14},{7,15},{8,0},{9,1},... | collective-permute-start | bytes 110600 | tf_op jit(solution)/shard_map/ppermute | solution.py:83
  52.0 4.0 %collective-permute-start.20 = (bf16[144,128]{1,0:T(8,128)(2,1)S(1)}, bf16[144,128]{1,0:T(8,128)(2,1)S(1)}, u32[]{:S(2)}, u32[]{:S(2)}) collective-permute-start(bf16[144,128]{1,0:T(8,128)(2,1)S(1)} %get-tuple-element.79), channel_id=1, source_target_pairs={{0,16},{1,17},{2,18},{3,19},{4,20},{5,21},{6,22},{7,23},{8,24},{9,... | collective-permute-start | bytes 110600 | tf_op jit(solution)/shard_map/ppermute | solution.py:83
  52.4 4.9 %collective-permute-start.21 = (bf16[144,128]{1,0:T(8,128)(2,1)S(1)}, bf16[144,128]{1,0:T(8,128)(2,1)S(1)}, u32[]{:S(2)}, u32[]{:S(2)}) collective-permute-start(bf16[144,128]{1,0:T(8,128)(2,1)S(1)} %get-tuple-element.80), channel_id=1, source_target_pairs={{0,24},{1,25},{2,26},{3,27},{4,28},{5,29},{6,30},{7,31},{8,16},{9,... | collective-permute-start | bytes 110600 | tf_op jit(solution)/shard_map/ppermute | solution.py:83
  57.4 4.0 %collective-permute-start.22 = (bf16[128,128]{1,0:T(8,128)(2,1)S(1)}, bf16[128,128]{1,0:T(8,128)(2,1)S(1)}, u32[]{:S(2)}, u32[]{:S(2)}) collective-permute-start(bf16[128,128]{1,0:T(8,128)(2,1)S(1)} %finish.1.refs_4_), channel_id=1, source_target_pairs={{0,2},{1,3},{2,0},{3,1},{4,6},{5,7},{6,4},{7,5},{8,10},{9,11},{10,... | collective-permute-start | bytes 98312 | tf_op jit(solution)/shard_map/ppermute | solution.py:86
  57.4 5.2 %collective-permute-start.23 = (bf16[128,128]{1,0:T(8,128)(2,1)S(1)}, bf16[128,128]{1,0:T(8,128)(2,1)S(1)}, u32[]{:S(2)}, u32[]{:S(2)}) collective-permute-start(bf16[128,128]{1,0:T(8,128)(2,1)S(1)} %finish.1.refs_4_), channel_id=1, source_target_pairs={{0,4},{1,5},{2,6},{3,7},{4,0},{5,1},{6,2},{7,3},{8,12},{9,13},{10,... | collective-permute-start | bytes 98312 | tf_op jit(solution)/shard_map/ppermute | solution.py:86
  61.3 4.8 %collective-permute-start.24 = (bf16[128,128]{1,0:T(8,128)(2,1)S(1)}, bf16[128,128]{1,0:T(8,128)(2,1)S(1)}, u32[]{:S(2)}, u32[]{:S(2)}) collective-permute-start(bf16[128,128]{1,0:T(8,128)(2,1)S(1)} %collective-permute-done.22.refs_5_), channel_id=1, source_target_pairs={{0,4},{1,5},{2,6},{3,7},{4,0},{5,1},{6,2},{7,3},{8,12},{9,13},{10,... | collective-permute-start | bytes 98312 | tf_op jit(solution)/shard_map/ppermute | solution.py:86
  62.0 4.6 %collective-permute-start.18 = (bf16[128,128]{1,0:T(8,128)(2,1)S(1)}, bf16[128,128]{1,0:T(8,128)(2,1)S(1)}, u32[]{:S(2)}, u32[]{:S(2)}) collective-permute-start(bf16[128,128]{1,0:T(8,128)(2,1)S(1)} %get-tuple-element.69), channel_id=1, source_target_pairs={{0,1},{1,0},{2,3},{3,2},{4,5},{5,4},{6,7},{7,6},{8,9},{9,8},{10,11... | collective-permute-start | bytes 98312 | tf_op jit(solution)/shard_map/ppermute | solution.py:80
  62.1 4.6 %collective-permute-start.25 = (bf16[128,128]{1,0:T(8,128)(2,1)S(1)}, bf16[128,128]{1,0:T(8,128)(2,1)S(1)}, u32[]{:S(2)}, u32[]{:S(2)}) collective-permute-start(bf16[128,128]{1,0:T(8,128)(2,1)S(1)} %finish.1.refs_4_), channel_id=1, source_target_pairs={{0,1},{1,0},{2,3},{3,2},{4,5},{5,4},{6,7},{7,6},{8,9},{9,8},{10,11... | collective-permute-start | bytes 98312 | tf_op jit(solution)/shard_map/ppermute | solution.py:80
  66.2 1.2 %collective-permute-start.26 = (bf16[128,128]{1,0:T(8,128)(2,1)S(1)}, bf16[128,128]{1,0:T(8,128)(2,1)S(1)}, u32[]{:S(2)}, u32[]{:S(2)}) collective-permute-start(bf16[128,128]{1,0:T(8,128)(2,1)S(1)} %collective-permute-done.22.refs_5_), channel_id=1, source_target_pairs={{0,1},{1,0},{2,3},{3,2},{4,5},{5,4},{6,7},{7,6},{8,9},{9,8},{10,11... | collective-permute-start | bytes 98312 | tf_op jit(solution)/shard_map/ppermute | solution.py:80
  66.2 1.4 %collective-permute-start.27 = (bf16[128,128]{1,0:T(8,128)(2,1)S(1)}, bf16[128,128]{1,0:T(8,128)(2,1)S(1)}, u32[]{:S(2)}, u32[]{:S(2)}) collective-permute-start(bf16[128,128]{1,0:T(8,128)(2,1)S(1)} %collective-permute-done.23.refs_6_), channel_id=1, source_target_pairs={{0,1},{1,0},{2,3},{3,2},{4,5},{5,4},{6,7},{7,6},{8,9},{9,8},{10,11... | collective-permute-start | bytes 98312 | tf_op jit(solution)/shard_map/ppermute | solution.py:80
  66.7 1.2 %collective-permute-start.28 = (bf16[128,128]{1,0:T(8,128)(2,1)S(1)}, bf16[128,128]{1,0:T(8,128)(2,1)S(1)}, u32[]{:S(2)}, u32[]{:S(2)}) collective-permute-start(bf16[128,128]{1,0:T(8,128)(2,1)S(1)} %collective-permute-done.24.refs_7_), channel_id=1, source_target_pairs={{0,1},{1,0},{2,3},{3,2},{4,5},{5,4},{6,7},{7,6},{8,9},{9,8},{10,11... | collective-permute-start | bytes 98312 | tf_op jit(solution)/shard_map/ppermute | solution.py:80

commit v3 on v2

--- a/solution.py
+++ b/solution.py
@@ -158,8 +158,11 @@
             f, z, q = here()
             w_mine = weight_ref[pl.ds(pl.multiple_of(q * F, F), F), :]
             w_other = weight_ref[pl.ds(pl.multiple_of((1 - q) * F, F), F), :]
+            whole_mine = jnp.concatenate([ref[...] for ref in mine_refs])
+            whole_other = jnp.concatenate([ref[...] for ref in other_refs])
+            whole = (dot(whole_mine, w_mine) + dot(whole_other, w_other)).astype(bf16)
             for d in range(R):
-                part = (dot(mine_refs[d][...], w_mine) + dot(other_refs[d][...], w_other)).astype(bf16)
+                part = whole[d * T : (d + 1) * T]
                 block = f ^ z ^ d
                 rows = pl.ds(pl.multiple_of(block * T, T), T)
                 for s in range(R):
@@ -211,17 +214,6 @@
             [pltpu.VMEM((R, k * T, H), bf16)],
         )
         grads = [grads[0]] + [over_z(grads[m], m) for m in range(1, R)]
-
-        parts, grads = lax.optimization_barrier((parts, grads))
-
-        def join(*refs):
-            own_ref, away_ref = refs[R:]
-            both_heads = sum(ref[...].astype(f32) for ref in refs[:R])
-            own_ref[...] = both_heads[:T].astype(bf16)
-            away_ref[...] = both_heads[T:].astype(bf16)
-
-        grad_own, grad_away = call(join, "join", grads, [jax.ShapeDtypeStruct((T, H), bf16)] * 2)
-        grad_away = across_chip(grad_away)
 
         def attend(*refs):
             part_refs = refs[:R]
@@ -270,6 +262,17 @@
         )
         sums = [sums[0]] + [over_row(sums[s], s) for s in range(1, R)]
 
+        sums, grads = lax.optimization_barrier((sums, grads))
+
+        def join(*refs):
+            own_ref, away_ref = refs[R:]
+            both_heads = sum(ref[...].astype(f32) for ref in refs[:R])
+            own_ref[...] = both_heads[:T].astype(bf16)
+            away_ref[...] = both_heads[T:].astype(bf16)
+
+        grad_own, grad_away = call(join, "join", grads, [jax.ShapeDtypeStruct((T, H), bf16)] * 2)
+        grad_away = across_chip(grad_away)
+
         def finish(*refs):
             sum_refs, out = refs[:R], refs[R]
             numerators = sum(ref[:T, :].astype(f32) for ref in sum_refs)
@@ -281,11 +284,7 @@
             out[...] = (numerators / totals).astype(bf16)
 
         (attention,) = call(finish, "finish", sums, [jax.ShapeDtypeStruct((T, H), bf16)])
-        heads = {0: attention}
-        for bit in near:
-            heads.update({m | bit: over_z(heads[m], bit) for m in list(heads)})
-        heads = [heads[m] for m in range(R)]
-        heads = [heads[0], *lax.optimization_barrier(heads[1:])]
+        heads = [attention] + [over_z(attention, m) for m in range(1, R)]
         heads_other = [across_chip(x) for x in heads]
 
         def output(*refs):

time: 69.2 us -> 64.6 us (0.934)
  waiting for transfers between devices: 25.5 us -> 20 us
  starting transfers between devices: 35.4 us -> 36.4 us
    ppermute x8, waiting for transfers between devices: 11.6 us -> 3.52 us  [over_z(): return lax.ppermute(x, both, route(lambda r, z, q: (r, z ^ m, q)))]
    ppermute x10, waiting for transfers between devices: 5.3 us -> 8.13 us  [over_row(): return lax.ppermute(x, both, route(lambda r, z, q: (r ^ s, z, q)))]
    ppermute x8, starting transfers between devices: 11.3 us -> 12.4 us  [over_z(): return lax.ppermute(x, both, route(lambda r, z, q: (r, z ^ m, q)))]
  transfers between devices with their start and end apart: 29 -> 29, of which waited for: 18 -> 17; matrix products, arithmetic and copies ran while one was open for 0% -> 0% of each run, Pallas kernels for 5% -> 8%
where the time goes in v3:
time: 64.6 us; the launch traced here: 64.4 us
  starting transfers between devices  36.4 us (56%)
  waiting for transfers between devices  20 us (31%)
  Pallas kernels  7.16 us (11%)
  between operations  0.78 us (1%)
    ppermute x10, starting transfers between devices, over_row(): return lax.ppermute(x, both, route(lambda r, z, q: (r ^ s, z, q)))  14.9 us
    ppermute x8, starting transfers between devices, over_z(): return lax.ppermute(x, both, route(lambda r, z, q: (r, z ^ m, q)))  12.4 us
    ppermute x10, waiting for transfers between devices, over_row(): return lax.ppermute(x, both, route(lambda r, z, q: (r ^ s, z, q)))  8.13 us
    pallas_call x7, Pallas kernels, call(): pl.pallas_call(fetch if far else kernel, out_shape=list(outs), in_specs=[...  7.16 us
    ppermute x2, starting transfers between devices, turned(): return lax.ppermute(x, both, route(lambda r, z, q: (z, r ^ z ^ d, q)))  7.09 us
    ppermute x2, waiting for transfers between devices, turned(): return lax.ppermute(x, both, route(lambda r, z, q: (z, r ^ z ^ d, q)))  6.21 us
    ppermute x8, waiting for transfers between devices, over_z(): return lax.ppermute(x, both, route(lambda r, z, q: (r, z ^ m, q)))  3.52 us
    ppermute x9, starting transfers between devices, across_chip(): return lax.ppermute(x, both, route(lambda r, z, q: (r, z, q ^ 1)))  2.11 us
  transfers between devices with their start and end apart: 29, of which 17 were waited for; matrix products, arithmetic and copies ran while one was open for 0% of the time, Pallas kernels for 8%

profile of v3, /device:TPU:0, one launch (start us, length us, event | category | flops | bytes accessed | tf_op | source)
XLA Modules:
  0.0 64.4 jit_solution(2866569170969966393)
XLA Ops:
  0.6 3.0 %collective-permute-start.5 = (bf16[256,768]{1,0:T(8,128)(2,1)}, bf16[256,768]{1,0:T(8,128)(2,1)S(1)}, u32[]{:S(2)}, u32[]{:S(2)}) collective-permute-start(bf16[256,768]{1,0:T(8,128)(2,1)} %refs_12_.1), channel_id=1, source_target_pairs={{0,16},{1,17},{2,18},{3,19},{4,20},{5,21},{6,22},{7,23},{8,24},{9,... | collective-permute-start | bytes 1179656 | tf_op jit(solution)/shard_map/ppermute | solution.py:83
  3.7 1.5 %collective-permute-start.4 = (bf16[256,768]{1,0:T(8,128)(2,1)}, bf16[256,768]{1,0:T(8,128)(2,1)S(1)}, u32[]{:S(2)}, u32[]{:S(2)}) collective-permute-start(bf16[256,768]{1,0:T(8,128)(2,1)} %refs_12_.1), channel_id=1, source_target_pairs={{0,8},{1,9},{2,10},{3,11},{4,12},{5,13},{6,14},{7,15},{8,0},{9,1},... | collective-permute-start | bytes 1179656 | tf_op jit(solution)/shard_map/ppermute | solution.py:83
  5.2 5.5 %collective-permute-start = (bf16[128,768]{1,0:T(8,128)(2,1)}, bf16[128,768]{1,0:T(8,128)(2,1)S(1)}, u32[]{:S(2)}, u32[]{:S(2)}) collective-permute-start(bf16[128,768]{1,0:T(8,128)(2,1)} %refs_0_.5), channel_id=1, source_target_pairs={{0,6},{1,7},{2,12},{3,13},{4,18},{5,19},{6,24},{7,25},{8,4},{9,5},... | collective-permute-start | bytes 589832 | tf_op jit(solution)/shard_map/ppermute | solution.py:89
  10.7 1.6 %collective-permute-start.1 = (bf16[128,768]{1,0:T(8,128)(2,1)}, bf16[128,768]{1,0:T(8,128)(2,1)S(1)}, u32[]{:S(2)}, u32[]{:S(2)}) collective-permute-start(bf16[128,768]{1,0:T(8,128)(2,1)} %refs_0_.5), channel_id=1, source_target_pairs={{0,0},{1,1},{2,10},{3,11},{4,20},{5,21},{6,30},{7,31},{8,2},{9,3},... | collective-permute-start | bytes 589832 | tf_op jit(solution)/shard_map/ppermute | solution.py:89
  12.2 6.2 %collective-permute-done.refs_3_ = bf16[128,768]{1,0:T(8,128)(2,1)S(1)} collective-permute-done((bf16[128,768]{1,0:T(8,128)(2,1)}, bf16[128,768]{1,0:T(8,128)(2,1)S(1)}, u32[]{:S(2)}, u32[]{:S(2)}) %collective-permute-start) | collective-permute-done | bytes 196640 | tf_op jit(solution)/shard_map/ppermute | solution.py:89
  18.5 2.6 %collective-permute-start.3 = (bf16[128,768]{1,0:T(8,128)(2,1)S(1)}, bf16[128,768]{1,0:T(8,128)(2,1)S(1)}, u32[]{:S(2)}, u32[]{:S(2)}) collective-permute-start(bf16[128,768]{1,0:T(8,128)(2,1)S(1)} %collective-permute-done.1.refs_0_), channel_id=1, source_target_pairs={{0,2},{1,3},{2,0},{3,1},{4,6},{5,7},{6,4},{7,5},{8,10},{9,11},{10,... | collective-permute-start | bytes 589832 | tf_op jit(solution)/shard_map/ppermute | solution.py:86
  21.1 3.2 %collective-permute-start.6 = (bf16[128,768]{1,0:T(8,128)(2,1)S(1)}, bf16[128,768]{1,0:T(8,128)(2,1)S(1)}, u32[]{:S(2)}, u32[]{:S(2)}) collective-permute-start(bf16[128,768]{1,0:T(8,128)(2,1)S(1)} %slice.8), channel_id=1, source_target_pairs={{0,8},{1,9},{2,10},{3,11},{4,12},{5,13},{6,14},{7,15},{8,0},{9,1},... | collective-permute-start | bytes 589832 | tf_op jit(solution)/shard_map/ppermute | solution.py:83
  24.3 0.0 copy-start.3
  24.3 0.1 collective-permute-start.7
  24.4 2.5 %prepare.1 = (bf16[128,2048]{1,0:T(8,128)(2,1)S(1)}, bf16[2048,256]{1,0:T(8,128)(2,1)S(1)}, bf16[1536,384]{1,0:T(8,128)(2,1)S(1)}, f32[2,128]{1,0:T(2,128)S(1)}) custom-call(bf16[2048,128]{1,0:T(8,128)(2,1)} %refs_0_.3, bf16[2048,128]{1,0:T(8,128)(2,1)} %refs_1_.1, bf16[1536,128]{1,0:T(8,128)(2,1)} %refs_2_.2, bf16[1536,128]{1,0:T(8,128)(2,1)} %refs_3_.1, ...), custom_call_target="tpu_custom_call" | custom-call | tf_op jit(solution)/shard_map/prepare/pallas_call | solution.py:37
  26.9 1.6 %collective-permute-done.3.refs_1_ = bf16[128,768]{1,0:T(8,128)(2,1)S(1)} collective-permute-done((bf16[128,768]{1,0:T(8,128)(2,1)S(1)}, bf16[128,768]{1,0:T(8,128)(2,1)S(1)}, u32[]{:S(2)}, u32[]{:S(2)}) %collective-permute-start.3) | collective-permute-done | bytes 196640 | tf_op jit(solution)/shard_map/ppermute | solution.py:86
  28.4 1.6 %collective-permute-done.7 = bf16[128,768]{1,0:T(8,128)(2,1)S(1)} collective-permute-done((bf16[128,768]{1,0:T(8,128)(2,1)S(1)}, bf16[128,768]{1,0:T(8,128)(2,1)S(1)}, u32[]{:S(2)}, u32[]{:S(2)}) %collective-permute-start.7) | collective-permute-done | bytes 196640 | tf_op jit(solution)/shard_map/ppermute | solution.py:83
  30.0 0.5 collective-permute-start.9
  30.5 0.0 collective-permute-start.10
  30.5 0.5 collective-permute-start.11
  31.1 0.0 copy-start.2
  31.1 0.4 collective-permute-done.8.refs_4_
  31.5 0.3 collective-permute-done.9.refs_5_
  31.7 0.3 collective-permute-done.10.refs_6_
  32.0 0.3 collective-permute-done.11.refs_7_
  32.3 1.0 %project.1 = (bf16[768,128]{1,0:T(8,128)(2,1)S(1)}, bf16[768,128]{1,0:T(8,128)(2,1)S(1)}, bf16[768,128]{1,0:T(8,128)(2,1)S(1)}, bf16[768,128]{1,0:T(8,128)(2,1)S(1)}) custom-call(bf16[128,768]{1,0:T(8,128)(2,1)S(1)} %collective-permute-done.1.refs_0_, bf16[128,768]{1,0:T(8,128)(2,1)S(1)} %collective-permute-done.3.refs_1_, ...), custom_call_target="tpu_custom_call" | custom-call | tf_op jit(solution)/shard_map/project/pallas_call | solution.py:37
  33.3 1.5 %collective-permute-start.12 = (bf16[768,128]{1,0:T(8,128)(2,1)S(1)}, bf16[768,128]{1,0:T(8,128)(2,1)S(1)}, u32[]{:S(2)}, u32[]{:S(2)}) collective-permute-start(bf16[768,128]{1,0:T(8,128)(2,1)S(1)} %get-tuple-element.50), channel_id=1, source_target_pairs={{0,8},{1,9},{2,10},{3,11},{4,12},{5,13},{6,14},{7,15},{8,0},{9,1},... | collective-permute-start | bytes 589832 | tf_op jit(solution)/shard_map/ppermute | solution.py:83
  34.8 0.3 collective-permute-start.13
  35.2 1.7 %collective-permute-start.14 = (bf16[768,128]{1,0:T(8,128)(2,1)S(1)}, bf16[768,128]{1,0:T(8,128)(2,1)S(1)}, u32[]{:S(2)}, u32[]{:S(2)}) collective-permute-start(bf16[768,128]{1,0:T(8,128)(2,1)S(1)} %get-tuple-element.52), channel_id=1, source_target_pairs={{0,24},{1,25},{2,26},{3,27},{4,28},{5,29},{6,30},{7,31},{8,16},{9,... | collective-permute-start | bytes 589832 | tf_op jit(solution)/shard_map/ppermute | solution.py:83
  36.9 0.7 %gradient.1 = (bf16[256,128]{1,0:T(8,128)(2,1)S(1)}, bf16[256,128]{1,0:T(8,128)(2,1)S(1)}, bf16[256,128]{1,0:T(8,128)(2,1)S(1)}, bf16[256,128]{1,0:T(8,128)(2,1)S(1)}) custom-call(bf16[128,768]{1,0:T(8,128)(2,1)S(1)} %copy-done.2, f32[1,768]{1,0:T(1,128)S(1)} %reshape.13.refs_1_, bf16[256,768]{1,0:T(8,128)(2,1)S(1)} %copy-done, ...), custom_call_target="tpu_custom_call" | custom-call | tf_op jit(solution)/shard_map/gradient/pallas_call | solution.py:37
  37.6 2.1 %collective-permute-start.18 = (bf16[256,128]{1,0:T(8,128)(2,1)S(1)}, bf16[256,128]{1,0:T(8,128)(2,1)S(1)}, u32[]{:S(2)}, u32[]{:S(2)}) collective-permute-start(bf16[256,128]{1,0:T(8,128)(2,1)S(1)} %get-tuple-element.65), channel_id=1, source_target_pairs={{0,2},{1,3},{2,0},{3,1},{4,6},{5,7},{6,4},{7,5},{8,10},{9,11},{10,... | collective-permute-start | bytes 196616 | tf_op jit(solution)/shard_map/ppermute | solution.py:86
  39.7 0.9 %collective-permute-start.19 = (bf16[256,128]{1,0:T(8,128)(2,1)S(1)}, bf16[256,128]{1,0:T(8,128)(2,1)S(1)}, u32[]{:S(2)}, u32[]{:S(2)}) collective-permute-start(bf16[256,128]{1,0:T(8,128)(2,1)S(1)} %get-tuple-element.66), channel_id=1, source_target_pairs={{0,4},{1,5},{2,6},{3,7},{4,0},{5,1},{6,2},{7,3},{8,12},{9,13},{10,... | collective-permute-start | bytes 196616 | tf_op jit(solution)/shard_map/ppermute | solution.py:86
  40.6 0.5 collective-permute-done.12.refs_1_
  41.1 2.3 %collective-permute-start.20 = (bf16[256,128]{1,0:T(8,128)(2,1)S(1)}, bf16[256,128]{1,0:T(8,128)(2,1)S(1)}, u32[]{:S(2)}, u32[]{:S(2)}) collective-permute-start(bf16[256,128]{1,0:T(8,128)(2,1)S(1)} %get-tuple-element.67), channel_id=1, source_target_pairs={{0,6},{1,7},{2,4},{3,5},{4,2},{5,3},{6,0},{7,1},{8,14},{9,15},{10,... | collective-permute-start | bytes 196616 | tf_op jit(solution)/shard_map/ppermute | solution.py:86
  43.4 0.6 collective-permute-done.13.refs_2_
  44.0 1.8 %collective-permute-done.14.refs_3_ = bf16[768,128]{1,0:T(8,128)(2,1)S(1)} collective-permute-done((bf16[768,128]{1,0:T(8,128)(2,1)S(1)}, bf16[768,128]{1,0:T(8,128)(2,1)S(1)}, u32[]{:S(2)}, u32[]{:S(2)}) %collective-permute-start.14) | collective-permute-done | bytes 196640 | tf_op jit(solution)/shard_map/ppermute | solution.py:83
  45.8 1.7 %attend.1 = (bf16[144,128]{1,0:T(8,128)(2,1)S(1)}, bf16[144,128]{1,0:T(8,128)(2,1)S(1)}, bf16[144,128]{1,0:T(8,128)(2,1)S(1)}, bf16[144,128]{1,0:T(8,128)(2,1)S(1)}) custom-call(bf16[768,128]{1,0:T(8,128)(2,1)S(1)} %get-tuple-element.49.refs_0_, bf16[768,128]{1,0:T(8,128)(2,1)S(1)} %collective-permute-done.12.refs_1_, ...), custom_call_target="tpu_custom_call" | custom-call | tf_op jit(solution)/shard_map/attend/pallas_call | solution.py:37
  47.6 0.6 %collective-permute-start.15 = (bf16[144,128]{1,0:T(8,128)(2,1)S(1)}, bf16[144,128]{1,0:T(8,128)(2,1)S(1)}, u32[]{:S(2)}, u32[]{:S(2)}) collective-permute-start(bf16[144,128]{1,0:T(8,128)(2,1)S(1)} %get-tuple-element.57), channel_id=1, source_target_pairs={{0,8},{1,9},{2,10},{3,11},{4,12},{5,13},{6,14},{7,15},{8,0},{9,1},... | collective-permute-start | bytes 110600 | tf_op jit(solution)/shard_map/ppermute | solution.py:83
  48.2 1.7 %collective-permute-start.16 = (bf16[144,128]{1,0:T(8,128)(2,1)S(1)}, bf16[144,128]{1,0:T(8,128)(2,1)S(1)}, u32[]{:S(2)}, u32[]{:S(2)}) collective-permute-start(bf16[144,128]{1,0:T(8,128)(2,1)S(1)} %get-tuple-element.58), channel_id=1, source_target_pairs={{0,16},{1,17},{2,18},{3,19},{4,20},{5,21},{6,22},{7,23},{8,24},{9,... | collective-permute-start | bytes 110600 | tf_op jit(solution)/shard_map/ppermute | solution.py:83
  49.9 1.2 %collective-permute-start.17 = (bf16[144,128]{1,0:T(8,128)(2,1)S(1)}, bf16[144,128]{1,0:T(8,128)(2,1)S(1)}, u32[]{:S(2)}, u32[]{:S(2)}) collective-permute-start(bf16[144,128]{1,0:T(8,128)(2,1)S(1)} %get-tuple-element.59), channel_id=1, source_target_pairs={{0,24},{1,25},{2,26},{3,27},{4,28},{5,29},{6,30},{7,31},{8,16},{9,... | collective-permute-start | bytes 110600 | tf_op jit(solution)/shard_map/ppermute | solution.py:83
  51.1 0.8 %collective-permute-done.15.refs_1_ = bf16[144,128]{1,0:T(8,128)(2,1)S(1)} collective-permute-done((bf16[144,128]{1,0:T(8,128)(2,1)S(1)}, bf16[144,128]{1,0:T(8,128)(2,1)S(1)}, u32[]{:S(2)}, u32[]{:S(2)}) %collective-permute-start.15) | collective-permute-done | bytes 36896 | tf_op jit(solution)/shard_map/ppermute | solution.py:83
  51.9 0.6 collective-permute-done.16.refs_2_
  52.6 2.2 %collective-permute-done.17.refs_3_ = bf16[144,128]{1,0:T(8,128)(2,1)S(1)} collective-permute-done((bf16[144,128]{1,0:T(8,128)(2,1)S(1)}, bf16[144,128]{1,0:T(8,128)(2,1)S(1)}, u32[]{:S(2)}, u32[]{:S(2)}) %collective-permute-start.17) | collective-permute-done | bytes 36896 | tf_op jit(solution)/shard_map/ppermute | solution.py:83
  54.8 0.1 finish.1.refs_4_
  54.9 2.2 %collective-permute-start.24 = (bf16[128,128]{1,0:T(8,128)(2,1)S(1)}, bf16[128,128]{1,0:T(8,128)(2,1)S(1)}, u32[]{:S(2)}, u32[]{:S(2)}) collective-permute-start(bf16[128,128]{1,0:T(8,128)(2,1)S(1)} %finish.1.refs_4_), channel_id=1, source_target_pairs={{0,6},{1,7},{2,4},{3,5},{4,2},{5,3},{6,0},{7,1},{8,14},{9,15},{10,... | collective-permute-start | bytes 98312 | tf_op jit(solution)/shard_map/ppermute | solution.py:86
  57.1 2.3 %collective-permute-start.22 = (bf16[128,128]{1,0:T(8,128)(2,1)S(1)}, bf16[128,128]{1,0:T(8,128)(2,1)S(1)}, u32[]{:S(2)}, u32[]{:S(2)}) collective-permute-start(bf16[128,128]{1,0:T(8,128)(2,1)S(1)} %finish.1.refs_4_), channel_id=1, source_target_pairs={{0,2},{1,3},{2,0},{3,1},{4,6},{5,7},{6,4},{7,5},{8,10},{9,11},{10,... | collective-permute-start | bytes 98312 | tf_op jit(solution)/shard_map/ppermute | solution.py:86
  59.4 0.6 collective-permute-start.21
  60.0 0.7 %collective-permute-done.24.refs_7_ = bf16[128,128]{1,0:T(8,128)(2,1)S(1)} collective-permute-done((bf16[128,128]{1,0:T(8,128)(2,1)S(1)}, bf16[128,128]{1,0:T(8,128)(2,1)S(1)}, u32[]{:S(2)}, u32[]{:S(2)}) %collective-permute-start.24) | collective-permute-done | bytes 32800 | tf_op jit(solution)/shard_map/ppermute | solution.py:86
  60.7 1.2 %collective-permute-done.23.refs_6_ = bf16[128,128]{1,0:T(8,128)(2,1)S(1)} collective-permute-done((bf16[128,128]{1,0:T(8,128)(2,1)S(1)}, bf16[128,128]{1,0:T(8,128)(2,1)S(1)}, u32[]{:S(2)}, u32[]{:S(2)}) %collective-permute-start.23) | collective-permute-done | bytes 32800 | tf_op jit(solution)/shard_map/ppermute | solution.py:86
  61.9 0.5 collective-permute-start.26
  62.4 0.7 %collective-permute-done.27.refs_10_ = bf16[128,128]{1,0:T(8,128)(2,1)S(1)} collective-permute-done((bf16[128,128]{1,0:T(8,128)(2,1)S(1)}, bf16[128,128]{1,0:T(8,128)(2,1)S(1)}, u32[]{:S(2)}, u32[]{:S(2)}) %collective-permute-start.27) | collective-permute-done | bytes 32800 | tf_op jit(solution)/shard_map/ppermute | solution.py:80
  63.1 0.2 collective-permute-done.26.refs_9_
  63.3 1.1 %output.1 = (bf16[128,768]{1,0:T(8,128)(2,1)}, bf16[128,128]{1,0:T(8,128)(2,1)}) custom-call(bf16[128,768]{1,0:T(8,128)(2,1)S(1)} %copy-done.1, f32[1,768]{1,0:T(1,128)S(1)} %reshape.13.refs_1_, bf16[128,128]{1,0:T(8,128)(2,1)S(1)} %get-tuple-element.72.refs_2_, bf16[128,128]{1,0:T(8,128)(2,1)S(1)} %collective-permute-done.21.refs_3_, ...), custom_call_target="tpu_custom_call" | custom-call | tf_op jit(solution)/shard_map/output/pallas_call | solution.py:37
  (30 shorter events, 0.2 us)
Async XLA Ops:
  0.6 20.5 %collective-permute-start.5 = (bf16[256,768]{1,0:T(8,128)(2,1)}, bf16[256,768]{1,0:T(8,128)(2,1)S(1)}, u32[]{:S(2)}, u32[]{:S(2)}) collective-permute-start(bf16[256,768]{1,0:T(8,128)(2,1)} %refs_12_.1), channel_id=1, source_target_pairs={{0,16},{1,17},{2,18},{3,19},{4,20},{5,21},{6,22},{7,23},{8,24},{9,... | collective-permute-start | bytes 1179656 | tf_op jit(solution)/shard_map/ppermute | solution.py:83
  3.7 20.6 %collective-permute-start.4 = (bf16[256,768]{1,0:T(8,128)(2,1)}, bf16[256,768]{1,0:T(8,128)(2,1)S(1)}, u32[]{:S(2)}, u32[]{:S(2)}) collective-permute-start(bf16[256,768]{1,0:T(8,128)(2,1)} %refs_12_.1), channel_id=1, source_target_pairs={{0,8},{1,9},{2,10},{3,11},{4,12},{5,13},{6,14},{7,15},{8,0},{9,1},... | collective-permute-start | bytes 1179656 | tf_op jit(solution)/shard_map/ppermute | solution.py:83
  5.2 13.3 %collective-permute-start = (bf16[128,768]{1,0:T(8,128)(2,1)}, bf16[128,768]{1,0:T(8,128)(2,1)S(1)}, u32[]{:S(2)}, u32[]{:S(2)}) collective-permute-start(bf16[128,768]{1,0:T(8,128)(2,1)} %refs_0_.5), channel_id=1, source_target_pairs={{0,6},{1,7},{2,12},{3,13},{4,18},{5,19},{6,24},{7,25},{8,4},{9,5},... | collective-permute-start | bytes 589832 | tf_op jit(solution)/shard_map/ppermute | solution.py:89
  10.7 7.8 %collective-permute-start.1 = (bf16[128,768]{1,0:T(8,128)(2,1)}, bf16[128,768]{1,0:T(8,128)(2,1)S(1)}, u32[]{:S(2)}, u32[]{:S(2)}) collective-permute-start(bf16[128,768]{1,0:T(8,128)(2,1)} %refs_0_.5), channel_id=1, source_target_pairs={{0,0},{1,1},{2,10},{3,11},{4,20},{5,21},{6,30},{7,31},{8,2},{9,3},... | collective-permute-start | bytes 589832 | tf_op jit(solution)/shard_map/ppermute | solution.py:89
  18.5 8.4 %collective-permute-start.2 = (bf16[128,768]{1,0:T(8,128)(2,1)S(1)}, bf16[128,768]{1,0:T(8,128)(2,1)S(1)}, u32[]{:S(2)}, u32[]{:S(2)}) collective-permute-start(bf16[128,768]{1,0:T(8,128)(2,1)S(1)} %collective-permute-done.refs_3_), channel_id=1, source_target_pairs={{0,2},{1,3},{2,0},{3,1},{4,6},{5,7},{6,4},{7,5},{8,10},{9,11},{10,... | collective-permute-start | bytes 589832 | tf_op jit(solution)/shard_map/ppermute | solution.py:86
  18.5 10.0 %collective-permute-start.3 = (bf16[128,768]{1,0:T(8,128)(2,1)S(1)}, bf16[128,768]{1,0:T(8,128)(2,1)S(1)}, u32[]{:S(2)}, u32[]{:S(2)}) collective-permute-start(bf16[128,768]{1,0:T(8,128)(2,1)S(1)} %collective-permute-done.1.refs_0_), channel_id=1, source_target_pairs={{0,2},{1,3},{2,0},{3,1},{4,6},{5,7},{6,4},{7,5},{8,10},{9,11},{10,... | collective-permute-start | bytes 589832 | tf_op jit(solution)/shard_map/ppermute | solution.py:86
  21.1 7.3 %collective-permute-start.6 = (bf16[128,768]{1,0:T(8,128)(2,1)S(1)}, bf16[128,768]{1,0:T(8,128)(2,1)S(1)}, u32[]{:S(2)}, u32[]{:S(2)}) collective-permute-start(bf16[128,768]{1,0:T(8,128)(2,1)S(1)} %slice.8), channel_id=1, source_target_pairs={{0,8},{1,9},{2,10},{3,11},{4,12},{5,13},{6,14},{7,15},{8,0},{9,1},... | collective-permute-start | bytes 589832 | tf_op jit(solution)/shard_map/ppermute | solution.py:83
  24.3 6.8 %copy-start.3 = (f32[768]{0:T(1024)S(1)}, f32[768]{0:T(1024)}, u32[]{:S(2)}) copy-start(f32[768]{0:T(1024)} %param.20) | copy-start | bytes 9220
  24.3 5.7 %collective-permute-start.7 = (bf16[128,768]{1,0:T(8,128)(2,1)S(1)}, bf16[128,768]{1,0:T(8,128)(2,1)S(1)}, u32[]{:S(2)}, u32[]{:S(2)}) collective-permute-start(bf16[128,768]{1,0:T(8,128)(2,1)S(1)} %slice.9), channel_id=1, source_target_pairs={{0,16},{1,17},{2,18},{3,19},{4,20},{5,21},{6,22},{7,23},{8,24},{9,... | collective-permute-start | bytes 589832 | tf_op jit(solution)/shard_map/ppermute | solution.py:83
  30.0 1.4 %collective-permute-start.8 = (bf16[128,768]{1,0:T(8,128)(2,1)S(1)}, bf16[128,768]{1,0:T(8,128)(2,1)S(1)}, u32[]{:S(2)}, u32[]{:S(2)}) collective-permute-start(bf16[128,768]{1,0:T(8,128)(2,1)S(1)} %collective-permute-done.1.refs_0_), channel_id=1, source_target_pairs={{0,1},{1,0},{2,3},{3,2},{4,5},{5,4},{6,7},{7,6},{8,9},{9,8},{10,11... | collective-permute-start | bytes 589832 | tf_op jit(solution)/shard_map/ppermute | solution.py:80
  30.0 1.7 %collective-permute-start.9 = (bf16[128,768]{1,0:T(8,128)(2,1)S(1)}, bf16[128,768]{1,0:T(8,128)(2,1)S(1)}, u32[]{:S(2)}, u32[]{:S(2)}) collective-permute-start(bf16[128,768]{1,0:T(8,128)(2,1)S(1)} %collective-permute-done.3.refs_1_), channel_id=1, source_target_pairs={{0,1},{1,0},{2,3},{3,2},{4,5},{5,4},{6,7},{7,6},{8,9},{9,8},{10,11... | collective-permute-start | bytes 589832 | tf_op jit(solution)/shard_map/ppermute | solution.py:80
  30.5 1.5 %collective-permute-start.10 = (bf16[128,768]{1,0:T(8,128)(2,1)S(1)}, bf16[128,768]{1,0:T(8,128)(2,1)S(1)}, u32[]{:S(2)}, u32[]{:S(2)}) collective-permute-start(bf16[128,768]{1,0:T(8,128)(2,1)S(1)} %collective-permute-done.2.refs_2_), channel_id=1, source_target_pairs={{0,1},{1,0},{2,3},{3,2},{4,5},{5,4},{6,7},{7,6},{8,9},{9,8},{10,11... | collective-permute-start | bytes 589832 | tf_op jit(solution)/shard_map/ppermute | solution.py:80
  30.5 1.8 %collective-permute-start.11 = (bf16[128,768]{1,0:T(8,128)(2,1)S(1)}, bf16[128,768]{1,0:T(8,128)(2,1)S(1)}, u32[]{:S(2)}, u32[]{:S(2)}) collective-permute-start(bf16[128,768]{1,0:T(8,128)(2,1)S(1)} %collective-permute-done.refs_3_), channel_id=1, source_target_pairs={{0,1},{1,0},{2,3},{3,2},{4,5},{5,4},{6,7},{7,6},{8,9},{9,8},{10,11... | collective-permute-start | bytes 589832 | tf_op jit(solution)/shard_map/ppermute | solution.py:80
  31.0 5.9 %copy-start = (bf16[256,768]{1,0:T(8,128)(2,1)S(1)}, bf16[256,768]{1,0:T(8,128)(2,1)}, u32[]{:S(2)}) copy-start(bf16[256,768]{1,0:T(8,128)(2,1)} %refs_12_.1) | copy-start | bytes 1179652
  31.1 5.9 %copy-start.2 = (bf16[128,768]{1,0:T(8,128)(2,1)S(1)}, bf16[128,768]{1,0:T(8,128)(2,1)}, u32[]{:S(2)}) copy-start(bf16[128,768]{1,0:T(8,128)(2,1)} %refs_0_.4) | copy-start | bytes 589828
  33.3 7.8 %collective-permute-start.12 = (bf16[768,128]{1,0:T(8,128)(2,1)S(1)}, bf16[768,128]{1,0:T(8,128)(2,1)S(1)}, u32[]{:S(2)}, u32[]{:S(2)}) collective-permute-start(bf16[768,128]{1,0:T(8,128)(2,1)S(1)} %get-tuple-element.50), channel_id=1, source_target_pairs={{0,8},{1,9},{2,10},{3,11},{4,12},{5,13},{6,14},{7,15},{8,0},{9,1},... | collective-permute-start | bytes 589832 | tf_op jit(solution)/shard_map/ppermute | solution.py:83
  34.8 9.1 %collective-permute-start.13 = (bf16[768,128]{1,0:T(8,128)(2,1)S(1)}, bf16[768,128]{1,0:T(8,128)(2,1)S(1)}, u32[]{:S(2)}, u32[]{:S(2)}) collective-permute-start(bf16[768,128]{1,0:T(8,128)(2,1)S(1)} %get-tuple-element.51), channel_id=1, source_target_pairs={{0,16},{1,17},{2,18},{3,19},{4,20},{5,21},{6,22},{7,23},{8,24},{9,... | collective-permute-start | bytes 589832 | tf_op jit(solution)/shard_map/ppermute | solution.py:83
  35.2 10.6 %collective-permute-start.14 = (bf16[768,128]{1,0:T(8,128)(2,1)S(1)}, bf16[768,128]{1,0:T(8,128)(2,1)S(1)}, u32[]{:S(2)}, u32[]{:S(2)}) collective-permute-start(bf16[768,128]{1,0:T(8,128)(2,1)S(1)} %get-tuple-element.52), channel_id=1, source_target_pairs={{0,24},{1,25},{2,26},{3,27},{4,28},{5,29},{6,30},{7,31},{8,16},{9,... | collective-permute-start | bytes 589832 | tf_op jit(solution)/shard_map/ppermute | solution.py:83
  37.6 12.3 %collective-permute-start.18 = (bf16[256,128]{1,0:T(8,128)(2,1)S(1)}, bf16[256,128]{1,0:T(8,128)(2,1)S(1)}, u32[]{:S(2)}, u32[]{:S(2)}) collective-permute-start(bf16[256,128]{1,0:T(8,128)(2,1)S(1)} %get-tuple-element.65), channel_id=1, source_target_pairs={{0,2},{1,3},{2,0},{3,1},{4,6},{5,7},{6,4},{7,5},{8,10},{9,11},{10,... | collective-permute-start | bytes 196616 | tf_op jit(solution)/shard_map/ppermute | solution.py:86
  39.7 11.4 %collective-permute-start.19 = (bf16[256,128]{1,0:T(8,128)(2,1)S(1)}, bf16[256,128]{1,0:T(8,128)(2,1)S(1)}, u32[]{:S(2)}, u32[]{:S(2)}) collective-permute-start(bf16[256,128]{1,0:T(8,128)(2,1)S(1)} %get-tuple-element.66), channel_id=1, source_target_pairs={{0,4},{1,5},{2,6},{3,7},{4,0},{5,1},{6,2},{7,3},{8,12},{9,13},{10,... | collective-permute-start | bytes 196616 | tf_op jit(solution)/shard_map/ppermute | solution.py:86
  41.1 10.0 %collective-permute-start.20 = (bf16[256,128]{1,0:T(8,128)(2,1)S(1)}, bf16[256,128]{1,0:T(8,128)(2,1)S(1)}, u32[]{:S(2)}, u32[]{:S(2)}) collective-permute-start(bf16[256,128]{1,0:T(8,128)(2,1)S(1)} %get-tuple-element.67), channel_id=1, source_target_pairs={{0,6},{1,7},{2,4},{3,5},{4,2},{5,3},{6,0},{7,1},{8,14},{9,15},{10,... | collective-permute-start | bytes 196616 | tf_op jit(solution)/shard_map/ppermute | solution.py:86
  45.8 17.5 %copy-start.1 = (bf16[128,768]{1,0:T(8,128)(2,1)S(1)}, bf16[128,768]{1,0:T(8,128)(2,1)}, u32[]{:S(2)}) copy-start(bf16[128,768]{1,0:T(8,128)(2,1)} %refs_0_.5) | copy-start | bytes 589828
  47.6 4.4 %collective-permute-start.15 = (bf16[144,128]{1,0:T(8,128)(2,1)S(1)}, bf16[144,128]{1,0:T(8,128)(2,1)S(1)}, u32[]{:S(2)}, u32[]{:S(2)}) collective-permute-start(bf16[144,128]{1,0:T(8,128)(2,1)S(1)} %get-tuple-element.57), channel_id=1, source_target_pairs={{0,8},{1,9},{2,10},{3,11},{4,12},{5,13},{6,14},{7,15},{8,0},{9,1},... | collective-permute-start | bytes 110600 | tf_op jit(solution)/shard_map/ppermute | solution.py:83
  48.2 4.4 %collective-permute-start.16 = (bf16[144,128]{1,0:T(8,128)(2,1)S(1)}, bf16[144,128]{1,0:T(8,128)(2,1)S(1)}, u32[]{:S(2)}, u32[]{:S(2)}) collective-permute-start(bf16[144,128]{1,0:T(8,128)(2,1)S(1)} %get-tuple-element.58), channel_id=1, source_target_pairs={{0,16},{1,17},{2,18},{3,19},{4,20},{5,21},{6,22},{7,23},{8,24},{9,... | collective-permute-start | bytes 110600 | tf_op jit(solution)/shard_map/ppermute | solution.py:83
  49.9 4.9 %collective-permute-start.17 = (bf16[144,128]{1,0:T(8,128)(2,1)S(1)}, bf16[144,128]{1,0:T(8,128)(2,1)S(1)}, u32[]{:S(2)}, u32[]{:S(2)}) collective-permute-start(bf16[144,128]{1,0:T(8,128)(2,1)S(1)} %get-tuple-element.59), channel_id=1, source_target_pairs={{0,24},{1,25},{2,26},{3,27},{4,28},{5,29},{6,30},{7,31},{8,16},{9,... | collective-permute-start | bytes 110600 | tf_op jit(solution)/shard_map/ppermute | solution.py:83
  54.9 5.8 %collective-permute-start.24 = (bf16[128,128]{1,0:T(8,128)(2,1)S(1)}, bf16[128,128]{1,0:T(8,128)(2,1)S(1)}, u32[]{:S(2)}, u32[]{:S(2)}) collective-permute-start(bf16[128,128]{1,0:T(8,128)(2,1)S(1)} %finish.1.refs_4_), channel_id=1, source_target_pairs={{0,6},{1,7},{2,4},{3,5},{4,2},{5,3},{6,0},{7,1},{8,14},{9,15},{10,... | collective-permute-start | bytes 98312 | tf_op jit(solution)/shard_map/ppermute | solution.py:86
  57.1 4.8 %collective-permute-start.23 = (bf16[128,128]{1,0:T(8,128)(2,1)S(1)}, bf16[128,128]{1,0:T(8,128)(2,1)S(1)}, u32[]{:S(2)}, u32[]{:S(2)}) collective-permute-start(bf16[128,128]{1,0:T(8,128)(2,1)S(1)} %finish.1.refs_4_), channel_id=1, source_target_pairs={{0,4},{1,5},{2,6},{3,7},{4,0},{5,1},{6,2},{7,3},{8,12},{9,13},{10,... | collective-permute-start | bytes 98312 | tf_op jit(solution)/shard_map/ppermute | solution.py:86
  57.1 4.8 %collective-permute-start.22 = (bf16[128,128]{1,0:T(8,128)(2,1)S(1)}, bf16[128,128]{1,0:T(8,128)(2,1)S(1)}, u32[]{:S(2)}, u32[]{:S(2)}) collective-permute-start(bf16[128,128]{1,0:T(8,128)(2,1)S(1)} %finish.1.refs_4_), channel_id=1, source_target_pairs={{0,2},{1,3},{2,0},{3,1},{4,6},{5,7},{6,4},{7,5},{8,10},{9,11},{10,... | collective-permute-start | bytes 98312 | tf_op jit(solution)/shard_map/ppermute | solution.py:86
  59.4 3.1 %collective-permute-start.25 = (bf16[128,128]{1,0:T(8,128)(2,1)S(1)}, bf16[128,128]{1,0:T(8,128)(2,1)S(1)}, u32[]{:S(2)}, u32[]{:S(2)}) collective-permute-start(bf16[128,128]{1,0:T(8,128)(2,1)S(1)} %finish.1.refs_4_), channel_id=1, source_target_pairs={{0,1},{1,0},{2,3},{3,2},{4,5},{5,4},{6,7},{7,6},{8,9},{9,8},{10,11... | collective-permute-start | bytes 98312 | tf_op jit(solution)/shard_map/ppermute | solution.py:80
  59.4 3.0 %collective-permute-start.21 = (bf16[128,128]{1,0:T(8,128)(2,1)S(1)}, bf16[128,128]{1,0:T(8,128)(2,1)S(1)}, u32[]{:S(2)}, u32[]{:S(2)}) collective-permute-start(bf16[128,128]{1,0:T(8,128)(2,1)S(1)} %get-tuple-element.73), channel_id=1, source_target_pairs={{0,1},{1,0},{2,3},{3,2},{4,5},{5,4},{6,7},{7,6},{8,9},{9,8},{10,11... | collective-permute-start | bytes 98312 | tf_op jit(solution)/shard_map/ppermute | solution.py:80
  60.7 1.7 %collective-permute-start.28 = (bf16[128,128]{1,0:T(8,128)(2,1)S(1)}, bf16[128,128]{1,0:T(8,128)(2,1)S(1)}, u32[]{:S(2)}, u32[]{:S(2)}) collective-permute-start(bf16[128,128]{1,0:T(8,128)(2,1)S(1)} %collective-permute-done.24.refs_7_), channel_id=1, source_target_pairs={{0,1},{1,0},{2,3},{3,2},{4,5},{5,4},{6,7},{7,6},{8,9},{9,8},{10,11... | collective-permute-start | bytes 98312 | tf_op jit(solution)/shard_map/ppermute | solution.py:80
  61.9 1.2 %collective-permute-start.27 = (bf16[128,128]{1,0:T(8,128)(2,1)S(1)}, bf16[128,128]{1,0:T(8,128)(2,1)S(1)}, u32[]{:S(2)}, u32[]{:S(2)}) collective-permute-start(bf16[128,128]{1,0:T(8,128)(2,1)S(1)} %collective-permute-done.23.refs_6_), channel_id=1, source_target_pairs={{0,1},{1,0},{2,3},{3,2},{4,5},{5,4},{6,7},{7,6},{8,9},{9,8},{10,11... | collective-permute-start | bytes 98312 | tf_op jit(solution)/shard_map/ppermute | solution.py:80
  61.9 1.4 %collective-permute-start.26 = (bf16[128,128]{1,0:T(8,128)(2,1)S(1)}, bf16[128,128]{1,0:T(8,128)(2,1)S(1)}, u32[]{:S(2)}, u32[]{:S(2)}) collective-permute-start(bf16[128,128]{1,0:T(8,128)(2,1)S(1)} %collective-permute-done.22.refs_5_), channel_id=1, source_target_pairs={{0,1},{1,0},{2,3},{3,2},{4,5},{5,4},{6,7},{7,6},{8,9},{9,8},{10,11... | collective-permute-start | bytes 98312 | tf_op jit(solution)/shard_map/ppermute | solution.py:80

commit v4 on v3

--- a/solution.py
+++ b/solution.py
@@ -86,7 +86,7 @@
         return lax.ppermute(x, both, route(lambda r, z, q: (r, z ^ m, q)))
 
     def turned(x, d):
-        return lax.ppermute(x, both, route(lambda r, z, q: (z, r ^ z ^ d, q)))
+        return lax.ppermute(x, both, route(lambda r, z, q: (z, r ^ z ^ d, q ^ (r == z == d))))
 
     def body(
         tokens,
@@ -158,8 +158,14 @@
             f, z, q = here()
             w_mine = weight_ref[pl.ds(pl.multiple_of(q * F, F), F), :]
             w_other = weight_ref[pl.ds(pl.multiple_of((1 - q) * F, F), F), :]
-            whole_mine = jnp.concatenate([ref[...] for ref in mine_refs])
-            whole_other = jnp.concatenate([ref[...] for ref in other_refs])
+            mine_blocks, other_blocks = [], []
+            for d in range(R):
+                direct = d if d in order else d ^ 1
+                crossed = jnp.logical_and(f == direct, z == d)
+                a, b = mine_refs[d][...], other_refs[d][...]
+                mine_blocks.append(jnp.where(crossed, b, a))
+                other_blocks.append(jnp.where(crossed, a, b))
+            whole_mine, whole_other = jnp.concatenate(mine_blocks), jnp.concatenate(other_blocks)
             whole = (dot(whole_mine, w_mine) + dot(whole_other, w_other)).astype(bf16)
             for d in range(R):
                 part = whole[d * T : (d + 1) * T]
@@ -191,7 +197,10 @@
             [jax.ShapeDtypeStruct(((R + 2) * T, H), bf16)] * R,
             [pltpu.VMEM((R, 2 * T, H), bf16)],
         )
-        parts = [parts[0]] + [over_row(parts[s], s) for s in range(1, R)]
+        far_first = list(range(R - 1, 0, -1))
+        sent_parts = lax.optimization_barrier([over_row(parts[s], s) for s in far_first])
+        parts = [parts[0], *sent_parts[::-1]]
+
         def gradient(*refs):
             cot_ref, gate_ref = refs[:2]
             rows_refs, outs, held = refs[2 : 2 + R], refs[2 + R : 2 + 2 * R], refs[-1]

time: 64.6 us -> 61.7 us (0.955)
  starting transfers between devices: 36.4 us -> 27.1 us
  waiting for transfers between devices: 20 us -> 26.4 us
    ppermute x8, starting transfers between devices: 12.4 us -> 8.4 us  [over_z(): return lax.ppermute(x, both, route(lambda r, z, q: (r, z ^ m, q)))]
    ppermute x2, waiting for transfers between devices: 6.21 us -> 9.7 us  [turned(): lax.ppermute(x, both, route(lambda r, z, q: (z, r ^ z ^ d, q ^ (r == z ==...]
    ppermute x2, starting transfers between devices: 7.09 us -> 3.6 us  [turned(): lax.ppermute(x, both, route(lambda r, z, q: (z, r ^ z ^ d, q ^ (r == z ==...]
    ppermute x8, waiting for transfers between devices: 3.52 us -> 6.33 us  [over_z(): return lax.ppermute(x, both, route(lambda r, z, q: (r, z ^ m, q)))]
    ppermute x10, starting transfers between devices: 14.9 us -> 13 us  [over_row(): return lax.ppermute(x, both, route(lambda r, z, q: (r ^ s, z, q)))]
where the time goes in v4:
time: 61.7 us; the launch traced here: 61.5 us
  starting transfers between devices  27.1 us (44%)
  waiting for transfers between devices  26.4 us (43%)
  Pallas kernels  7.16 us (12%)
  between operations  0.77 us (1%)
    ppermute x10, starting transfers between devices, over_row(): return lax.ppermute(x, both, route(lambda r, z, q: (r ^ s, z, q)))  13 us
    ppermute x2, waiting for transfers between devices, turned(): lax.ppermute(x, both, route(lambda r, z, q: (z, r ^ z ^ d, q ^ (r == z ==...  9.7 us
    ppermute x8, starting transfers between devices, over_z(): return lax.ppermute(x, both, route(lambda r, z, q: (r, z ^ m, q)))  8.4 us
    ppermute x10, waiting for transfers between devices, over_row(): return lax.ppermute(x, both, route(lambda r, z, q: (r ^ s, z, q)))  8.27 us
    pallas_call x7, Pallas kernels, call(): pl.pallas_call(fetch if far else kernel, out_shape=list(outs), in_specs=[...  7.16 us
    ppermute x8, waiting for transfers between devices, over_z(): return lax.ppermute(x, both, route(lambda r, z, q: (r, z ^ m, q)))  6.33 us
    ppermute x2, starting transfers between devices, turned(): lax.ppermute(x, both, route(lambda r, z, q: (z, r ^ z ^ d, q ^ (r == z ==...  3.6 us
    ppermute x9, starting transfers between devices, across_chip(): return lax.ppermute(x, both, route(lambda r, z, q: (r, z, q ^ 1)))  2.1 us
  transfers between devices with their start and end apart: 29, of which 17 were waited for; matrix products, arithmetic and copies ran while one was open for 0% of the time, Pallas kernels for 8%

profile of v4, /device:TPU:0, one launch (start us, length us, event | category | flops | bytes accessed | tf_op | source)
XLA Modules:
  0.0 61.5 jit_solution(2154298374538423142)
XLA Ops:
  0.6 3.0 %collective-permute-start.5 = (bf16[256,768]{1,0:T(8,128)(2,1)}, bf16[256,768]{1,0:T(8,128)(2,1)S(1)}, u32[]{:S(2)}, u32[]{:S(2)}) collective-permute-start(bf16[256,768]{1,0:T(8,128)(2,1)} %refs_12_.1), channel_id=1, source_target_pairs={{0,16},{1,17},{2,18},{3,19},{4,20},{5,21},{6,22},{7,23},{8,24},{9,... | collective-permute-start | bytes 1179656 | tf_op jit(solution)/shard_map/ppermute | solution.py:83
  3.7 1.5 %collective-permute-start.4 = (bf16[256,768]{1,0:T(8,128)(2,1)}, bf16[256,768]{1,0:T(8,128)(2,1)S(1)}, u32[]{:S(2)}, u32[]{:S(2)}) collective-permute-start(bf16[256,768]{1,0:T(8,128)(2,1)} %refs_12_.1), channel_id=1, source_target_pairs={{0,8},{1,9},{2,10},{3,11},{4,12},{5,13},{6,14},{7,15},{8,0},{9,1},... | collective-permute-start | bytes 1179656 | tf_op jit(solution)/shard_map/ppermute | solution.py:83
  5.2 3.6 %collective-permute-start = (bf16[128,768]{1,0:T(8,128)(2,1)}, bf16[128,768]{1,0:T(8,128)(2,1)S(1)}, u32[]{:S(2)}, u32[]{:S(2)}) collective-permute-start(bf16[128,768]{1,0:T(8,128)(2,1)} %refs_0_.5), channel_id=1, source_target_pairs={{0,6},{1,7},{2,12},{3,13},{4,18},{5,19},{6,24},{7,25},{8,4},{9,5},... | collective-permute-start | bytes 589832 | tf_op jit(solution)/shard_map/ppermute | solution.py:89
  8.8 9.7 %collective-permute-done.refs_3_ = bf16[128,768]{1,0:T(8,128)(2,1)S(1)} collective-permute-done((bf16[128,768]{1,0:T(8,128)(2,1)}, bf16[128,768]{1,0:T(8,128)(2,1)S(1)}, u32[]{:S(2)}, u32[]{:S(2)}) %collective-permute-start) | collective-permute-done | bytes 196640 | tf_op jit(solution)/shard_map/ppermute | solution.py:89
  18.5 2.0 %collective-permute-start.3 = (bf16[128,768]{1,0:T(8,128)(2,1)S(1)}, bf16[128,768]{1,0:T(8,128)(2,1)S(1)}, u32[]{:S(2)}, u32[]{:S(2)}) collective-permute-start(bf16[128,768]{1,0:T(8,128)(2,1)S(1)} %collective-permute-done.1.refs_0_), channel_id=1, source_target_pairs={{0,2},{1,3},{2,0},{3,1},{4,6},{5,7},{6,4},{7,5},{8,10},{9,11},{10,... | collective-permute-start | bytes 589832 | tf_op jit(solution)/shard_map/ppermute | solution.py:86
  20.5 1.3 %collective-permute-start.6 = (bf16[128,768]{1,0:T(8,128)(2,1)S(1)}, bf16[128,768]{1,0:T(8,128)(2,1)S(1)}, u32[]{:S(2)}, u32[]{:S(2)}) collective-permute-start(bf16[128,768]{1,0:T(8,128)(2,1)S(1)} %slice.8), channel_id=1, source_target_pairs={{0,8},{1,9},{2,10},{3,11},{4,12},{5,13},{6,14},{7,15},{8,0},{9,1},... | collective-permute-start | bytes 589832 | tf_op jit(solution)/shard_map/ppermute | solution.py:83
  21.8 0.0 copy-start.3
  21.8 0.1 collective-permute-start.7
  21.9 2.5 %prepare.1 = (bf16[128,2048]{1,0:T(8,128)(2,1)S(1)}, bf16[2048,256]{1,0:T(8,128)(2,1)S(1)}, bf16[1536,384]{1,0:T(8,128)(2,1)S(1)}, f32[2,128]{1,0:T(2,128)S(1)}) custom-call(bf16[2048,128]{1,0:T(8,128)(2,1)} %refs_0_.3, bf16[2048,128]{1,0:T(8,128)(2,1)} %refs_1_.1, bf16[1536,128]{1,0:T(8,128)(2,1)} %refs_2_.2, bf16[1536,128]{1,0:T(8,128)(2,1)} %refs_3_.1, ...), custom_call_target="tpu_custom_call" | custom-call | tf_op jit(solution)/shard_map/prepare/pallas_call | solution.py:37
  24.4 1.9 %collective-permute-done.2.refs_2_ = bf16[128,768]{1,0:T(8,128)(2,1)S(1)} collective-permute-done((bf16[128,768]{1,0:T(8,128)(2,1)S(1)}, bf16[128,768]{1,0:T(8,128)(2,1)S(1)}, u32[]{:S(2)}, u32[]{:S(2)}) %collective-permute-start.2) | collective-permute-done | bytes 196640 | tf_op jit(solution)/shard_map/ppermute | solution.py:86
  26.3 2.1 %collective-permute-done.3.refs_1_ = bf16[128,768]{1,0:T(8,128)(2,1)S(1)} collective-permute-done((bf16[128,768]{1,0:T(8,128)(2,1)S(1)}, bf16[128,768]{1,0:T(8,128)(2,1)S(1)}, u32[]{:S(2)}, u32[]{:S(2)}) %collective-permute-start.3) | collective-permute-done | bytes 196640 | tf_op jit(solution)/shard_map/ppermute | solution.py:86
  28.5 0.5 collective-permute-start.9
  29.0 0.1 collective-permute-start.10
  29.0 0.4 collective-permute-start.11
  29.5 0.0 copy-start.2
  29.5 0.4 collective-permute-done.8.refs_4_
  29.9 0.3 collective-permute-done.9.refs_5_
  30.2 0.3 collective-permute-done.10.refs_6_
  30.5 0.3 collective-permute-done.11.refs_7_
  30.7 1.0 %project.1 = (bf16[768,128]{1,0:T(8,128)(2,1)S(1)}, bf16[768,128]{1,0:T(8,128)(2,1)S(1)}, bf16[768,128]{1,0:T(8,128)(2,1)S(1)}, bf16[768,128]{1,0:T(8,128)(2,1)S(1)}) custom-call(bf16[128,768]{1,0:T(8,128)(2,1)S(1)} %collective-permute-done.1.refs_0_, bf16[128,768]{1,0:T(8,128)(2,1)S(1)} %collective-permute-done.3.refs_1_, ...), custom_call_target="tpu_custom_call" | custom-call | tf_op jit(solution)/shard_map/project/pallas_call | solution.py:37
  31.8 0.1 collective-permute-start.12
  31.8 1.7 %collective-permute-start.13 = (bf16[768,128]{1,0:T(8,128)(2,1)S(1)}, bf16[768,128]{1,0:T(8,128)(2,1)S(1)}, u32[]{:S(2)}, u32[]{:S(2)}) collective-permute-start(bf16[768,128]{1,0:T(8,128)(2,1)S(1)} %get-tuple-element.54), channel_id=1, source_target_pairs={{0,16},{1,17},{2,18},{3,19},{4,20},{5,21},{6,22},{7,23},{8,24},{9,... | collective-permute-start | bytes 589832 | tf_op jit(solution)/shard_map/ppermute | solution.py:83
  33.6 1.7 %collective-permute-start.14 = (bf16[768,128]{1,0:T(8,128)(2,1)S(1)}, bf16[768,128]{1,0:T(8,128)(2,1)S(1)}, u32[]{:S(2)}, u32[]{:S(2)}) collective-permute-start(bf16[768,128]{1,0:T(8,128)(2,1)S(1)} %get-tuple-element.55), channel_id=1, source_target_pairs={{0,8},{1,9},{2,10},{3,11},{4,12},{5,13},{6,14},{7,15},{8,0},{9,1},... | collective-permute-start | bytes 589832 | tf_op jit(solution)/shard_map/ppermute | solution.py:83
  35.4 0.7 %gradient.1 = (bf16[256,128]{1,0:T(8,128)(2,1)S(1)}, bf16[256,128]{1,0:T(8,128)(2,1)S(1)}, bf16[256,128]{1,0:T(8,128)(2,1)S(1)}, bf16[256,128]{1,0:T(8,128)(2,1)S(1)}) custom-call(bf16[128,768]{1,0:T(8,128)(2,1)S(1)} %copy-done.2, f32[1,768]{1,0:T(1,128)S(1)} %reshape.13.refs_1_, bf16[256,768]{1,0:T(8,128)(2,1)S(1)} %copy-done, ...), custom_call_target="tpu_custom_call" | custom-call | tf_op jit(solution)/shard_map/gradient/pallas_call | solution.py:37
  36.1 0.3 collective-permute-start.18
  36.4 1.0 %collective-permute-start.19 = (bf16[256,128]{1,0:T(8,128)(2,1)S(1)}, bf16[256,128]{1,0:T(8,128)(2,1)S(1)}, u32[]{:S(2)}, u32[]{:S(2)}) collective-permute-start(bf16[256,128]{1,0:T(8,128)(2,1)S(1)} %get-tuple-element.72), channel_id=1, source_target_pairs={{0,4},{1,5},{2,6},{3,7},{4,0},{5,1},{6,2},{7,3},{8,12},{9,13},{10,... | collective-permute-start | bytes 196616 | tf_op jit(solution)/shard_map/ppermute | solution.py:86
  37.4 3.1 %collective-permute-done.12.refs_3_ = bf16[768,128]{1,0:T(8,128)(2,1)S(1)} collective-permute-done((bf16[768,128]{1,0:T(8,128)(2,1)S(1)}, bf16[768,128]{1,0:T(8,128)(2,1)S(1)}, u32[]{:S(2)}, u32[]{:S(2)}) %collective-permute-start.12) | collective-permute-done | bytes 196640 | tf_op jit(solution)/shard_map/ppermute | solution.py:83
  40.5 0.6 collective-permute-start.20
  41.1 2.0 %collective-permute-done.13.refs_2_ = bf16[768,128]{1,0:T(8,128)(2,1)S(1)} collective-permute-done((bf16[768,128]{1,0:T(8,128)(2,1)S(1)}, bf16[768,128]{1,0:T(8,128)(2,1)S(1)}, u32[]{:S(2)}, u32[]{:S(2)}) %collective-permute-start.13) | collective-permute-done | bytes 196640 | tf_op jit(solution)/shard_map/ppermute | solution.py:83
  43.1 0.8 %collective-permute-done.14.refs_1_ = bf16[768,128]{1,0:T(8,128)(2,1)S(1)} collective-permute-done((bf16[768,128]{1,0:T(8,128)(2,1)S(1)}, bf16[768,128]{1,0:T(8,128)(2,1)S(1)}, u32[]{:S(2)}, u32[]{:S(2)}) %collective-permute-start.14) | collective-permute-done | bytes 196640 | tf_op jit(solution)/shard_map/ppermute | solution.py:83
  44.0 1.7 %attend.1 = (bf16[144,128]{1,0:T(8,128)(2,1)S(1)}, bf16[144,128]{1,0:T(8,128)(2,1)S(1)}, bf16[144,128]{1,0:T(8,128)(2,1)S(1)}, bf16[144,128]{1,0:T(8,128)(2,1)S(1)}) custom-call(bf16[768,128]{1,0:T(8,128)(2,1)S(1)} %get-tuple-element.52.refs_0_, bf16[768,128]{1,0:T(8,128)(2,1)S(1)} %collective-permute-done.14.refs_1_, ...), custom_call_target="tpu_custom_call" | custom-call | tf_op jit(solution)/shard_map/attend/pallas_call | solution.py:37
  45.7 0.4 collective-permute-start.15
  46.1 0.6 %collective-permute-start.16 = (bf16[144,128]{1,0:T(8,128)(2,1)S(1)}, bf16[144,128]{1,0:T(8,128)(2,1)S(1)}, u32[]{:S(2)}, u32[]{:S(2)}) collective-permute-start(bf16[144,128]{1,0:T(8,128)(2,1)S(1)} %get-tuple-element.64), channel_id=1, source_target_pairs={{0,16},{1,17},{2,18},{3,19},{4,20},{5,21},{6,22},{7,23},{8,24},{9,... | collective-permute-start | bytes 110600 | tf_op jit(solution)/shard_map/ppermute | solution.py:83
  46.7 2.6 %collective-permute-start.17 = (bf16[144,128]{1,0:T(8,128)(2,1)S(1)}, bf16[144,128]{1,0:T(8,128)(2,1)S(1)}, u32[]{:S(2)}, u32[]{:S(2)}) collective-permute-start(bf16[144,128]{1,0:T(8,128)(2,1)S(1)} %get-tuple-element.65), channel_id=1, source_target_pairs={{0,24},{1,25},{2,26},{3,27},{4,28},{5,29},{6,30},{7,31},{8,16},{9,... | collective-permute-start | bytes 110600 | tf_op jit(solution)/shard_map/ppermute | solution.py:83
  49.3 0.6 collective-permute-done.15.refs_1_
  49.9 0.5 collective-permute-done.16.refs_2_
  50.4 1.1 %collective-permute-done.17.refs_3_ = bf16[144,128]{1,0:T(8,128)(2,1)S(1)} collective-permute-done((bf16[144,128]{1,0:T(8,128)(2,1)S(1)}, bf16[144,128]{1,0:T(8,128)(2,1)S(1)}, u32[]{:S(2)}, u32[]{:S(2)}) %collective-permute-start.17) | collective-permute-done | bytes 36896 | tf_op jit(solution)/shard_map/ppermute | solution.py:83
  51.6 0.1 finish.1.refs_4_
  51.7 2.2 %collective-permute-start.24 = (bf16[128,128]{1,0:T(8,128)(2,1)S(1)}, bf16[128,128]{1,0:T(8,128)(2,1)S(1)}, u32[]{:S(2)}, u32[]{:S(2)}) collective-permute-start(bf16[128,128]{1,0:T(8,128)(2,1)S(1)} %finish.1.refs_4_), channel_id=1, source_target_pairs={{0,6},{1,7},{2,4},{3,5},{4,2},{5,3},{6,0},{7,1},{8,14},{9,15},{10,... | collective-permute-start | bytes 98312 | tf_op jit(solution)/shard_map/ppermute | solution.py:86
  53.9 1.1 %collective-permute-start.23 = (bf16[128,128]{1,0:T(8,128)(2,1)S(1)}, bf16[128,128]{1,0:T(8,128)(2,1)S(1)}, u32[]{:S(2)}, u32[]{:S(2)}) collective-permute-start(bf16[128,128]{1,0:T(8,128)(2,1)S(1)} %finish.1.refs_4_), channel_id=1, source_target_pairs={{0,4},{1,5},{2,6},{3,7},{4,0},{5,1},{6,2},{7,3},{8,12},{9,13},{10,... | collective-permute-start | bytes 98312 | tf_op jit(solution)/shard_map/ppermute | solution.py:86
  54.9 1.2 %collective-permute-start.22 = (bf16[128,128]{1,0:T(8,128)(2,1)S(1)}, bf16[128,128]{1,0:T(8,128)(2,1)S(1)}, u32[]{:S(2)}, u32[]{:S(2)}) collective-permute-start(bf16[128,128]{1,0:T(8,128)(2,1)S(1)} %finish.1.refs_4_), channel_id=1, source_target_pairs={{0,2},{1,3},{2,0},{3,1},{4,6},{5,7},{6,4},{7,5},{8,10},{9,11},{10,... | collective-permute-start | bytes 98312 | tf_op jit(solution)/shard_map/ppermute | solution.py:86
  56.2 0.6 collective-permute-start.21
  56.7 0.7 %collective-permute-done.24.refs_7_ = bf16[128,128]{1,0:T(8,128)(2,1)S(1)} collective-permute-done((bf16[128,128]{1,0:T(8,128)(2,1)S(1)}, bf16[128,128]{1,0:T(8,128)(2,1)S(1)}, u32[]{:S(2)}, u32[]{:S(2)}) %collective-permute-start.24) | collective-permute-done | bytes 32800 | tf_op jit(solution)/shard_map/ppermute | solution.py:86
  57.5 1.5 %collective-permute-done.23.refs_6_ = bf16[128,128]{1,0:T(8,128)(2,1)S(1)} collective-permute-done((bf16[128,128]{1,0:T(8,128)(2,1)S(1)}, bf16[128,128]{1,0:T(8,128)(2,1)S(1)}, u32[]{:S(2)}, u32[]{:S(2)}) %collective-permute-start.23) | collective-permute-done | bytes 32800 | tf_op jit(solution)/shard_map/ppermute | solution.py:86
  59.0 0.5 collective-permute-start.26
  59.6 0.7 %collective-permute-done.27.refs_10_ = bf16[128,128]{1,0:T(8,128)(2,1)S(1)} collective-permute-done((bf16[128,128]{1,0:T(8,128)(2,1)S(1)}, bf16[128,128]{1,0:T(8,128)(2,1)S(1)}, u32[]{:S(2)}, u32[]{:S(2)}) %collective-permute-start.27) | collective-permute-done | bytes 32800 | tf_op jit(solution)/shard_map/ppermute | solution.py:80
  60.2 0.2 collective-permute-done.26.refs_9_
  60.4 1.1 %output.1 = (bf16[128,768]{1,0:T(8,128)(2,1)}, bf16[128,128]{1,0:T(8,128)(2,1)}) custom-call(bf16[128,768]{1,0:T(8,128)(2,1)S(1)} %copy-done.1, f32[1,768]{1,0:T(1,128)S(1)} %reshape.13.refs_1_, bf16[128,128]{1,0:T(8,128)(2,1)S(1)} %get-tuple-element.78.refs_2_, bf16[128,128]{1,0:T(8,128)(2,1)S(1)} %collective-permute-done.21.refs_3_, ...), custom_call_target="tpu_custom_call" | custom-call | tf_op jit(solution)/shard_map/output/pallas_call | solution.py:37
  (30 shorter events, 0.2 us)
Async XLA Ops:
  0.6 19.9 %collective-permute-start.5 = (bf16[256,768]{1,0:T(8,128)(2,1)}, bf16[256,768]{1,0:T(8,128)(2,1)S(1)}, u32[]{:S(2)}, u32[]{:S(2)}) collective-permute-start(bf16[256,768]{1,0:T(8,128)(2,1)} %refs_12_.1), channel_id=1, source_target_pairs={{0,16},{1,17},{2,18},{3,19},{4,20},{5,21},{6,22},{7,23},{8,24},{9,... | collective-permute-start | bytes 1179656 | tf_op jit(solution)/shard_map/ppermute | solution.py:83
  3.7 18.2 %collective-permute-start.4 = (bf16[256,768]{1,0:T(8,128)(2,1)}, bf16[256,768]{1,0:T(8,128)(2,1)S(1)}, u32[]{:S(2)}, u32[]{:S(2)}) collective-permute-start(bf16[256,768]{1,0:T(8,128)(2,1)} %refs_12_.1), channel_id=1, source_target_pairs={{0,8},{1,9},{2,10},{3,11},{4,12},{5,13},{6,14},{7,15},{8,0},{9,1},... | collective-permute-start | bytes 1179656 | tf_op jit(solution)/shard_map/ppermute | solution.py:83
  5.2 13.3 %collective-permute-start = (bf16[128,768]{1,0:T(8,128)(2,1)}, bf16[128,768]{1,0:T(8,128)(2,1)S(1)}, u32[]{:S(2)}, u32[]{:S(2)}) collective-permute-start(bf16[128,768]{1,0:T(8,128)(2,1)} %refs_0_.5), channel_id=1, source_target_pairs={{0,6},{1,7},{2,12},{3,13},{4,18},{5,19},{6,24},{7,25},{8,4},{9,5},... | collective-permute-start | bytes 589832 | tf_op jit(solution)/shard_map/ppermute | solution.py:89
  8.8 9.7 %collective-permute-start.1 = (bf16[128,768]{1,0:T(8,128)(2,1)}, bf16[128,768]{1,0:T(8,128)(2,1)S(1)}, u32[]{:S(2)}, u32[]{:S(2)}) collective-permute-start(bf16[128,768]{1,0:T(8,128)(2,1)} %refs_0_.5), channel_id=1, source_target_pairs={{0,1},{1,0},{2,10},{3,11},{4,20},{5,21},{6,30},{7,31},{8,2},{9,3},... | collective-permute-start | bytes 589832 | tf_op jit(solution)/shard_map/ppermute | solution.py:89
  18.5 7.8 %collective-permute-start.2 = (bf16[128,768]{1,0:T(8,128)(2,1)S(1)}, bf16[128,768]{1,0:T(8,128)(2,1)S(1)}, u32[]{:S(2)}, u32[]{:S(2)}) collective-permute-start(bf16[128,768]{1,0:T(8,128)(2,1)S(1)} %collective-permute-done.refs_3_), channel_id=1, source_target_pairs={{0,2},{1,3},{2,0},{3,1},{4,6},{5,7},{6,4},{7,5},{8,10},{9,11},{10,... | collective-permute-start | bytes 589832 | tf_op jit(solution)/shard_map/ppermute | solution.py:86
  18.5 10.0 %collective-permute-start.3 = (bf16[128,768]{1,0:T(8,128)(2,1)S(1)}, bf16[128,768]{1,0:T(8,128)(2,1)S(1)}, u32[]{:S(2)}, u32[]{:S(2)}) collective-permute-start(bf16[128,768]{1,0:T(8,128)(2,1)S(1)} %collective-permute-done.1.refs_0_), channel_id=1, source_target_pairs={{0,2},{1,3},{2,0},{3,1},{4,6},{5,7},{6,4},{7,5},{8,10},{9,11},{10,... | collective-permute-start | bytes 589832 | tf_op jit(solution)/shard_map/ppermute | solution.py:86
  20.5 7.9 %collective-permute-start.6 = (bf16[128,768]{1,0:T(8,128)(2,1)S(1)}, bf16[128,768]{1,0:T(8,128)(2,1)S(1)}, u32[]{:S(2)}, u32[]{:S(2)}) collective-permute-start(bf16[128,768]{1,0:T(8,128)(2,1)S(1)} %slice.8), channel_id=1, source_target_pairs={{0,8},{1,9},{2,10},{3,11},{4,12},{5,13},{6,14},{7,15},{8,0},{9,1},... | collective-permute-start | bytes 589832 | tf_op jit(solution)/shard_map/ppermute | solution.py:83
  21.8 7.6 %copy-start.3 = (f32[768]{0:T(1024)S(1)}, f32[768]{0:T(1024)}, u32[]{:S(2)}) copy-start(f32[768]{0:T(1024)} %param.20) | copy-start | bytes 9220
  21.8 6.6 %collective-permute-start.7 = (bf16[128,768]{1,0:T(8,128)(2,1)S(1)}, bf16[128,768]{1,0:T(8,128)(2,1)S(1)}, u32[]{:S(2)}, u32[]{:S(2)}) collective-permute-start(bf16[128,768]{1,0:T(8,128)(2,1)S(1)} %slice.9), channel_id=1, source_target_pairs={{0,16},{1,17},{2,18},{3,19},{4,20},{5,21},{6,22},{7,23},{8,24},{9,... | collective-permute-start | bytes 589832 | tf_op jit(solution)/shard_map/ppermute | solution.py:83
  28.4 1.4 %collective-permute-start.8 = (bf16[128,768]{1,0:T(8,128)(2,1)S(1)}, bf16[128,768]{1,0:T(8,128)(2,1)S(1)}, u32[]{:S(2)}, u32[]{:S(2)}) collective-permute-start(bf16[128,768]{1,0:T(8,128)(2,1)S(1)} %collective-permute-done.1.refs_0_), channel_id=1, source_target_pairs={{0,1},{1,0},{2,3},{3,2},{4,5},{5,4},{6,7},{7,6},{8,9},{9,8},{10,11... | collective-permute-start | bytes 589832 | tf_op jit(solution)/shard_map/ppermute | solution.py:80
  28.5 1.7 %collective-permute-start.9 = (bf16[128,768]{1,0:T(8,128)(2,1)S(1)}, bf16[128,768]{1,0:T(8,128)(2,1)S(1)}, u32[]{:S(2)}, u32[]{:S(2)}) collective-permute-start(bf16[128,768]{1,0:T(8,128)(2,1)S(1)} %collective-permute-done.3.refs_1_), channel_id=1, source_target_pairs={{0,1},{1,0},{2,3},{3,2},{4,5},{5,4},{6,7},{7,6},{8,9},{9,8},{10,11... | collective-permute-start | bytes 589832 | tf_op jit(solution)/shard_map/ppermute | solution.py:80
  29.0 1.5 %collective-permute-start.10 = (bf16[128,768]{1,0:T(8,128)(2,1)S(1)}, bf16[128,768]{1,0:T(8,128)(2,1)S(1)}, u32[]{:S(2)}, u32[]{:S(2)}) collective-permute-start(bf16[128,768]{1,0:T(8,128)(2,1)S(1)} %collective-permute-done.2.refs_2_), channel_id=1, source_target_pairs={{0,1},{1,0},{2,3},{3,2},{4,5},{5,4},{6,7},{7,6},{8,9},{9,8},{10,11... | collective-permute-start | bytes 589832 | tf_op jit(solution)/shard_map/ppermute | solution.py:80
  29.0 1.7 %collective-permute-start.11 = (bf16[128,768]{1,0:T(8,128)(2,1)S(1)}, bf16[128,768]{1,0:T(8,128)(2,1)S(1)}, u32[]{:S(2)}, u32[]{:S(2)}) collective-permute-start(bf16[128,768]{1,0:T(8,128)(2,1)S(1)} %collective-permute-done.refs_3_), channel_id=1, source_target_pairs={{0,1},{1,0},{2,3},{3,2},{4,5},{5,4},{6,7},{7,6},{8,9},{9,8},{10,11... | collective-permute-start | bytes 589832 | tf_op jit(solution)/shard_map/ppermute | solution.py:80
  29.5 5.9 %copy-start = (bf16[256,768]{1,0:T(8,128)(2,1)S(1)}, bf16[256,768]{1,0:T(8,128)(2,1)}, u32[]{:S(2)}) copy-start(bf16[256,768]{1,0:T(8,128)(2,1)} %refs_12_.1) | copy-start | bytes 1179652
  29.5 5.9 %copy-start.2 = (bf16[128,768]{1,0:T(8,128)(2,1)S(1)}, bf16[128,768]{1,0:T(8,128)(2,1)}, u32[]{:S(2)}) copy-start(bf16[128,768]{1,0:T(8,128)(2,1)} %refs_0_.4) | copy-start | bytes 589828
  31.8 8.7 %collective-permute-start.12 = (bf16[768,128]{1,0:T(8,128)(2,1)S(1)}, bf16[768,128]{1,0:T(8,128)(2,1)S(1)}, u32[]{:S(2)}, u32[]{:S(2)}) collective-permute-start(bf16[768,128]{1,0:T(8,128)(2,1)S(1)} %get-tuple-element.53), channel_id=1, source_target_pairs={{0,24},{1,25},{2,26},{3,27},{4,28},{5,29},{6,30},{7,31},{8,16},{9,... | collective-permute-start | bytes 589832 | tf_op jit(solution)/shard_map/ppermute | solution.py:83
  31.8 11.3 %collective-permute-start.13 = (bf16[768,128]{1,0:T(8,128)(2,1)S(1)}, bf16[768,128]{1,0:T(8,128)(2,1)S(1)}, u32[]{:S(2)}, u32[]{:S(2)}) collective-permute-start(bf16[768,128]{1,0:T(8,128)(2,1)S(1)} %get-tuple-element.54), channel_id=1, source_target_pairs={{0,16},{1,17},{2,18},{3,19},{4,20},{5,21},{6,22},{7,23},{8,24},{9,... | collective-permute-start | bytes 589832 | tf_op jit(solution)/shard_map/ppermute | solution.py:83
  33.6 10.4 %collective-permute-start.14 = (bf16[768,128]{1,0:T(8,128)(2,1)S(1)}, bf16[768,128]{1,0:T(8,128)(2,1)S(1)}, u32[]{:S(2)}, u32[]{:S(2)}) collective-permute-start(bf16[768,128]{1,0:T(8,128)(2,1)S(1)} %get-tuple-element.55), channel_id=1, source_target_pairs={{0,8},{1,9},{2,10},{3,11},{4,12},{5,13},{6,14},{7,15},{8,0},{9,1},... | collective-permute-start | bytes 589832 | tf_op jit(solution)/shard_map/ppermute | solution.py:83
  36.1 10.6 %collective-permute-start.18 = (bf16[256,128]{1,0:T(8,128)(2,1)S(1)}, bf16[256,128]{1,0:T(8,128)(2,1)S(1)}, u32[]{:S(2)}, u32[]{:S(2)}) collective-permute-start(bf16[256,128]{1,0:T(8,128)(2,1)S(1)} %get-tuple-element.71), channel_id=1, source_target_pairs={{0,2},{1,3},{2,0},{3,1},{4,6},{5,7},{6,4},{7,5},{8,10},{9,11},{10,... | collective-permute-start | bytes 196616 | tf_op jit(solution)/shard_map/ppermute | solution.py:86
  36.4 12.9 %collective-permute-start.19 = (bf16[256,128]{1,0:T(8,128)(2,1)S(1)}, bf16[256,128]{1,0:T(8,128)(2,1)S(1)}, u32[]{:S(2)}, u32[]{:S(2)}) collective-permute-start(bf16[256,128]{1,0:T(8,128)(2,1)S(1)} %get-tuple-element.72), channel_id=1, source_target_pairs={{0,4},{1,5},{2,6},{3,7},{4,0},{5,1},{6,2},{7,3},{8,12},{9,13},{10,... | collective-permute-start | bytes 196616 | tf_op jit(solution)/shard_map/ppermute | solution.py:86
  40.5 8.8 %collective-permute-start.20 = (bf16[256,128]{1,0:T(8,128)(2,1)S(1)}, bf16[256,128]{1,0:T(8,128)(2,1)S(1)}, u32[]{:S(2)}, u32[]{:S(2)}) collective-permute-start(bf16[256,128]{1,0:T(8,128)(2,1)S(1)} %get-tuple-element.73), channel_id=1, source_target_pairs={{0,6},{1,7},{2,4},{3,5},{4,2},{5,3},{6,0},{7,1},{8,14},{9,15},{10,... | collective-permute-start | bytes 196616 | tf_op jit(solution)/shard_map/ppermute | solution.py:86
  44.0 16.4 %copy-start.1 = (bf16[128,768]{1,0:T(8,128)(2,1)S(1)}, bf16[128,768]{1,0:T(8,128)(2,1)}, u32[]{:S(2)}) copy-start(bf16[128,768]{1,0:T(8,128)(2,1)} %refs_0_.5) | copy-start | bytes 589828
  45.7 4.2 %collective-permute-start.15 = (bf16[144,128]{1,0:T(8,128)(2,1)S(1)}, bf16[144,128]{1,0:T(8,128)(2,1)S(1)}, u32[]{:S(2)}, u32[]{:S(2)}) collective-permute-start(bf16[144,128]{1,0:T(8,128)(2,1)S(1)} %get-tuple-element.63), channel_id=1, source_target_pairs={{0,8},{1,9},{2,10},{3,11},{4,12},{5,13},{6,14},{7,15},{8,0},{9,1},... | collective-permute-start | bytes 110600 | tf_op jit(solution)/shard_map/ppermute | solution.py:83
  46.1 4.3 %collective-permute-start.16 = (bf16[144,128]{1,0:T(8,128)(2,1)S(1)}, bf16[144,128]{1,0:T(8,128)(2,1)S(1)}, u32[]{:S(2)}, u32[]{:S(2)}) collective-permute-start(bf16[144,128]{1,0:T(8,128)(2,1)S(1)} %get-tuple-element.64), channel_id=1, source_target_pairs={{0,16},{1,17},{2,18},{3,19},{4,20},{5,21},{6,22},{7,23},{8,24},{9,... | collective-permute-start | bytes 110600 | tf_op jit(solution)/shard_map/ppermute | solution.py:83
  46.7 4.9 %collective-permute-start.17 = (bf16[144,128]{1,0:T(8,128)(2,1)S(1)}, bf16[144,128]{1,0:T(8,128)(2,1)S(1)}, u32[]{:S(2)}, u32[]{:S(2)}) collective-permute-start(bf16[144,128]{1,0:T(8,128)(2,1)S(1)} %get-tuple-element.65), channel_id=1, source_target_pairs={{0,24},{1,25},{2,26},{3,27},{4,28},{5,29},{6,30},{7,31},{8,16},{9,... | collective-permute-start | bytes 110600 | tf_op jit(solution)/shard_map/ppermute | solution.py:83
  51.7 5.8 %collective-permute-start.24 = (bf16[128,128]{1,0:T(8,128)(2,1)S(1)}, bf16[128,128]{1,0:T(8,128)(2,1)S(1)}, u32[]{:S(2)}, u32[]{:S(2)}) collective-permute-start(bf16[128,128]{1,0:T(8,128)(2,1)S(1)} %finish.1.refs_4_), channel_id=1, source_target_pairs={{0,6},{1,7},{2,4},{3,5},{4,2},{5,3},{6,0},{7,1},{8,14},{9,15},{10,... | collective-permute-start | bytes 98312 | tf_op jit(solution)/shard_map/ppermute | solution.py:86
  53.9 5.2 %collective-permute-start.23 = (bf16[128,128]{1,0:T(8,128)(2,1)S(1)}, bf16[128,128]{1,0:T(8,128)(2,1)S(1)}, u32[]{:S(2)}, u32[]{:S(2)}) collective-permute-start(bf16[128,128]{1,0:T(8,128)(2,1)S(1)} %finish.1.refs_4_), channel_id=1, source_target_pairs={{0,4},{1,5},{2,6},{3,7},{4,0},{5,1},{6,2},{7,3},{8,12},{9,13},{10,... | collective-permute-start | bytes 98312 | tf_op jit(solution)/shard_map/ppermute | solution.py:86
  54.9 4.1 %collective-permute-start.22 = (bf16[128,128]{1,0:T(8,128)(2,1)S(1)}, bf16[128,128]{1,0:T(8,128)(2,1)S(1)}, u32[]{:S(2)}, u32[]{:S(2)}) collective-permute-start(bf16[128,128]{1,0:T(8,128)(2,1)S(1)} %finish.1.refs_4_), channel_id=1, source_target_pairs={{0,2},{1,3},{2,0},{3,1},{4,6},{5,7},{6,4},{7,5},{8,10},{9,11},{10,... | collective-permute-start | bytes 98312 | tf_op jit(solution)/shard_map/ppermute | solution.py:86
  56.1 3.4 %collective-permute-start.25 = (bf16[128,128]{1,0:T(8,128)(2,1)S(1)}, bf16[128,128]{1,0:T(8,128)(2,1)S(1)}, u32[]{:S(2)}, u32[]{:S(2)}) collective-permute-start(bf16[128,128]{1,0:T(8,128)(2,1)S(1)} %finish.1.refs_4_), channel_id=1, source_target_pairs={{0,1},{1,0},{2,3},{3,2},{4,5},{5,4},{6,7},{7,6},{8,9},{9,8},{10,11... | collective-permute-start | bytes 98312 | tf_op jit(solution)/shard_map/ppermute | solution.py:80
  56.2 3.4 %collective-permute-start.21 = (bf16[128,128]{1,0:T(8,128)(2,1)S(1)}, bf16[128,128]{1,0:T(8,128)(2,1)S(1)}, u32[]{:S(2)}, u32[]{:S(2)}) collective-permute-start(bf16[128,128]{1,0:T(8,128)(2,1)S(1)} %get-tuple-element.79), channel_id=1, source_target_pairs={{0,1},{1,0},{2,3},{3,2},{4,5},{5,4},{6,7},{7,6},{8,9},{9,8},{10,11... | collective-permute-start | bytes 98312 | tf_op jit(solution)/shard_map/ppermute | solution.py:80
  57.5 2.1 %collective-permute-start.28 = (bf16[128,128]{1,0:T(8,128)(2,1)S(1)}, bf16[128,128]{1,0:T(8,128)(2,1)S(1)}, u32[]{:S(2)}, u32[]{:S(2)}) collective-permute-start(bf16[128,128]{1,0:T(8,128)(2,1)S(1)} %collective-permute-done.24.refs_7_), channel_id=1, source_target_pairs={{0,1},{1,0},{2,3},{3,2},{4,5},{5,4},{6,7},{7,6},{8,9},{9,8},{10,11... | collective-permute-start | bytes 98312 | tf_op jit(solution)/shard_map/ppermute | solution.py:80
  59.0 1.2 %collective-permute-start.27 = (bf16[128,128]{1,0:T(8,128)(2,1)S(1)}, bf16[128,128]{1,0:T(8,128)(2,1)S(1)}, u32[]{:S(2)}, u32[]{:S(2)}) collective-permute-start(bf16[128,128]{1,0:T(8,128)(2,1)S(1)} %collective-permute-done.23.refs_6_), channel_id=1, source_target_pairs={{0,1},{1,0},{2,3},{3,2},{4,5},{5,4},{6,7},{7,6},{8,9},{9,8},{10,11... | collective-permute-start | bytes 98312 | tf_op jit(solution)/shard_map/ppermute | solution.py:80
  59.0 1.4 %collective-permute-start.26 = (bf16[128,128]{1,0:T(8,128)(2,1)S(1)}, bf16[128,128]{1,0:T(8,128)(2,1)S(1)}, u32[]{:S(2)}, u32[]{:S(2)}) collective-permute-start(bf16[128,128]{1,0:T(8,128)(2,1)S(1)} %collective-permute-done.22.refs_5_), channel_id=1, source_target_pairs={{0,1},{1,0},{2,3},{3,2},{4,5},{5,4},{6,7},{7,6},{8,9},{9,8},{10,11... | collective-permute-start | bytes 98312 | tf_op jit(solution)/shard_map/ppermute | solution.py:80

commit v5 on v4

--- a/solution.py
+++ b/solution.py
@@ -152,32 +152,50 @@
             far=7,
         )
 
-        def project(*refs):
-            mine_refs, other_refs, weight_ref = refs[:R], refs[R : 2 * R], refs[2 * R]
-            outs, held = refs[2 * R + 1 : 3 * R + 1], refs[-1]
+        def product(mine_refs, other_refs, weight_ref, ds):
             f, z, q = here()
             w_mine = weight_ref[pl.ds(pl.multiple_of(q * F, F), F), :]
             w_other = weight_ref[pl.ds(pl.multiple_of((1 - q) * F, F), F), :]
             mine_blocks, other_blocks = [], []
-            for d in range(R):
+            for d, mine_ref, other_ref in zip(ds, mine_refs, other_refs):
                 direct = d if d in order else d ^ 1
                 crossed = jnp.logical_and(f == direct, z == d)
-                a, b = mine_refs[d][...], other_refs[d][...]
+                a, b = mine_ref[...], other_ref[...]
                 mine_blocks.append(jnp.where(crossed, b, a))
                 other_blocks.append(jnp.where(crossed, a, b))
             whole_mine, whole_other = jnp.concatenate(mine_blocks), jnp.concatenate(other_blocks)
-            whole = (dot(whole_mine, w_mine) + dot(whole_other, w_other)).astype(bf16)
-            for d in range(R):
-                part = whole[d * T : (d + 1) * T]
-                block = f ^ z ^ d
-                rows = pl.ds(pl.multiple_of(block * T, T), T)
-                for s in range(R):
-                    outs[s][rows, :] = part[:, :H]
-                held[block, :T] = part[:, H : 2 * H]
-                held[block, T:] = part[:, 2 * H :]
+            return (dot(whole_mine, w_mine) + dot(whole_other, w_other)).astype(bf16)
+
+        later = [d ^ 1 for d in order]
+        n = len(order)
+
+        def project_direct(*refs):
+            refs[-1][...] = product(refs[:n], refs[n : 2 * n], refs[2 * n], order)
+
+        def project(*refs):
+            direct_ref, weight_ref = refs[2 * n : 2 * n + 2]
+            outs, held = refs[2 * n + 2 : -1], refs[-1]
+            f, z, _ = here()
+            whole = product(refs[:n], refs[n : 2 * n], weight_ref, later)
+            for ds, found in ((order, direct_ref), (later, whole)):
+                for i, d in enumerate(ds):
+                    part = found[i * T : (i + 1) * T]
+                    block = f ^ z ^ d
+                    rows = pl.ds(pl.multiple_of(block * T, T), T)
+                    for s in range(R):
+                        outs[s][rows, :] = part[:, :H]
+                    held[block, :T] = part[:, H : 2 * H]
+                    held[block, T:] = part[:, 2 * H :]
             for s in range(R):
                 outs[s][R * T :, :] = held[f ^ s]
 
+        direct_other = [across_chip(mine[d]) for d in order]
+        (direct_part,) = call(
+            project_direct,
+            "project_direct",
+            (*[mine[d] for d in order], *direct_other, weights),
+            [jax.ShapeDtypeStruct((n * T, 3 * H), bf16)],
+        )
         joined = lax.optimization_barrier(
             (
                 list(mine.values()),
@@ -186,14 +204,13 @@
             )
         )
         slots, out_rows = dict(zip(mine, joined[0])), [w_out, *joined[1]]
-        slots = [slots[d] for d in range(R)]
         keys_t, values_one, weights, gains = joined[2]
         out_rows = [x if not isinstance(x, tuple) else x[0] if len(x) == 1 else jnp.concatenate(x) for x in out_rows]
-        slots_other = [across_chip(x) for x in slots]
+        later_other = [across_chip(slots[d]) for d in later]
         parts = call(
             project,
             "project",
-            (*slots, *slots_other, weights),
+            (*[slots[d] for d in later], *later_other, direct_part, weights),
             [jax.ShapeDtypeStruct(((R + 2) * T, H), bf16)] * R,
             [pltpu.VMEM((R, 2 * T, H), bf16)],
         )

time: 61.7 us -> 60.7 us (0.984)
  waiting for transfers between devices: 26.4 us -> 25.6 us
    ppermute x9, waiting for transfers between devices: 2.09 us -> 1.41 us  [across_chip(): return lax.ppermute(x, both, route(lambda r, z, q: (r, z, q ^ 1)))]
    pallas_call x7 -> x8, Pallas kernels: 7.16 us -> 7.37 us  [call(): pl.pallas_call(fetch if far else kernel, out_shape=list(outs), in_specs=[...]
  transfers between devices with their start and end apart: 29 -> 29, of which waited for: 17 -> 15; matrix products, arithmetic and copies ran while one was open for 0% -> 0% of each run, Pallas kernels for 8% -> 9%
where the time goes in v5:
time: 60.7 us; the launch traced here: 60.6 us
  starting transfers between devices  26.7 us (44%)
  waiting for transfers between devices  25.6 us (42%)
  Pallas kernels  7.37 us (12%)
  between operations  0.8 us (1%)
    ppermute x10, starting transfers between devices, over_row(): return lax.ppermute(x, both, route(lambda r, z, q: (r ^ s, z, q)))  13 us
    ppermute x2, waiting for transfers between devices, turned(): lax.ppermute(x, both, route(lambda r, z, q: (z, r ^ z ^ d, q ^ (r == z ==...  9.7 us
    ppermute x8, starting transfers between devices, over_z(): return lax.ppermute(x, both, route(lambda r, z, q: (r, z ^ m, q)))  8.39 us
    ppermute x10, waiting for transfers between devices, over_row(): return lax.ppermute(x, both, route(lambda r, z, q: (r ^ s, z, q)))  8.27 us
    pallas_call x8, Pallas kernels, call(): pl.pallas_call(fetch if far else kernel, out_shape=list(outs), in_specs=[...  7.37 us
    ppermute x8, waiting for transfers between devices, over_z(): return lax.ppermute(x, both, route(lambda r, z, q: (r, z ^ m, q)))  6.24 us
    ppermute x2, starting transfers between devices, turned(): lax.ppermute(x, both, route(lambda r, z, q: (z, r ^ z ^ d, q ^ (r == z ==...  3.6 us
    ppermute x9, starting transfers between devices, across_chip(): return lax.ppermute(x, both, route(lambda r, z, q: (r, z, q ^ 1)))  1.67 us
  transfers between devices with their start and end apart: 29, of which 15 were waited for; matrix products, arithmetic and copies ran while one was open for 0% of the time, Pallas kernels for 9%

profile of v5, /device:TPU:0, one launch (start us, length us, event | category | flops | bytes accessed | tf_op | source)
XLA Modules:
  0.0 60.6 jit_solution(15933799401480726479)
XLA Ops:
  0.6 3.0 %collective-permute-start.5 = (bf16[256,768]{1,0:T(8,128)(2,1)}, bf16[256,768]{1,0:T(8,128)(2,1)S(1)}, u32[]{:S(2)}, u32[]{:S(2)}) collective-permute-start(bf16[256,768]{1,0:T(8,128)(2,1)} %refs_12_.1), channel_id=1, source_target_pairs={{0,16},{1,17},{2,18},{3,19},{4,20},{5,21},{6,22},{7,23},{8,24},{9,... | collective-permute-start | bytes 1179656 | tf_op jit(solution)/shard_map/ppermute | solution.py:83
  3.7 1.5 %collective-permute-start.4 = (bf16[256,768]{1,0:T(8,128)(2,1)}, bf16[256,768]{1,0:T(8,128)(2,1)S(1)}, u32[]{:S(2)}, u32[]{:S(2)}) collective-permute-start(bf16[256,768]{1,0:T(8,128)(2,1)} %refs_12_.1), channel_id=1, source_target_pairs={{0,8},{1,9},{2,10},{3,11},{4,12},{5,13},{6,14},{7,15},{8,0},{9,1},... | collective-permute-start | bytes 1179656 | tf_op jit(solution)/shard_map/ppermute | solution.py:83
  5.2 3.6 %collective-permute-start = (bf16[128,768]{1,0:T(8,128)(2,1)}, bf16[128,768]{1,0:T(8,128)(2,1)S(1)}, u32[]{:S(2)}, u32[]{:S(2)}) collective-permute-start(bf16[128,768]{1,0:T(8,128)(2,1)} %refs_0_.5), channel_id=1, source_target_pairs={{0,6},{1,7},{2,12},{3,13},{4,18},{5,19},{6,24},{7,25},{8,4},{9,5},... | collective-permute-start | bytes 589832 | tf_op jit(solution)/shard_map/ppermute | solution.py:89
  8.8 9.7 %collective-permute-done.refs_0_ = bf16[128,768]{1,0:T(8,128)(2,1)S(1)} collective-permute-done((bf16[128,768]{1,0:T(8,128)(2,1)}, bf16[128,768]{1,0:T(8,128)(2,1)S(1)}, u32[]{:S(2)}, u32[]{:S(2)}) %collective-permute-start) | collective-permute-done | bytes 196640 | tf_op jit(solution)/shard_map/ppermute | solution.py:89
  18.5 2.0 %collective-permute-start.3 = (bf16[128,768]{1,0:T(8,128)(2,1)S(1)}, bf16[128,768]{1,0:T(8,128)(2,1)S(1)}, u32[]{:S(2)}, u32[]{:S(2)}) collective-permute-start(bf16[128,768]{1,0:T(8,128)(2,1)S(1)} %collective-permute-done.1.refs_1_), channel_id=1, source_target_pairs={{0,2},{1,3},{2,0},{3,1},{4,6},{5,7},{6,4},{7,5},{8,10},{9,11},{10,... | collective-permute-start | bytes 589832 | tf_op jit(solution)/shard_map/ppermute | solution.py:86
  20.5 0.0 collective-permute-done.5.refs_4_.refs_14_
  20.5 1.3 %collective-permute-start.6 = (bf16[128,768]{1,0:T(8,128)(2,1)S(1)}, bf16[128,768]{1,0:T(8,128)(2,1)S(1)}, u32[]{:S(2)}, u32[]{:S(2)}) collective-permute-start(bf16[128,768]{1,0:T(8,128)(2,1)S(1)} %slice.8), channel_id=1, source_target_pairs={{0,8},{1,9},{2,10},{3,11},{4,12},{5,13},{6,14},{7,15},{8,0},{9,1},... | collective-permute-start | bytes 589832 | tf_op jit(solution)/shard_map/ppermute | solution.py:83
  21.8 0.0 copy-start.3
  21.8 0.1 collective-permute-start.7
  21.9 2.5 %prepare.1 = (bf16[128,2048]{1,0:T(8,128)(2,1)S(1)}, bf16[2048,256]{1,0:T(8,128)(2,1)S(1)}, bf16[1536,384]{1,0:T(8,128)(2,1)S(1)}, f32[2,128]{1,0:T(2,128)S(1)}) custom-call(bf16[2048,128]{1,0:T(8,128)(2,1)} %refs_0_.3, bf16[2048,128]{1,0:T(8,128)(2,1)} %refs_1_.1, bf16[1536,128]{1,0:T(8,128)(2,1)} %refs_2_.2, bf16[1536,128]{1,0:T(8,128)(2,1)} %refs_3_.1, ...), custom_call_target="tpu_custom_call" | custom-call | tf_op jit(solution)/shard_map/prepare/pallas_call | solution.py:37
  24.4 0.1 collective-permute-start.10
  24.5 1.8 %collective-permute-done.2.refs_0_ = bf16[128,768]{1,0:T(8,128)(2,1)S(1)} collective-permute-done((bf16[128,768]{1,0:T(8,128)(2,1)S(1)}, bf16[128,768]{1,0:T(8,128)(2,1)S(1)}, u32[]{:S(2)}, u32[]{:S(2)}) %collective-permute-start.2) | collective-permute-done | bytes 196640 | tf_op jit(solution)/shard_map/ppermute | solution.py:86
  26.3 2.1 %collective-permute-done.3.refs_1_ = bf16[128,768]{1,0:T(8,128)(2,1)S(1)} collective-permute-done((bf16[128,768]{1,0:T(8,128)(2,1)S(1)}, bf16[128,768]{1,0:T(8,128)(2,1)S(1)}, u32[]{:S(2)}, u32[]{:S(2)}) %collective-permute-start.3) | collective-permute-done | bytes 196640 | tf_op jit(solution)/shard_map/ppermute | solution.py:86
  28.5 0.5 collective-permute-start.9
  29.0 0.6 project_direct.1.refs_4_
  29.6 0.0 copy-start
  29.6 0.0 copy-start.2
  29.6 0.3 collective-permute-done.8.refs_2_
  29.9 0.3 collective-permute-done.9.refs_3_
  30.2 0.6 %project.1 = (bf16[768,128]{1,0:T(8,128)(2,1)S(1)}, bf16[768,128]{1,0:T(8,128)(2,1)S(1)}, bf16[768,128]{1,0:T(8,128)(2,1)S(1)}, bf16[768,128]{1,0:T(8,128)(2,1)S(1)}) custom-call(bf16[128,768]{1,0:T(8,128)(2,1)S(1)} %collective-permute-done.2.refs_0_, bf16[128,768]{1,0:T(8,128)(2,1)S(1)} %collective-permute-done.3.refs_1_, ...), custom_call_target="tpu_custom_call" | custom-call | tf_op jit(solution)/shard_map/project/pallas_call | solution.py:37
  30.8 0.1 collective-permute-start.12
  30.9 1.7 %collective-permute-start.13 = (bf16[768,128]{1,0:T(8,128)(2,1)S(1)}, bf16[768,128]{1,0:T(8,128)(2,1)S(1)}, u32[]{:S(2)}, u32[]{:S(2)}) collective-permute-start(bf16[768,128]{1,0:T(8,128)(2,1)S(1)} %get-tuple-element.50), channel_id=1, source_target_pairs={{0,16},{1,17},{2,18},{3,19},{4,20},{5,21},{6,22},{7,23},{8,24},{9,... | collective-permute-start | bytes 589832 | tf_op jit(solution)/shard_map/ppermute | solution.py:83
  32.6 1.7 %collective-permute-start.14 = (bf16[768,128]{1,0:T(8,128)(2,1)S(1)}, bf16[768,128]{1,0:T(8,128)(2,1)S(1)}, u32[]{:S(2)}, u32[]{:S(2)}) collective-permute-start(bf16[768,128]{1,0:T(8,128)(2,1)S(1)} %get-tuple-element.51), channel_id=1, source_target_pairs={{0,8},{1,9},{2,10},{3,11},{4,12},{5,13},{6,14},{7,15},{8,0},{9,1},... | collective-permute-start | bytes 589832 | tf_op jit(solution)/shard_map/ppermute | solution.py:83
  34.4 0.7 %gradient.1 = (bf16[256,128]{1,0:T(8,128)(2,1)S(1)}, bf16[256,128]{1,0:T(8,128)(2,1)S(1)}, bf16[256,128]{1,0:T(8,128)(2,1)S(1)}, bf16[256,128]{1,0:T(8,128)(2,1)S(1)}) custom-call(bf16[128,768]{1,0:T(8,128)(2,1)S(1)} %copy-done.2, f32[1,768]{1,0:T(1,128)S(1)} %reshape.13.refs_1_, bf16[256,768]{1,0:T(8,128)(2,1)S(1)} %copy-done, ...), custom_call_target="tpu_custom_call" | custom-call | tf_op jit(solution)/shard_map/gradient/pallas_call | solution.py:37
  35.1 0.4 collective-permute-start.18
  35.5 1.0 %collective-permute-start.19 = (bf16[256,128]{1,0:T(8,128)(2,1)S(1)}, bf16[256,128]{1,0:T(8,128)(2,1)S(1)}, u32[]{:S(2)}, u32[]{:S(2)}) collective-permute-start(bf16[256,128]{1,0:T(8,128)(2,1)S(1)} %get-tuple-element.68), channel_id=1, source_target_pairs={{0,4},{1,5},{2,6},{3,7},{4,0},{5,1},{6,2},{7,3},{8,12},{9,13},{10,... | collective-permute-start | bytes 196616 | tf_op jit(solution)/shard_map/ppermute | solution.py:86
  36.4 3.1 %collective-permute-done.12.refs_3_ = bf16[768,128]{1,0:T(8,128)(2,1)S(1)} collective-permute-done((bf16[768,128]{1,0:T(8,128)(2,1)S(1)}, bf16[768,128]{1,0:T(8,128)(2,1)S(1)}, u32[]{:S(2)}, u32[]{:S(2)}) %collective-permute-start.12) | collective-permute-done | bytes 196640 | tf_op jit(solution)/shard_map/ppermute | solution.py:83
  39.6 0.6 collective-permute-start.20
  40.2 2.0 %collective-permute-done.13.refs_2_ = bf16[768,128]{1,0:T(8,128)(2,1)S(1)} collective-permute-done((bf16[768,128]{1,0:T(8,128)(2,1)S(1)}, bf16[768,128]{1,0:T(8,128)(2,1)S(1)}, u32[]{:S(2)}, u32[]{:S(2)}) %collective-permute-start.13) | collective-permute-done | bytes 196640 | tf_op jit(solution)/shard_map/ppermute | solution.py:83
  42.2 0.8 %collective-permute-done.14.refs_1_ = bf16[768,128]{1,0:T(8,128)(2,1)S(1)} collective-permute-done((bf16[768,128]{1,0:T(8,128)(2,1)S(1)}, bf16[768,128]{1,0:T(8,128)(2,1)S(1)}, u32[]{:S(2)}, u32[]{:S(2)}) %collective-permute-start.14) | collective-permute-done | bytes 196640 | tf_op jit(solution)/shard_map/ppermute | solution.py:83
  43.0 1.7 %attend.1 = (bf16[144,128]{1,0:T(8,128)(2,1)S(1)}, bf16[144,128]{1,0:T(8,128)(2,1)S(1)}, bf16[144,128]{1,0:T(8,128)(2,1)S(1)}, bf16[144,128]{1,0:T(8,128)(2,1)S(1)}) custom-call(bf16[768,128]{1,0:T(8,128)(2,1)S(1)} %get-tuple-element.48.refs_0_, bf16[768,128]{1,0:T(8,128)(2,1)S(1)} %collective-permute-done.14.refs_1_, ...), custom_call_target="tpu_custom_call" | custom-call | tf_op jit(solution)/shard_map/attend/pallas_call | solution.py:37
  44.8 0.4 collective-permute-start.15
  45.1 0.6 %collective-permute-start.16 = (bf16[144,128]{1,0:T(8,128)(2,1)S(1)}, bf16[144,128]{1,0:T(8,128)(2,1)S(1)}, u32[]{:S(2)}, u32[]{:S(2)}) collective-permute-start(bf16[144,128]{1,0:T(8,128)(2,1)S(1)} %get-tuple-element.60), channel_id=1, source_target_pairs={{0,16},{1,17},{2,18},{3,19},{4,20},{5,21},{6,22},{7,23},{8,24},{9,... | collective-permute-start | bytes 110600 | tf_op jit(solution)/shard_map/ppermute | solution.py:83
  45.7 2.6 %collective-permute-start.17 = (bf16[144,128]{1,0:T(8,128)(2,1)S(1)}, bf16[144,128]{1,0:T(8,128)(2,1)S(1)}, u32[]{:S(2)}, u32[]{:S(2)}) collective-permute-start(bf16[144,128]{1,0:T(8,128)(2,1)S(1)} %get-tuple-element.61), channel_id=1, source_target_pairs={{0,24},{1,25},{2,26},{3,27},{4,28},{5,29},{6,30},{7,31},{8,16},{9,... | collective-permute-start | bytes 110600 | tf_op jit(solution)/shard_map/ppermute | solution.py:83
  48.3 0.6 collective-permute-done.15.refs_1_
  48.9 0.5 collective-permute-done.16.refs_2_
  49.5 1.1 %collective-permute-done.17.refs_3_ = bf16[144,128]{1,0:T(8,128)(2,1)S(1)} collective-permute-done((bf16[144,128]{1,0:T(8,128)(2,1)S(1)}, bf16[144,128]{1,0:T(8,128)(2,1)S(1)}, u32[]{:S(2)}, u32[]{:S(2)}) %collective-permute-start.17) | collective-permute-done | bytes 36896 | tf_op jit(solution)/shard_map/ppermute | solution.py:83
  50.6 0.1 finish.1.refs_4_
  50.7 2.2 %collective-permute-start.24 = (bf16[128,128]{1,0:T(8,128)(2,1)S(1)}, bf16[128,128]{1,0:T(8,128)(2,1)S(1)}, u32[]{:S(2)}, u32[]{:S(2)}) collective-permute-start(bf16[128,128]{1,0:T(8,128)(2,1)S(1)} %finish.1.refs_4_), channel_id=1, source_target_pairs={{0,6},{1,7},{2,4},{3,5},{4,2},{5,3},{6,0},{7,1},{8,14},{9,15},{10,... | collective-permute-start | bytes 98312 | tf_op jit(solution)/shard_map/ppermute | solution.py:86
  52.9 1.1 %collective-permute-start.23 = (bf16[128,128]{1,0:T(8,128)(2,1)S(1)}, bf16[128,128]{1,0:T(8,128)(2,1)S(1)}, u32[]{:S(2)}, u32[]{:S(2)}) collective-permute-start(bf16[128,128]{1,0:T(8,128)(2,1)S(1)} %finish.1.refs_4_), channel_id=1, source_target_pairs={{0,4},{1,5},{2,6},{3,7},{4,0},{5,1},{6,2},{7,3},{8,12},{9,13},{10,... | collective-permute-start | bytes 98312 | tf_op jit(solution)/shard_map/ppermute | solution.py:86
  54.0 1.2 %collective-permute-start.22 = (bf16[128,128]{1,0:T(8,128)(2,1)S(1)}, bf16[128,128]{1,0:T(8,128)(2,1)S(1)}, u32[]{:S(2)}, u32[]{:S(2)}) collective-permute-start(bf16[128,128]{1,0:T(8,128)(2,1)S(1)} %finish.1.refs_4_), channel_id=1, source_target_pairs={{0,2},{1,3},{2,0},{3,1},{4,6},{5,7},{6,4},{7,5},{8,10},{9,11},{10,... | collective-permute-start | bytes 98312 | tf_op jit(solution)/shard_map/ppermute | solution.py:86
  55.2 0.6 collective-permute-start.21
  55.8 0.7 %collective-permute-done.24.refs_7_ = bf16[128,128]{1,0:T(8,128)(2,1)S(1)} collective-permute-done((bf16[128,128]{1,0:T(8,128)(2,1)S(1)}, bf16[128,128]{1,0:T(8,128)(2,1)S(1)}, u32[]{:S(2)}, u32[]{:S(2)}) %collective-permute-start.24) | collective-permute-done | bytes 32800 | tf_op jit(solution)/shard_map/ppermute | solution.py:86
  56.5 1.5 %collective-permute-done.23.refs_6_ = bf16[128,128]{1,0:T(8,128)(2,1)S(1)} collective-permute-done((bf16[128,128]{1,0:T(8,128)(2,1)S(1)}, bf16[128,128]{1,0:T(8,128)(2,1)S(1)}, u32[]{:S(2)}, u32[]{:S(2)}) %collective-permute-start.23) | collective-permute-done | bytes 32800 | tf_op jit(solution)/shard_map/ppermute | solution.py:86
  58.1 0.5 collective-permute-start.26
  58.6 0.7 %collective-permute-done.27.refs_10_ = bf16[128,128]{1,0:T(8,128)(2,1)S(1)} collective-permute-done((bf16[128,128]{1,0:T(8,128)(2,1)S(1)}, bf16[128,128]{1,0:T(8,128)(2,1)S(1)}, u32[]{:S(2)}, u32[]{:S(2)}) %collective-permute-start.27) | collective-permute-done | bytes 32800 | tf_op jit(solution)/shard_map/ppermute | solution.py:80
  59.3 0.2 collective-permute-done.26.refs_9_
  59.4 1.1 %output.1 = (bf16[128,768]{1,0:T(8,128)(2,1)}, bf16[128,128]{1,0:T(8,128)(2,1)}) custom-call(bf16[128,768]{1,0:T(8,128)(2,1)S(1)} %copy-done.1, f32[1,768]{1,0:T(1,128)S(1)} %reshape.13.refs_1_, bf16[128,128]{1,0:T(8,128)(2,1)S(1)} %get-tuple-element.74.refs_2_, bf16[128,128]{1,0:T(8,128)(2,1)S(1)} %collective-permute-done.21.refs_3_, ...), custom_call_target="tpu_custom_call" | custom-call | tf_op jit(solution)/shard_map/output/pallas_call | solution.py:37
  (31 shorter events, 0.2 us)
Async XLA Ops:
  0.6 19.9 %collective-permute-start.5 = (bf16[256,768]{1,0:T(8,128)(2,1)}, bf16[256,768]{1,0:T(8,128)(2,1)S(1)}, u32[]{:S(2)}, u32[]{:S(2)}) collective-permute-start(bf16[256,768]{1,0:T(8,128)(2,1)} %refs_12_.1), channel_id=1, source_target_pairs={{0,16},{1,17},{2,18},{3,19},{4,20},{5,21},{6,22},{7,23},{8,24},{9,... | collective-permute-start | bytes 1179656 | tf_op jit(solution)/shard_map/ppermute | solution.py:83
  3.7 18.2 %collective-permute-start.4 = (bf16[256,768]{1,0:T(8,128)(2,1)}, bf16[256,768]{1,0:T(8,128)(2,1)S(1)}, u32[]{:S(2)}, u32[]{:S(2)}) collective-permute-start(bf16[256,768]{1,0:T(8,128)(2,1)} %refs_12_.1), channel_id=1, source_target_pairs={{0,8},{1,9},{2,10},{3,11},{4,12},{5,13},{6,14},{7,15},{8,0},{9,1},... | collective-permute-start | bytes 1179656 | tf_op jit(solution)/shard_map/ppermute | solution.py:83
  5.2 13.3 %collective-permute-start = (bf16[128,768]{1,0:T(8,128)(2,1)}, bf16[128,768]{1,0:T(8,128)(2,1)S(1)}, u32[]{:S(2)}, u32[]{:S(2)}) collective-permute-start(bf16[128,768]{1,0:T(8,128)(2,1)} %refs_0_.5), channel_id=1, source_target_pairs={{0,6},{1,7},{2,12},{3,13},{4,18},{5,19},{6,24},{7,25},{8,4},{9,5},... | collective-permute-start | bytes 589832 | tf_op jit(solution)/shard_map/ppermute | solution.py:89
  8.8 9.7 %collective-permute-start.1 = (bf16[128,768]{1,0:T(8,128)(2,1)}, bf16[128,768]{1,0:T(8,128)(2,1)S(1)}, u32[]{:S(2)}, u32[]{:S(2)}) collective-permute-start(bf16[128,768]{1,0:T(8,128)(2,1)} %refs_0_.5), channel_id=1, source_target_pairs={{0,1},{1,0},{2,10},{3,11},{4,20},{5,21},{6,30},{7,31},{8,2},{9,3},... | collective-permute-start | bytes 589832 | tf_op jit(solution)/shard_map/ppermute | solution.py:89
  18.5 7.8 %collective-permute-start.2 = (bf16[128,768]{1,0:T(8,128)(2,1)S(1)}, bf16[128,768]{1,0:T(8,128)(2,1)S(1)}, u32[]{:S(2)}, u32[]{:S(2)}) collective-permute-start(bf16[128,768]{1,0:T(8,128)(2,1)S(1)} %collective-permute-done.refs_0_), channel_id=1, source_target_pairs={{0,2},{1,3},{2,0},{3,1},{4,6},{5,7},{6,4},{7,5},{8,10},{9,11},{10,... | collective-permute-start | bytes 589832 | tf_op jit(solution)/shard_map/ppermute | solution.py:86
  18.5 10.0 %collective-permute-start.3 = (bf16[128,768]{1,0:T(8,128)(2,1)S(1)}, bf16[128,768]{1,0:T(8,128)(2,1)S(1)}, u32[]{:S(2)}, u32[]{:S(2)}) collective-permute-start(bf16[128,768]{1,0:T(8,128)(2,1)S(1)} %collective-permute-done.1.refs_1_), channel_id=1, source_target_pairs={{0,2},{1,3},{2,0},{3,1},{4,6},{5,7},{6,4},{7,5},{8,10},{9,11},{10,... | collective-permute-start | bytes 589832 | tf_op jit(solution)/shard_map/ppermute | solution.py:86
  20.5 7.9 %collective-permute-start.6 = (bf16[128,768]{1,0:T(8,128)(2,1)S(1)}, bf16[128,768]{1,0:T(8,128)(2,1)S(1)}, u32[]{:S(2)}, u32[]{:S(2)}) collective-permute-start(bf16[128,768]{1,0:T(8,128)(2,1)S(1)} %slice.8), channel_id=1, source_target_pairs={{0,8},{1,9},{2,10},{3,11},{4,12},{5,13},{6,14},{7,15},{8,0},{9,1},... | collective-permute-start | bytes 589832 | tf_op jit(solution)/shard_map/ppermute | solution.py:83
  21.8 7.1 %copy-start.3 = (f32[768]{0:T(1024)S(1)}, f32[768]{0:T(1024)}, u32[]{:S(2)}) copy-start(f32[768]{0:T(1024)} %param.20) | copy-start | bytes 9220
  21.8 6.6 %collective-permute-start.7 = (bf16[128,768]{1,0:T(8,128)(2,1)S(1)}, bf16[128,768]{1,0:T(8,128)(2,1)S(1)}, u32[]{:S(2)}, u32[]{:S(2)}) collective-permute-start(bf16[128,768]{1,0:T(8,128)(2,1)S(1)} %slice.9), channel_id=1, source_target_pairs={{0,16},{1,17},{2,18},{3,19},{4,20},{5,21},{6,22},{7,23},{8,24},{9,... | collective-permute-start | bytes 589832 | tf_op jit(solution)/shard_map/ppermute | solution.py:83
  24.4 4.6 %collective-permute-start.10 = (bf16[128,768]{1,0:T(8,128)(2,1)S(1)}, bf16[128,768]{1,0:T(8,128)(2,1)S(1)}, u32[]{:S(2)}, u32[]{:S(2)}) collective-permute-start(bf16[128,768]{1,0:T(8,128)(2,1)S(1)} %collective-permute-done.refs_0_), channel_id=1, source_target_pairs={{0,1},{1,0},{2,3},{3,2},{4,5},{5,4},{6,7},{7,6},{8,9},{9,8},{10,11... | collective-permute-start | bytes 589832 | tf_op jit(solution)/shard_map/ppermute | solution.py:80
  26.3 2.7 %collective-permute-start.11 = (bf16[128,768]{1,0:T(8,128)(2,1)S(1)}, bf16[128,768]{1,0:T(8,128)(2,1)S(1)}, u32[]{:S(2)}, u32[]{:S(2)}) collective-permute-start(bf16[128,768]{1,0:T(8,128)(2,1)S(1)} %collective-permute-done.1.refs_1_), channel_id=1, source_target_pairs={{0,1},{1,0},{2,3},{3,2},{4,5},{5,4},{6,7},{7,6},{8,9},{9,8},{10,11... | collective-permute-start | bytes 589832 | tf_op jit(solution)/shard_map/ppermute | solution.py:80
  28.4 1.4 %collective-permute-start.8 = (bf16[128,768]{1,0:T(8,128)(2,1)S(1)}, bf16[128,768]{1,0:T(8,128)(2,1)S(1)}, u32[]{:S(2)}, u32[]{:S(2)}) collective-permute-start(bf16[128,768]{1,0:T(8,128)(2,1)S(1)} %collective-permute-done.2.refs_0_), channel_id=1, source_target_pairs={{0,1},{1,0},{2,3},{3,2},{4,5},{5,4},{6,7},{7,6},{8,9},{9,8},{10,11... | collective-permute-start | bytes 589832 | tf_op jit(solution)/shard_map/ppermute | solution.py:80
  28.5 1.7 %collective-permute-start.9 = (bf16[128,768]{1,0:T(8,128)(2,1)S(1)}, bf16[128,768]{1,0:T(8,128)(2,1)S(1)}, u32[]{:S(2)}, u32[]{:S(2)}) collective-permute-start(bf16[128,768]{1,0:T(8,128)(2,1)S(1)} %collective-permute-done.3.refs_1_), channel_id=1, source_target_pairs={{0,1},{1,0},{2,3},{3,2},{4,5},{5,4},{6,7},{7,6},{8,9},{9,8},{10,11... | collective-permute-start | bytes 589832 | tf_op jit(solution)/shard_map/ppermute | solution.py:80
  29.6 4.8 %copy-start = (bf16[256,768]{1,0:T(8,128)(2,1)S(1)}, bf16[256,768]{1,0:T(8,128)(2,1)}, u32[]{:S(2)}) copy-start(bf16[256,768]{1,0:T(8,128)(2,1)} %refs_12_.1) | copy-start | bytes 1179652
  29.6 4.8 %copy-start.2 = (bf16[128,768]{1,0:T(8,128)(2,1)S(1)}, bf16[128,768]{1,0:T(8,128)(2,1)}, u32[]{:S(2)}) copy-start(bf16[128,768]{1,0:T(8,128)(2,1)} %refs_0_.4) | copy-start | bytes 589828
  30.8 8.7 %collective-permute-start.12 = (bf16[768,128]{1,0:T(8,128)(2,1)S(1)}, bf16[768,128]{1,0:T(8,128)(2,1)S(1)}, u32[]{:S(2)}, u32[]{:S(2)}) collective-permute-start(bf16[768,128]{1,0:T(8,128)(2,1)S(1)} %get-tuple-element.49), channel_id=1, source_target_pairs={{0,24},{1,25},{2,26},{3,27},{4,28},{5,29},{6,30},{7,31},{8,16},{9,... | collective-permute-start | bytes 589832 | tf_op jit(solution)/shard_map/ppermute | solution.py:83
  30.9 11.3 %collective-permute-start.13 = (bf16[768,128]{1,0:T(8,128)(2,1)S(1)}, bf16[768,128]{1,0:T(8,128)(2,1)S(1)}, u32[]{:S(2)}, u32[]{:S(2)}) collective-permute-start(bf16[768,128]{1,0:T(8,128)(2,1)S(1)} %get-tuple-element.50), channel_id=1, source_target_pairs={{0,16},{1,17},{2,18},{3,19},{4,20},{5,21},{6,22},{7,23},{8,24},{9,... | collective-permute-start | bytes 589832 | tf_op jit(solution)/shard_map/ppermute | solution.py:83
  32.6 10.4 %collective-permute-start.14 = (bf16[768,128]{1,0:T(8,128)(2,1)S(1)}, bf16[768,128]{1,0:T(8,128)(2,1)S(1)}, u32[]{:S(2)}, u32[]{:S(2)}) collective-permute-start(bf16[768,128]{1,0:T(8,128)(2,1)S(1)} %get-tuple-element.51), channel_id=1, source_target_pairs={{0,8},{1,9},{2,10},{3,11},{4,12},{5,13},{6,14},{7,15},{8,0},{9,1},... | collective-permute-start | bytes 589832 | tf_op jit(solution)/shard_map/ppermute | solution.py:83
  35.1 10.6 %collective-permute-start.18 = (bf16[256,128]{1,0:T(8,128)(2,1)S(1)}, bf16[256,128]{1,0:T(8,128)(2,1)S(1)}, u32[]{:S(2)}, u32[]{:S(2)}) collective-permute-start(bf16[256,128]{1,0:T(8,128)(2,1)S(1)} %get-tuple-element.67), channel_id=1, source_target_pairs={{0,2},{1,3},{2,0},{3,1},{4,6},{5,7},{6,4},{7,5},{8,10},{9,11},{10,... | collective-permute-start | bytes 196616 | tf_op jit(solution)/shard_map/ppermute | solution.py:86
  35.5 12.9 %collective-permute-start.19 = (bf16[256,128]{1,0:T(8,128)(2,1)S(1)}, bf16[256,128]{1,0:T(8,128)(2,1)S(1)}, u32[]{:S(2)}, u32[]{:S(2)}) collective-permute-start(bf16[256,128]{1,0:T(8,128)(2,1)S(1)} %get-tuple-element.68), channel_id=1, source_target_pairs={{0,4},{1,5},{2,6},{3,7},{4,0},{5,1},{6,2},{7,3},{8,12},{9,13},{10,... | collective-permute-start | bytes 196616 | tf_op jit(solution)/shard_map/ppermute | solution.py:86
  39.6 8.8 %collective-permute-start.20 = (bf16[256,128]{1,0:T(8,128)(2,1)S(1)}, bf16[256,128]{1,0:T(8,128)(2,1)S(1)}, u32[]{:S(2)}, u32[]{:S(2)}) collective-permute-start(bf16[256,128]{1,0:T(8,128)(2,1)S(1)} %get-tuple-element.69), channel_id=1, source_target_pairs={{0,6},{1,7},{2,4},{3,5},{4,2},{5,3},{6,0},{7,1},{8,14},{9,15},{10,... | collective-permute-start | bytes 196616 | tf_op jit(solution)/shard_map/ppermute | solution.py:86
  43.0 16.4 %copy-start.1 = (bf16[128,768]{1,0:T(8,128)(2,1)S(1)}, bf16[128,768]{1,0:T(8,128)(2,1)}, u32[]{:S(2)}) copy-start(bf16[128,768]{1,0:T(8,128)(2,1)} %refs_0_.5) | copy-start | bytes 589828
  44.8 4.2 %collective-permute-start.15 = (bf16[144,128]{1,0:T(8,128)(2,1)S(1)}, bf16[144,128]{1,0:T(8,128)(2,1)S(1)}, u32[]{:S(2)}, u32[]{:S(2)}) collective-permute-start(bf16[144,128]{1,0:T(8,128)(2,1)S(1)} %get-tuple-element.59), channel_id=1, source_target_pairs={{0,8},{1,9},{2,10},{3,11},{4,12},{5,13},{6,14},{7,15},{8,0},{9,1},... | collective-permute-start | bytes 110600 | tf_op jit(solution)/shard_map/ppermute | solution.py:83
  45.1 4.3 %collective-permute-start.16 = (bf16[144,128]{1,0:T(8,128)(2,1)S(1)}, bf16[144,128]{1,0:T(8,128)(2,1)S(1)}, u32[]{:S(2)}, u32[]{:S(2)}) collective-permute-start(bf16[144,128]{1,0:T(8,128)(2,1)S(1)} %get-tuple-element.60), channel_id=1, source_target_pairs={{0,16},{1,17},{2,18},{3,19},{4,20},{5,21},{6,22},{7,23},{8,24},{9,... | collective-permute-start | bytes 110600 | tf_op jit(solution)/shard_map/ppermute | solution.py:83
  45.7 4.9 %collective-permute-start.17 = (bf16[144,128]{1,0:T(8,128)(2,1)S(1)}, bf16[144,128]{1,0:T(8,128)(2,1)S(1)}, u32[]{:S(2)}, u32[]{:S(2)}) collective-permute-start(bf16[144,128]{1,0:T(8,128)(2,1)S(1)} %get-tuple-element.61), channel_id=1, source_target_pairs={{0,24},{1,25},{2,26},{3,27},{4,28},{5,29},{6,30},{7,31},{8,16},{9,... | collective-permute-start | bytes 110600 | tf_op jit(solution)/shard_map/ppermute | solution.py:83
  50.7 5.8 %collective-permute-start.24 = (bf16[128,128]{1,0:T(8,128)(2,1)S(1)}, bf16[128,128]{1,0:T(8,128)(2,1)S(1)}, u32[]{:S(2)}, u32[]{:S(2)}) collective-permute-start(bf16[128,128]{1,0:T(8,128)(2,1)S(1)} %finish.1.refs_4_), channel_id=1, source_target_pairs={{0,6},{1,7},{2,4},{3,5},{4,2},{5,3},{6,0},{7,1},{8,14},{9,15},{10,... | collective-permute-start | bytes 98312 | tf_op jit(solution)/shard_map/ppermute | solution.py:86
  52.9 5.2 %collective-permute-start.23 = (bf16[128,128]{1,0:T(8,128)(2,1)S(1)}, bf16[128,128]{1,0:T(8,128)(2,1)S(1)}, u32[]{:S(2)}, u32[]{:S(2)}) collective-permute-start(bf16[128,128]{1,0:T(8,128)(2,1)S(1)} %finish.1.refs_4_), channel_id=1, source_target_pairs={{0,4},{1,5},{2,6},{3,7},{4,0},{5,1},{6,2},{7,3},{8,12},{9,13},{10,... | collective-permute-start | bytes 98312 | tf_op jit(solution)/shard_map/ppermute | solution.py:86
  54.0 4.1 %collective-permute-start.22 = (bf16[128,128]{1,0:T(8,128)(2,1)S(1)}, bf16[128,128]{1,0:T(8,128)(2,1)S(1)}, u32[]{:S(2)}, u32[]{:S(2)}) collective-permute-start(bf16[128,128]{1,0:T(8,128)(2,1)S(1)} %finish.1.refs_4_), channel_id=1, source_target_pairs={{0,2},{1,3},{2,0},{3,1},{4,6},{5,7},{6,4},{7,5},{8,10},{9,11},{10,... | collective-permute-start | bytes 98312 | tf_op jit(solution)/shard_map/ppermute | solution.py:86
  55.2 3.4 %collective-permute-start.25 = (bf16[128,128]{1,0:T(8,128)(2,1)S(1)}, bf16[128,128]{1,0:T(8,128)(2,1)S(1)}, u32[]{:S(2)}, u32[]{:S(2)}) collective-permute-start(bf16[128,128]{1,0:T(8,128)(2,1)S(1)} %finish.1.refs_4_), channel_id=1, source_target_pairs={{0,1},{1,0},{2,3},{3,2},{4,5},{5,4},{6,7},{7,6},{8,9},{9,8},{10,11... | collective-permute-start | bytes 98312 | tf_op jit(solution)/shard_map/ppermute | solution.py:80
  55.2 3.4 %collective-permute-start.21 = (bf16[128,128]{1,0:T(8,128)(2,1)S(1)}, bf16[128,128]{1,0:T(8,128)(2,1)S(1)}, u32[]{:S(2)}, u32[]{:S(2)}) collective-permute-start(bf16[128,128]{1,0:T(8,128)(2,1)S(1)} %get-tuple-element.75), channel_id=1, source_target_pairs={{0,1},{1,0},{2,3},{3,2},{4,5},{5,4},{6,7},{7,6},{8,9},{9,8},{10,11... | collective-permute-start | bytes 98312 | tf_op jit(solution)/shard_map/ppermute | solution.py:80
  56.5 2.1 %collective-permute-start.28 = (bf16[128,128]{1,0:T(8,128)(2,1)S(1)}, bf16[128,128]{1,0:T(8,128)(2,1)S(1)}, u32[]{:S(2)}, u32[]{:S(2)}) collective-permute-start(bf16[128,128]{1,0:T(8,128)(2,1)S(1)} %collective-permute-done.24.refs_7_), channel_id=1, source_target_pairs={{0,1},{1,0},{2,3},{3,2},{4,5},{5,4},{6,7},{7,6},{8,9},{9,8},{10,11... | collective-permute-start | bytes 98312 | tf_op jit(solution)/shard_map/ppermute | solution.py:80
  58.1 1.2 %collective-permute-start.27 = (bf16[128,128]{1,0:T(8,128)(2,1)S(1)}, bf16[128,128]{1,0:T(8,128)(2,1)S(1)}, u32[]{:S(2)}, u32[]{:S(2)}) collective-permute-start(bf16[128,128]{1,0:T(8,128)(2,1)S(1)} %collective-permute-done.23.refs_6_), channel_id=1, source_target_pairs={{0,1},{1,0},{2,3},{3,2},{4,5},{5,4},{6,7},{7,6},{8,9},{9,8},{10,11... | collective-permute-start | bytes 98312 | tf_op jit(solution)/shard_map/ppermute | solution.py:80
  58.1 1.4 %collective-permute-start.26 = (bf16[128,128]{1,0:T(8,128)(2,1)S(1)}, bf16[128,128]{1,0:T(8,128)(2,1)S(1)}, u32[]{:S(2)}, u32[]{:S(2)}) collective-permute-start(bf16[128,128]{1,0:T(8,128)(2,1)S(1)} %collective-permute-done.22.refs_5_), channel_id=1, source_target_pairs={{0,1},{1,0},{2,3},{3,2},{4,5},{5,4},{6,7},{7,6},{8,9},{9,8},{10,11... | collective-permute-start | bytes 98312 | tf_op jit(solution)/shard_map/ppermute | solution.py:80

commit v6 on v5

--- a/solution.py
+++ b/solution.py
@@ -286,41 +286,42 @@
             [jax.ShapeDtypeStruct((T + tail, H), bf16)] * R,
             [pltpu.VMEM((R * T, H), bf16), pltpu.VMEM((R, T + tail, H), bf16)],
         )
-        sums = [sums[0]] + [over_row(sums[s], s) for s in range(1, R)]
+        sums = [sums[0]] + [over_row(sums[s], s) for s in far_first]
 
         sums, grads = lax.optimization_barrier((sums, grads))
 
-        def join(*refs):
-            own_ref, away_ref = refs[R:]
-            both_heads = sum(ref[...].astype(f32) for ref in refs[:R])
-            own_ref[...] = both_heads[:T].astype(bf16)
-            away_ref[...] = both_heads[T:].astype(bf16)
-
-        grad_own, grad_away = call(join, "join", grads, [jax.ShapeDtypeStruct((T, H), bf16)] * 2)
-        grad_away = across_chip(grad_away)
-
         def finish(*refs):
-            sum_refs, out = refs[:R], refs[R]
+            sum_refs, grad_refs = refs[:R], refs[R : 2 * R]
+            out, grad_own_ref, crossing_ref = refs[2 * R :]
             numerators = sum(ref[:T, :].astype(f32) for ref in sum_refs)
             row = sum(ref[T : T + 1, :].astype(f32) + ref[T + 1 : T + 2, :].astype(f32) for ref in sum_refs)
             eye = lax.broadcasted_iota(jnp.int32, (T, H), 0) == lax.broadcasted_iota(
                 jnp.int32, (T, H), 1
             )
             totals = jnp.sum(jnp.where(eye, row, 0.0), axis=1, keepdims=True)
-            out[...] = (numerators / totals).astype(bf16)
-
-        (attention,) = call(finish, "finish", sums, [jax.ShapeDtypeStruct((T, H), bf16)])
+            attention = (numerators / totals).astype(bf16)
+            both_heads = sum(ref[...].astype(f32) for ref in grad_refs)
+            out[...] = attention
+            grad_own_ref[...] = both_heads[:T].astype(bf16)
+            crossing_ref[:T] = attention
+            crossing_ref[T:] = both_heads[T:].astype(bf16)
+
+        block = jax.ShapeDtypeStruct((T, H), bf16)
+        attention, grad_own, crossing = call(
+            finish, "finish", (*sums, *grads), [block, block, jax.ShapeDtypeStruct((2 * T, H), bf16)]
+        )
+        crossing = across_chip(crossing)
         heads = [attention] + [over_z(attention, m) for m in range(1, R)]
-        heads_other = [across_chip(x) for x in heads]
+        heads_other = [crossing] + [across_chip(x) for x in heads[1:]]
 
         def output(*refs):
-            tokens_ref, gate_ref, own_ref, away_ref = refs[:4]
-            mine_refs, other_refs, rows_refs = (refs[i * R + 4 : (i + 1) * R + 4] for i in range(3))
-            layer_ref, grad_ref, held = refs[3 * R + 4 :]
+            tokens_ref, gate_ref, own_ref = refs[:3]
+            mine_refs, other_refs, rows_refs = (refs[i * R + 3 : (i + 1) * R + 3] for i in range(3))
+            layer_ref, grad_ref, held = refs[3 * R + 3 :]
             f, z, q = here()
-            grad_ref[...] = (own_ref[...].astype(f32) + away_ref[...].astype(f32)).astype(bf16)
+            grad_ref[...] = (own_ref[...].astype(f32) + other_refs[0][T:].astype(f32)).astype(bf16)
             for m in range(R):
-                own, away = mine_refs[m][...], other_refs[m][...]
+                own, away = mine_refs[m][...], other_refs[m][:T]
                 held[z ^ m, :, :H] = jnp.where(q == 0, own, away)
                 held[z ^ m, :, H:] = jnp.where(q == 0, away, own)
             branch = sum(dot(held[f ^ s], rows_refs[s][...]) for s in range(R))
@@ -329,7 +330,7 @@
         layer_out, attention_cotangent = call(
             output,
             "output",
-            (tokens, out_gate, grad_own, grad_away, *heads, *heads_other, *out_rows),
+            (tokens, out_gate, grad_own, *heads, *heads_other, *out_rows),
             [jax.ShapeDtypeStruct((T, wide_out), bf16), jax.ShapeDtypeStruct((T, H), bf16)],
             [pltpu.VMEM((R, T, k * H), bf16)],
         )

time: 60.7 us -> 60.5 us (level)
  starting transfers between devices: 26.7 us -> 25.8 us
  waiting for transfers between devices: 25.6 us -> 26.3 us
    ppermute x9 -> x8, starting transfers between devices: 1.67 us -> 0.77 us  [across_chip(): return lax.ppermute(x, both, route(lambda r, z, q: (r, z, q ^ 1)))]
    ppermute x9 -> x8, waiting for transfers between devices: 1.41 us -> 1.58 us  [across_chip(): return lax.ppermute(x, both, route(lambda r, z, q: (r, z, q ^ 1)))]
    pallas_call x8 -> x7, Pallas kernels: 7.37 us -> 7.34 us  [call(): pl.pallas_call(fetch if far else kernel, out_shape=list(outs), in_specs=[...]
  transfers between devices with their start and end apart: 29 -> 28, of which waited for: 15 -> 15; matrix products, arithmetic and copies ran while one was open for 0% -> 0% of each run, Pallas kernels for 9% -> 9%
where the time goes in v6:
time: 60.5 us; the launch traced here: 60.3 us
  waiting for transfers between devices  26.3 us (43%)
  starting transfers between devices  25.8 us (43%)
  Pallas kernels  7.34 us (12%)
  between operations  0.79 us (1%)
    ppermute x10, starting transfers between devices, over_row(): return lax.ppermute(x, both, route(lambda r, z, q: (r ^ s, z, q)))  13 us
    ppermute x2, waiting for transfers between devices, turned(): lax.ppermute(x, both, route(lambda r, z, q: (z, r ^ z ^ d, q ^ (r == z ==...  9.7 us
    ppermute x8, starting transfers between devices, over_z(): return lax.ppermute(x, both, route(lambda r, z, q: (r, z ^ m, q)))  8.39 us
    ppermute x10, waiting for transfers between devices, over_row(): return lax.ppermute(x, both, route(lambda r, z, q: (r ^ s, z, q)))  8.22 us
    pallas_call x7, Pallas kernels, call(): pl.pallas_call(fetch if far else kernel, out_shape=list(outs), in_specs=[...  7.34 us
    ppermute x8, waiting for transfers between devices, over_z(): return lax.ppermute(x, both, route(lambda r, z, q: (r, z ^ m, q)))  6.85 us
    ppermute x2, starting transfers between devices, turned(): lax.ppermute(x, both, route(lambda r, z, q: (z, r ^ z ^ d, q ^ (r == z ==...  3.6 us
    ppermute x8, waiting for transfers between devices, across_chip(): return lax.ppermute(x, both, route(lambda r, z, q: (r, z, q ^ 1)))  1.58 us
  transfers between devices with their start and end apart: 28, of which 15 were waited for; matrix products, arithmetic and copies ran while one was open for 0% of the time, Pallas kernels for 9%

profile of v6, /device:TPU:0, one launch (start us, length us, event | category | flops | bytes accessed | tf_op | source)
XLA Modules:
  0.0 60.3 jit_solution(18243745712718507218)
XLA Ops:
  0.6 3.0 %collective-permute-start.5 = (bf16[256,768]{1,0:T(8,128)(2,1)}, bf16[256,768]{1,0:T(8,128)(2,1)S(1)}, u32[]{:S(2)}, u32[]{:S(2)}) collective-permute-start(bf16[256,768]{1,0:T(8,128)(2,1)} %refs_11_.1), channel_id=1, source_target_pairs={{0,16},{1,17},{2,18},{3,19},{4,20},{5,21},{6,22},{7,23},{8,24},{9,... | collective-permute-start | bytes 1179656 | tf_op jit(solution)/shard_map/ppermute | solution.py:83
  3.7 1.5 %collective-permute-start.4 = (bf16[256,768]{1,0:T(8,128)(2,1)}, bf16[256,768]{1,0:T(8,128)(2,1)S(1)}, u32[]{:S(2)}, u32[]{:S(2)}) collective-permute-start(bf16[256,768]{1,0:T(8,128)(2,1)} %refs_11_.1), channel_id=1, source_target_pairs={{0,8},{1,9},{2,10},{3,11},{4,12},{5,13},{6,14},{7,15},{8,0},{9,1},... | collective-permute-start | bytes 1179656 | tf_op jit(solution)/shard_map/ppermute | solution.py:83
  5.2 3.6 %collective-permute-start = (bf16[128,768]{1,0:T(8,128)(2,1)}, bf16[128,768]{1,0:T(8,128)(2,1)S(1)}, u32[]{:S(2)}, u32[]{:S(2)}) collective-permute-start(bf16[128,768]{1,0:T(8,128)(2,1)} %refs_0_.5), channel_id=1, source_target_pairs={{0,6},{1,7},{2,12},{3,13},{4,18},{5,19},{6,24},{7,25},{8,4},{9,5},... | collective-permute-start | bytes 589832 | tf_op jit(solution)/shard_map/ppermute | solution.py:89
  8.8 0.0 collective-permute-start.1
  8.8 9.7 %collective-permute-done.refs_0_ = bf16[128,768]{1,0:T(8,128)(2,1)S(1)} collective-permute-done((bf16[128,768]{1,0:T(8,128)(2,1)}, bf16[128,768]{1,0:T(8,128)(2,1)S(1)}, u32[]{:S(2)}, u32[]{:S(2)}) %collective-permute-start) | collective-permute-done | bytes 196640 | tf_op jit(solution)/shard_map/ppermute | solution.py:89
  18.5 0.0 collective-permute-done.1.refs_1_
  18.5 2.0 %collective-permute-start.3 = (bf16[128,768]{1,0:T(8,128)(2,1)S(1)}, bf16[128,768]{1,0:T(8,128)(2,1)S(1)}, u32[]{:S(2)}, u32[]{:S(2)}) collective-permute-start(bf16[128,768]{1,0:T(8,128)(2,1)S(1)} %collective-permute-done.1.refs_1_), channel_id=1, source_target_pairs={{0,2},{1,3},{2,0},{3,1},{4,6},{5,7},{6,4},{7,5},{8,10},{9,11},{10,... | collective-permute-start | bytes 589832 | tf_op jit(solution)/shard_map/ppermute | solution.py:86
  20.5 1.3 %collective-permute-start.6 = (bf16[128,768]{1,0:T(8,128)(2,1)S(1)}, bf16[128,768]{1,0:T(8,128)(2,1)S(1)}, u32[]{:S(2)}, u32[]{:S(2)}) collective-permute-start(bf16[128,768]{1,0:T(8,128)(2,1)S(1)} %slice.8), channel_id=1, source_target_pairs={{0,8},{1,9},{2,10},{3,11},{4,12},{5,13},{6,14},{7,15},{8,0},{9,1},... | collective-permute-start | bytes 589832 | tf_op jit(solution)/shard_map/ppermute | solution.py:83
  21.8 0.0 copy-start.3
  21.8 0.1 collective-permute-start.7
  21.9 2.5 %prepare.1 = (bf16[128,2048]{1,0:T(8,128)(2,1)S(1)}, bf16[2048,256]{1,0:T(8,128)(2,1)S(1)}, bf16[1536,384]{1,0:T(8,128)(2,1)S(1)}, f32[2,128]{1,0:T(2,128)S(1)}) custom-call(bf16[2048,128]{1,0:T(8,128)(2,1)} %refs_0_.3, bf16[2048,128]{1,0:T(8,128)(2,1)} %refs_1_.1, bf16[1536,128]{1,0:T(8,128)(2,1)} %refs_2_.2, bf16[1536,128]{1,0:T(8,128)(2,1)} %refs_3_.1, ...), custom_call_target="tpu_custom_call" | custom-call | tf_op jit(solution)/shard_map/prepare/pallas_call | solution.py:37
  24.4 0.1 collective-permute-start.10
  24.5 1.8 %collective-permute-done.2.refs_0_ = bf16[128,768]{1,0:T(8,128)(2,1)S(1)} collective-permute-done((bf16[128,768]{1,0:T(8,128)(2,1)S(1)}, bf16[128,768]{1,0:T(8,128)(2,1)S(1)}, u32[]{:S(2)}, u32[]{:S(2)}) %collective-permute-start.2) | collective-permute-done | bytes 196640 | tf_op jit(solution)/shard_map/ppermute | solution.py:86
  26.3 2.1 %collective-permute-done.3.refs_1_ = bf16[128,768]{1,0:T(8,128)(2,1)S(1)} collective-permute-done((bf16[128,768]{1,0:T(8,128)(2,1)S(1)}, bf16[128,768]{1,0:T(8,128)(2,1)S(1)}, u32[]{:S(2)}, u32[]{:S(2)}) %collective-permute-start.3) | collective-permute-done | bytes 196640 | tf_op jit(solution)/shard_map/ppermute | solution.py:86
  28.5 0.5 collective-permute-start.9
  29.0 0.6 %project_direct.1.refs_4_ = bf16[256,384]{1,0:T(8,128)(2,1)S(1)} custom-call(bf16[128,768]{1,0:T(8,128)(2,1)S(1)} %collective-permute-done.refs_0_, bf16[128,768]{1,0:T(8,128)(2,1)S(1)} %collective-permute-done.1.refs_1_, bf16[128,768]{1,0:T(8,128)(2,1)S(1)} %collective-permute-done.10.refs_2_, bf16[128,768]{1,0:T(8,128)(2,1)S(1)} %collective-permute-done.11.refs_3_, ...), custom_call_target="tpu_custom_call" | custom-call | tf_op jit(solution)/shard_map/project_direct/pallas_call | solution.py:37
  29.6 0.0 copy-start
  29.6 0.0 copy-start.2
  29.6 0.3 collective-permute-done.8.refs_2_
  29.9 0.3 collective-permute-done.9.refs_3_
  30.2 0.6 %project.1 = (bf16[768,128]{1,0:T(8,128)(2,1)S(1)}, bf16[768,128]{1,0:T(8,128)(2,1)S(1)}, bf16[768,128]{1,0:T(8,128)(2,1)S(1)}, bf16[768,128]{1,0:T(8,128)(2,1)S(1)}) custom-call(bf16[128,768]{1,0:T(8,128)(2,1)S(1)} %collective-permute-done.2.refs_0_, bf16[128,768]{1,0:T(8,128)(2,1)S(1)} %collective-permute-done.3.refs_1_, ...), custom_call_target="tpu_custom_call" | custom-call | tf_op jit(solution)/shard_map/project/pallas_call | solution.py:37
  30.8 0.1 collective-permute-start.12
  30.9 1.7 %collective-permute-start.13 = (bf16[768,128]{1,0:T(8,128)(2,1)S(1)}, bf16[768,128]{1,0:T(8,128)(2,1)S(1)}, u32[]{:S(2)}, u32[]{:S(2)}) collective-permute-start(bf16[768,128]{1,0:T(8,128)(2,1)S(1)} %get-tuple-element.51), channel_id=1, source_target_pairs={{0,16},{1,17},{2,18},{3,19},{4,20},{5,21},{6,22},{7,23},{8,24},{9,... | collective-permute-start | bytes 589832 | tf_op jit(solution)/shard_map/ppermute | solution.py:83
  32.6 1.7 %collective-permute-start.14 = (bf16[768,128]{1,0:T(8,128)(2,1)S(1)}, bf16[768,128]{1,0:T(8,128)(2,1)S(1)}, u32[]{:S(2)}, u32[]{:S(2)}) collective-permute-start(bf16[768,128]{1,0:T(8,128)(2,1)S(1)} %get-tuple-element.52), channel_id=1, source_target_pairs={{0,8},{1,9},{2,10},{3,11},{4,12},{5,13},{6,14},{7,15},{8,0},{9,1},... | collective-permute-start | bytes 589832 | tf_op jit(solution)/shard_map/ppermute | solution.py:83
  34.4 0.7 %gradient.1 = (bf16[256,128]{1,0:T(8,128)(2,1)S(1)}, bf16[256,128]{1,0:T(8,128)(2,1)S(1)}, bf16[256,128]{1,0:T(8,128)(2,1)S(1)}, bf16[256,128]{1,0:T(8,128)(2,1)S(1)}) custom-call(bf16[128,768]{1,0:T(8,128)(2,1)S(1)} %copy-done.2, f32[1,768]{1,0:T(1,128)S(1)} %reshape.13.refs_1_, bf16[256,768]{1,0:T(8,128)(2,1)S(1)} %copy-done, ...), custom_call_target="tpu_custom_call" | custom-call | tf_op jit(solution)/shard_map/gradient/pallas_call | solution.py:37
  35.1 0.4 collective-permute-start.18
  35.5 1.0 %collective-permute-start.19 = (bf16[256,128]{1,0:T(8,128)(2,1)S(1)}, bf16[256,128]{1,0:T(8,128)(2,1)S(1)}, u32[]{:S(2)}, u32[]{:S(2)}) collective-permute-start(bf16[256,128]{1,0:T(8,128)(2,1)S(1)} %get-tuple-element.69), channel_id=1, source_target_pairs={{0,4},{1,5},{2,6},{3,7},{4,0},{5,1},{6,2},{7,3},{8,12},{9,13},{10,... | collective-permute-start | bytes 196616 | tf_op jit(solution)/shard_map/ppermute | solution.py:86
  36.4 3.1 %collective-permute-done.12.refs_3_ = bf16[768,128]{1,0:T(8,128)(2,1)S(1)} collective-permute-done((bf16[768,128]{1,0:T(8,128)(2,1)S(1)}, bf16[768,128]{1,0:T(8,128)(2,1)S(1)}, u32[]{:S(2)}, u32[]{:S(2)}) %collective-permute-start.12) | collective-permute-done | bytes 196640 | tf_op jit(solution)/shard_map/ppermute | solution.py:83
  39.6 0.6 collective-permute-start.20
  40.2 2.0 %collective-permute-done.13.refs_2_ = bf16[768,128]{1,0:T(8,128)(2,1)S(1)} collective-permute-done((bf16[768,128]{1,0:T(8,128)(2,1)S(1)}, bf16[768,128]{1,0:T(8,128)(2,1)S(1)}, u32[]{:S(2)}, u32[]{:S(2)}) %collective-permute-start.13) | collective-permute-done | bytes 196640 | tf_op jit(solution)/shard_map/ppermute | solution.py:83
  42.2 0.8 %collective-permute-done.14.refs_1_ = bf16[768,128]{1,0:T(8,128)(2,1)S(1)} collective-permute-done((bf16[768,128]{1,0:T(8,128)(2,1)S(1)}, bf16[768,128]{1,0:T(8,128)(2,1)S(1)}, u32[]{:S(2)}, u32[]{:S(2)}) %collective-permute-start.14) | collective-permute-done | bytes 196640 | tf_op jit(solution)/shard_map/ppermute | solution.py:83
  43.0 1.7 %attend.1 = (bf16[144,128]{1,0:T(8,128)(2,1)S(1)}, bf16[144,128]{1,0:T(8,128)(2,1)S(1)}, bf16[144,128]{1,0:T(8,128)(2,1)S(1)}, bf16[144,128]{1,0:T(8,128)(2,1)S(1)}) custom-call(bf16[768,128]{1,0:T(8,128)(2,1)S(1)} %get-tuple-element.49.refs_0_, bf16[768,128]{1,0:T(8,128)(2,1)S(1)} %collective-permute-done.14.refs_1_, ...), custom_call_target="tpu_custom_call" | custom-call | tf_op jit(solution)/shard_map/attend/pallas_call | solution.py:37
  44.8 0.4 collective-permute-start.15
  45.2 1.4 %collective-permute-start.16 = (bf16[144,128]{1,0:T(8,128)(2,1)S(1)}, bf16[144,128]{1,0:T(8,128)(2,1)S(1)}, u32[]{:S(2)}, u32[]{:S(2)}) collective-permute-start(bf16[144,128]{1,0:T(8,128)(2,1)S(1)} %get-tuple-element.61), channel_id=1, source_target_pairs={{0,16},{1,17},{2,18},{3,19},{4,20},{5,21},{6,22},{7,23},{8,24},{9,... | collective-permute-start | bytes 110600 | tf_op jit(solution)/shard_map/ppermute | solution.py:83
  46.6 1.7 %collective-permute-start.17 = (bf16[144,128]{1,0:T(8,128)(2,1)S(1)}, bf16[144,128]{1,0:T(8,128)(2,1)S(1)}, u32[]{:S(2)}, u32[]{:S(2)}) collective-permute-start(bf16[144,128]{1,0:T(8,128)(2,1)S(1)} %get-tuple-element.62), channel_id=1, source_target_pairs={{0,8},{1,9},{2,10},{3,11},{4,12},{5,13},{6,14},{7,15},{8,0},{9,1},... | collective-permute-start | bytes 110600 | tf_op jit(solution)/shard_map/ppermute | solution.py:83
  48.3 1.4 %collective-permute-done.15.refs_1_ = bf16[144,128]{1,0:T(8,128)(2,1)S(1)} collective-permute-done((bf16[144,128]{1,0:T(8,128)(2,1)S(1)}, bf16[144,128]{1,0:T(8,128)(2,1)S(1)}, u32[]{:S(2)}, u32[]{:S(2)}) %collective-permute-start.15) | collective-permute-done | bytes 36896 | tf_op jit(solution)/shard_map/ppermute | solution.py:83
  49.7 0.9 %collective-permute-done.17.refs_3_ = bf16[144,128]{1,0:T(8,128)(2,1)S(1)} collective-permute-done((bf16[144,128]{1,0:T(8,128)(2,1)S(1)}, bf16[144,128]{1,0:T(8,128)(2,1)S(1)}, u32[]{:S(2)}, u32[]{:S(2)}) %collective-permute-start.17) | collective-permute-done | bytes 36896 | tf_op jit(solution)/shard_map/ppermute | solution.py:83
  50.5 0.1 finish.1
  50.7 2.2 %collective-permute-start.23 = (bf16[128,128]{1,0:T(8,128)(2,1)S(1)}, bf16[128,128]{1,0:T(8,128)(2,1)S(1)}, u32[]{:S(2)}, u32[]{:S(2)}) collective-permute-start(bf16[128,128]{1,0:T(8,128)(2,1)S(1)} %get-tuple-element.80.refs_3_), channel_id=1, source_target_pairs={{0,6},{1,7},{2,4},{3,5},{4,2},{5,3},{6,0},{7,1},{8,14},{9,15},{10,... | collective-permute-start | bytes 98312 | tf_op jit(solution)/shard_map/ppermute | solution.py:86
  52.8 1.0 %collective-permute-start.22 = (bf16[128,128]{1,0:T(8,128)(2,1)S(1)}, bf16[128,128]{1,0:T(8,128)(2,1)S(1)}, u32[]{:S(2)}, u32[]{:S(2)}) collective-permute-start(bf16[128,128]{1,0:T(8,128)(2,1)S(1)} %get-tuple-element.80.refs_3_), channel_id=1, source_target_pairs={{0,4},{1,5},{2,6},{3,7},{4,0},{5,1},{6,2},{7,3},{8,12},{9,13},{10,... | collective-permute-start | bytes 98312 | tf_op jit(solution)/shard_map/ppermute | solution.py:86
  53.9 1.2 %collective-permute-start.21 = (bf16[128,128]{1,0:T(8,128)(2,1)S(1)}, bf16[128,128]{1,0:T(8,128)(2,1)S(1)}, u32[]{:S(2)}, u32[]{:S(2)}) collective-permute-start(bf16[128,128]{1,0:T(8,128)(2,1)S(1)} %get-tuple-element.80.refs_3_), channel_id=1, source_target_pairs={{0,2},{1,3},{2,0},{3,1},{4,6},{5,7},{6,4},{7,5},{8,10},{9,11},{10,... | collective-permute-start | bytes 98312 | tf_op jit(solution)/shard_map/ppermute | solution.py:86
  55.1 1.6 %collective-permute-done.23.refs_6_ = bf16[128,128]{1,0:T(8,128)(2,1)S(1)} collective-permute-done((bf16[128,128]{1,0:T(8,128)(2,1)S(1)}, bf16[128,128]{1,0:T(8,128)(2,1)S(1)}, u32[]{:S(2)}, u32[]{:S(2)}) %collective-permute-start.23) | collective-permute-done | bytes 32800 | tf_op jit(solution)/shard_map/ppermute | solution.py:86
  56.7 1.0 %collective-permute-done.22.refs_5_ = bf16[128,128]{1,0:T(8,128)(2,1)S(1)} collective-permute-done((bf16[128,128]{1,0:T(8,128)(2,1)S(1)}, bf16[128,128]{1,0:T(8,128)(2,1)S(1)}, u32[]{:S(2)}, u32[]{:S(2)}) %collective-permute-start.22) | collective-permute-done | bytes 32800 | tf_op jit(solution)/shard_map/ppermute | solution.py:86
  57.7 0.3 collective-permute-done.21.refs_4_
  58.0 0.2 collective-permute-start.25
  58.2 0.7 %collective-permute-done.26.refs_9_ = bf16[128,128]{1,0:T(8,128)(2,1)S(1)} collective-permute-done((bf16[128,128]{1,0:T(8,128)(2,1)S(1)}, bf16[128,128]{1,0:T(8,128)(2,1)S(1)}, u32[]{:S(2)}, u32[]{:S(2)}) %collective-permute-start.26) | collective-permute-done | bytes 32800 | tf_op jit(solution)/shard_map/ppermute | solution.py:80
  58.9 0.3 collective-permute-done.25.refs_8_
  59.2 1.1 %output.1 = (bf16[128,768]{1,0:T(8,128)(2,1)}, bf16[128,128]{1,0:T(8,128)(2,1)}) custom-call(bf16[128,768]{1,0:T(8,128)(2,1)S(1)} %copy-done.1, f32[1,768]{1,0:T(1,128)S(1)} %reshape.13.refs_1_, bf16[128,128]{1,0:T(8,128)(2,1)S(1)} %get-tuple-element.79.refs_2_, bf16[128,128]{1,0:T(8,128)(2,1)S(1)} %get-tuple-element.80.refs_3_, ...), custom_call_target="tpu_custom_call" | custom-call | tf_op jit(solution)/shard_map/output/pallas_call | solution.py:37
  (28 shorter events, 0.1 us)
Async XLA Ops:
  0.6 19.9 %collective-permute-start.5 = (bf16[256,768]{1,0:T(8,128)(2,1)}, bf16[256,768]{1,0:T(8,128)(2,1)S(1)}, u32[]{:S(2)}, u32[]{:S(2)}) collective-permute-start(bf16[256,768]{1,0:T(8,128)(2,1)} %refs_11_.1), channel_id=1, source_target_pairs={{0,16},{1,17},{2,18},{3,19},{4,20},{5,21},{6,22},{7,23},{8,24},{9,... | collective-permute-start | bytes 1179656 | tf_op jit(solution)/shard_map/ppermute | solution.py:83
  3.7 18.2 %collective-permute-start.4 = (bf16[256,768]{1,0:T(8,128)(2,1)}, bf16[256,768]{1,0:T(8,128)(2,1)S(1)}, u32[]{:S(2)}, u32[]{:S(2)}) collective-permute-start(bf16[256,768]{1,0:T(8,128)(2,1)} %refs_11_.1), channel_id=1, source_target_pairs={{0,8},{1,9},{2,10},{3,11},{4,12},{5,13},{6,14},{7,15},{8,0},{9,1},... | collective-permute-start | bytes 1179656 | tf_op jit(solution)/shard_map/ppermute | solution.py:83
  5.2 13.3 %collective-permute-start = (bf16[128,768]{1,0:T(8,128)(2,1)}, bf16[128,768]{1,0:T(8,128)(2,1)S(1)}, u32[]{:S(2)}, u32[]{:S(2)}) collective-permute-start(bf16[128,768]{1,0:T(8,128)(2,1)} %refs_0_.5), channel_id=1, source_target_pairs={{0,6},{1,7},{2,12},{3,13},{4,18},{5,19},{6,24},{7,25},{8,4},{9,5},... | collective-permute-start | bytes 589832 | tf_op jit(solution)/shard_map/ppermute | solution.py:89
  8.8 9.7 %collective-permute-start.1 = (bf16[128,768]{1,0:T(8,128)(2,1)}, bf16[128,768]{1,0:T(8,128)(2,1)S(1)}, u32[]{:S(2)}, u32[]{:S(2)}) collective-permute-start(bf16[128,768]{1,0:T(8,128)(2,1)} %refs_0_.5), channel_id=1, source_target_pairs={{0,1},{1,0},{2,10},{3,11},{4,20},{5,21},{6,30},{7,31},{8,2},{9,3},... | collective-permute-start | bytes 589832 | tf_op jit(solution)/shard_map/ppermute | solution.py:89
  18.5 7.8 %collective-permute-start.2 = (bf16[128,768]{1,0:T(8,128)(2,1)S(1)}, bf16[128,768]{1,0:T(8,128)(2,1)S(1)}, u32[]{:S(2)}, u32[]{:S(2)}) collective-permute-start(bf16[128,768]{1,0:T(8,128)(2,1)S(1)} %collective-permute-done.refs_0_), channel_id=1, source_target_pairs={{0,2},{1,3},{2,0},{3,1},{4,6},{5,7},{6,4},{7,5},{8,10},{9,11},{10,... | collective-permute-start | bytes 589832 | tf_op jit(solution)/shard_map/ppermute | solution.py:86
  18.5 10.0 %collective-permute-start.3 = (bf16[128,768]{1,0:T(8,128)(2,1)S(1)}, bf16[128,768]{1,0:T(8,128)(2,1)S(1)}, u32[]{:S(2)}, u32[]{:S(2)}) collective-permute-start(bf16[128,768]{1,0:T(8,128)(2,1)S(1)} %collective-permute-done.1.refs_1_), channel_id=1, source_target_pairs={{0,2},{1,3},{2,0},{3,1},{4,6},{5,7},{6,4},{7,5},{8,10},{9,11},{10,... | collective-permute-start | bytes 589832 | tf_op jit(solution)/shard_map/ppermute | solution.py:86
  20.5 7.9 %collective-permute-start.6 = (bf16[128,768]{1,0:T(8,128)(2,1)S(1)}, bf16[128,768]{1,0:T(8,128)(2,1)S(1)}, u32[]{:S(2)}, u32[]{:S(2)}) collective-permute-start(bf16[128,768]{1,0:T(8,128)(2,1)S(1)} %slice.8), channel_id=1, source_target_pairs={{0,8},{1,9},{2,10},{3,11},{4,12},{5,13},{6,14},{7,15},{8,0},{9,1},... | collective-permute-start | bytes 589832 | tf_op jit(solution)/shard_map/ppermute | solution.py:83
  21.8 7.1 %copy-start.3 = (f32[768]{0:T(1024)S(1)}, f32[768]{0:T(1024)}, u32[]{:S(2)}) copy-start(f32[768]{0:T(1024)} %param.20) | copy-start | bytes 9220
  21.8 6.6 %collective-permute-start.7 = (bf16[128,768]{1,0:T(8,128)(2,1)S(1)}, bf16[128,768]{1,0:T(8,128)(2,1)S(1)}, u32[]{:S(2)}, u32[]{:S(2)}) collective-permute-start(bf16[128,768]{1,0:T(8,128)(2,1)S(1)} %slice.9), channel_id=1, source_target_pairs={{0,16},{1,17},{2,18},{3,19},{4,20},{5,21},{6,22},{7,23},{8,24},{9,... | collective-permute-start | bytes 589832 | tf_op jit(solution)/shard_map/ppermute | solution.py:83
  24.4 4.6 %collective-permute-start.10 = (bf16[128,768]{1,0:T(8,128)(2,1)S(1)}, bf16[128,768]{1,0:T(8,128)(2,1)S(1)}, u32[]{:S(2)}, u32[]{:S(2)}) collective-permute-start(bf16[128,768]{1,0:T(8,128)(2,1)S(1)} %collective-permute-done.refs_0_), channel_id=1, source_target_pairs={{0,1},{1,0},{2,3},{3,2},{4,5},{5,4},{6,7},{7,6},{8,9},{9,8},{10,11... | collective-permute-start | bytes 589832 | tf_op jit(solution)/shard_map/ppermute | solution.py:80
  26.3 2.7 %collective-permute-start.11 = (bf16[128,768]{1,0:T(8,128)(2,1)S(1)}, bf16[128,768]{1,0:T(8,128)(2,1)S(1)}, u32[]{:S(2)}, u32[]{:S(2)}) collective-permute-start(bf16[128,768]{1,0:T(8,128)(2,1)S(1)} %collective-permute-done.1.refs_1_), channel_id=1, source_target_pairs={{0,1},{1,0},{2,3},{3,2},{4,5},{5,4},{6,7},{7,6},{8,9},{9,8},{10,11... | collective-permute-start | bytes 589832 | tf_op jit(solution)/shard_map/ppermute | solution.py:80
  28.4 1.4 %collective-permute-start.8 = (bf16[128,768]{1,0:T(8,128)(2,1)S(1)}, bf16[128,768]{1,0:T(8,128)(2,1)S(1)}, u32[]{:S(2)}, u32[]{:S(2)}) collective-permute-start(bf16[128,768]{1,0:T(8,128)(2,1)S(1)} %collective-permute-done.2.refs_0_), channel_id=1, source_target_pairs={{0,1},{1,0},{2,3},{3,2},{4,5},{5,4},{6,7},{7,6},{8,9},{9,8},{10,11... | collective-permute-start | bytes 589832 | tf_op jit(solution)/shard_map/ppermute | solution.py:80
  28.5 1.7 %collective-permute-start.9 = (bf16[128,768]{1,0:T(8,128)(2,1)S(1)}, bf16[128,768]{1,0:T(8,128)(2,1)S(1)}, u32[]{:S(2)}, u32[]{:S(2)}) collective-permute-start(bf16[128,768]{1,0:T(8,128)(2,1)S(1)} %collective-permute-done.3.refs_1_), channel_id=1, source_target_pairs={{0,1},{1,0},{2,3},{3,2},{4,5},{5,4},{6,7},{7,6},{8,9},{9,8},{10,11... | collective-permute-start | bytes 589832 | tf_op jit(solution)/shard_map/ppermute | solution.py:80
  29.6 4.8 %copy-start = (bf16[256,768]{1,0:T(8,128)(2,1)S(1)}, bf16[256,768]{1,0:T(8,128)(2,1)}, u32[]{:S(2)}) copy-start(bf16[256,768]{1,0:T(8,128)(2,1)} %refs_11_.1) | copy-start | bytes 1179652
  29.6 4.8 %copy-start.2 = (bf16[128,768]{1,0:T(8,128)(2,1)S(1)}, bf16[128,768]{1,0:T(8,128)(2,1)}, u32[]{:S(2)}) copy-start(bf16[128,768]{1,0:T(8,128)(2,1)} %refs_0_.4) | copy-start | bytes 589828
  30.8 8.7 %collective-permute-start.12 = (bf16[768,128]{1,0:T(8,128)(2,1)S(1)}, bf16[768,128]{1,0:T(8,128)(2,1)S(1)}, u32[]{:S(2)}, u32[]{:S(2)}) collective-permute-start(bf16[768,128]{1,0:T(8,128)(2,1)S(1)} %get-tuple-element.50), channel_id=1, source_target_pairs={{0,24},{1,25},{2,26},{3,27},{4,28},{5,29},{6,30},{7,31},{8,16},{9,... | collective-permute-start | bytes 589832 | tf_op jit(solution)/shard_map/ppermute | solution.py:83
  30.9 11.3 %collective-permute-start.13 = (bf16[768,128]{1,0:T(8,128)(2,1)S(1)}, bf16[768,128]{1,0:T(8,128)(2,1)S(1)}, u32[]{:S(2)}, u32[]{:S(2)}) collective-permute-start(bf16[768,128]{1,0:T(8,128)(2,1)S(1)} %get-tuple-element.51), channel_id=1, source_target_pairs={{0,16},{1,17},{2,18},{3,19},{4,20},{5,21},{6,22},{7,23},{8,24},{9,... | collective-permute-start | bytes 589832 | tf_op jit(solution)/shard_map/ppermute | solution.py:83
  32.6 10.4 %collective-permute-start.14 = (bf16[768,128]{1,0:T(8,128)(2,1)S(1)}, bf16[768,128]{1,0:T(8,128)(2,1)S(1)}, u32[]{:S(2)}, u32[]{:S(2)}) collective-permute-start(bf16[768,128]{1,0:T(8,128)(2,1)S(1)} %get-tuple-element.52), channel_id=1, source_target_pairs={{0,8},{1,9},{2,10},{3,11},{4,12},{5,13},{6,14},{7,15},{8,0},{9,1},... | collective-permute-start | bytes 589832 | tf_op jit(solution)/shard_map/ppermute | solution.py:83
  35.1 11.5 %collective-permute-start.18 = (bf16[256,128]{1,0:T(8,128)(2,1)S(1)}, bf16[256,128]{1,0:T(8,128)(2,1)S(1)}, u32[]{:S(2)}, u32[]{:S(2)}) collective-permute-start(bf16[256,128]{1,0:T(8,128)(2,1)S(1)} %get-tuple-element.68), channel_id=1, source_target_pairs={{0,2},{1,3},{2,0},{3,1},{4,6},{5,7},{6,4},{7,5},{8,10},{9,11},{10,... | collective-permute-start | bytes 196616 | tf_op jit(solution)/shard_map/ppermute | solution.py:86
  35.5 12.9 %collective-permute-start.19 = (bf16[256,128]{1,0:T(8,128)(2,1)S(1)}, bf16[256,128]{1,0:T(8,128)(2,1)S(1)}, u32[]{:S(2)}, u32[]{:S(2)}) collective-permute-start(bf16[256,128]{1,0:T(8,128)(2,1)S(1)} %get-tuple-element.69), channel_id=1, source_target_pairs={{0,4},{1,5},{2,6},{3,7},{4,0},{5,1},{6,2},{7,3},{8,12},{9,13},{10,... | collective-permute-start | bytes 196616 | tf_op jit(solution)/shard_map/ppermute | solution.py:86
  39.6 8.8 %collective-permute-start.20 = (bf16[256,128]{1,0:T(8,128)(2,1)S(1)}, bf16[256,128]{1,0:T(8,128)(2,1)S(1)}, u32[]{:S(2)}, u32[]{:S(2)}) collective-permute-start(bf16[256,128]{1,0:T(8,128)(2,1)S(1)} %get-tuple-element.70), channel_id=1, source_target_pairs={{0,6},{1,7},{2,4},{3,5},{4,2},{5,3},{6,0},{7,1},{8,14},{9,15},{10,... | collective-permute-start | bytes 196616 | tf_op jit(solution)/shard_map/ppermute | solution.py:86
  43.0 16.2 %copy-start.1 = (bf16[128,768]{1,0:T(8,128)(2,1)S(1)}, bf16[128,768]{1,0:T(8,128)(2,1)}, u32[]{:S(2)}) copy-start(bf16[128,768]{1,0:T(8,128)(2,1)} %refs_0_.5) | copy-start | bytes 589828
  44.8 4.9 %collective-permute-start.15 = (bf16[144,128]{1,0:T(8,128)(2,1)S(1)}, bf16[144,128]{1,0:T(8,128)(2,1)S(1)}, u32[]{:S(2)}, u32[]{:S(2)}) collective-permute-start(bf16[144,128]{1,0:T(8,128)(2,1)S(1)} %get-tuple-element.60), channel_id=1, source_target_pairs={{0,24},{1,25},{2,26},{3,27},{4,28},{5,29},{6,30},{7,31},{8,16},{9,... | collective-permute-start | bytes 110600 | tf_op jit(solution)/shard_map/ppermute | solution.py:83
  45.2 4.5 %collective-permute-start.16 = (bf16[144,128]{1,0:T(8,128)(2,1)S(1)}, bf16[144,128]{1,0:T(8,128)(2,1)S(1)}, u32[]{:S(2)}, u32[]{:S(2)}) collective-permute-start(bf16[144,128]{1,0:T(8,128)(2,1)S(1)} %get-tuple-element.61), channel_id=1, source_target_pairs={{0,16},{1,17},{2,18},{3,19},{4,20},{5,21},{6,22},{7,23},{8,24},{9,... | collective-permute-start | bytes 110600 | tf_op jit(solution)/shard_map/ppermute | solution.py:83
  46.6 4.0 %collective-permute-start.17 = (bf16[144,128]{1,0:T(8,128)(2,1)S(1)}, bf16[144,128]{1,0:T(8,128)(2,1)S(1)}, u32[]{:S(2)}, u32[]{:S(2)}) collective-permute-start(bf16[144,128]{1,0:T(8,128)(2,1)S(1)} %get-tuple-element.62), channel_id=1, source_target_pairs={{0,8},{1,9},{2,10},{3,11},{4,12},{5,13},{6,14},{7,15},{8,0},{9,1},... | collective-permute-start | bytes 110600 | tf_op jit(solution)/shard_map/ppermute | solution.py:83
  50.7 6.0 %collective-permute-start.23 = (bf16[128,128]{1,0:T(8,128)(2,1)S(1)}, bf16[128,128]{1,0:T(8,128)(2,1)S(1)}, u32[]{:S(2)}, u32[]{:S(2)}) collective-permute-start(bf16[128,128]{1,0:T(8,128)(2,1)S(1)} %get-tuple-element.80.refs_3_), channel_id=1, source_target_pairs={{0,6},{1,7},{2,4},{3,5},{4,2},{5,3},{6,0},{7,1},{8,14},{9,15},{10,... | collective-permute-start | bytes 98312 | tf_op jit(solution)/shard_map/ppermute | solution.py:86
  52.8 4.8 %collective-permute-start.22 = (bf16[128,128]{1,0:T(8,128)(2,1)S(1)}, bf16[128,128]{1,0:T(8,128)(2,1)S(1)}, u32[]{:S(2)}, u32[]{:S(2)}) collective-permute-start(bf16[128,128]{1,0:T(8,128)(2,1)S(1)} %get-tuple-element.80.refs_3_), channel_id=1, source_target_pairs={{0,4},{1,5},{2,6},{3,7},{4,0},{5,1},{6,2},{7,3},{8,12},{9,13},{10,... | collective-permute-start | bytes 98312 | tf_op jit(solution)/shard_map/ppermute | solution.py:86
  53.9 4.1 %collective-permute-start.21 = (bf16[128,128]{1,0:T(8,128)(2,1)S(1)}, bf16[128,128]{1,0:T(8,128)(2,1)S(1)}, u32[]{:S(2)}, u32[]{:S(2)}) collective-permute-start(bf16[128,128]{1,0:T(8,128)(2,1)S(1)} %get-tuple-element.80.refs_3_), channel_id=1, source_target_pairs={{0,2},{1,3},{2,0},{3,1},{4,6},{5,7},{6,4},{7,5},{8,10},{9,11},{10,... | collective-permute-start | bytes 98312 | tf_op jit(solution)/shard_map/ppermute | solution.py:86
  55.1 4.1 %collective-permute-start.24 = (bf16[256,128]{1,0:T(8,128)(2,1)S(1)}, bf16[256,128]{1,0:T(8,128)(2,1)S(1)}, u32[]{:S(2)}, u32[]{:S(2)}) collective-permute-start(bf16[256,128]{1,0:T(8,128)(2,1)S(1)} %get-tuple-element.81), channel_id=1, source_target_pairs={{0,1},{1,0},{2,3},{3,2},{4,5},{5,4},{6,7},{7,6},{8,9},{9,8},{10,11... | collective-permute-start | bytes 196616 | tf_op jit(solution)/shard_map/ppermute | solution.py:80
  56.7 1.5 %collective-permute-start.27 = (bf16[128,128]{1,0:T(8,128)(2,1)S(1)}, bf16[128,128]{1,0:T(8,128)(2,1)S(1)}, u32[]{:S(2)}, u32[]{:S(2)}) collective-permute-start(bf16[128,128]{1,0:T(8,128)(2,1)S(1)} %collective-permute-done.23.refs_6_), channel_id=1, source_target_pairs={{0,1},{1,0},{2,3},{3,2},{4,5},{5,4},{6,7},{7,6},{8,9},{9,8},{10,11... | collective-permute-start | bytes 98312 | tf_op jit(solution)/shard_map/ppermute | solution.py:80
  57.7 1.2 %collective-permute-start.26 = (bf16[128,128]{1,0:T(8,128)(2,1)S(1)}, bf16[128,128]{1,0:T(8,128)(2,1)S(1)}, u32[]{:S(2)}, u32[]{:S(2)}) collective-permute-start(bf16[128,128]{1,0:T(8,128)(2,1)S(1)} %collective-permute-done.22.refs_5_), channel_id=1, source_target_pairs={{0,1},{1,0},{2,3},{3,2},{4,5},{5,4},{6,7},{7,6},{8,9},{9,8},{10,11... | collective-permute-start | bytes 98312 | tf_op jit(solution)/shard_map/ppermute | solution.py:80
  58.0 1.2 %collective-permute-start.25 = (bf16[128,128]{1,0:T(8,128)(2,1)S(1)}, bf16[128,128]{1,0:T(8,128)(2,1)S(1)}, u32[]{:S(2)}, u32[]{:S(2)}) collective-permute-start(bf16[128,128]{1,0:T(8,128)(2,1)S(1)} %collective-permute-done.21.refs_4_), channel_id=1, source_target_pairs={{0,1},{1,0},{2,3},{3,2},{4,5},{5,4},{6,7},{7,6},{8,9},{9,8},{10,11... | collective-permute-start | bytes 98312 | tf_op jit(solution)/shard_map/ppermute | solution.py:80

commit v7 on v6

--- a/solution.py
+++ b/solution.py
@@ -189,7 +189,7 @@
             for s in range(R):
                 outs[s][R * T :, :] = held[f ^ s]
 
-        direct_other = [across_chip(mine[d]) for d in order]
+        direct_other = [across_chip(x) for x in lax.optimization_barrier([mine[d] for d in order])]
         (direct_part,) = call(
             project_direct,
             "project_direct",

time: 60.5 us -> 60.5 us (level)
  no operation moved by 1% of the time
where the time goes in v7:
time: 60.5 us; the launch traced here: 60.3 us
  waiting for transfers between devices  26.3 us (43%)
  starting transfers between devices  25.8 us (43%)
  Pallas kernels  7.34 us (12%)
  between operations  0.79 us (1%)
    ppermute x10, starting transfers between devices, over_row(): return lax.ppermute(x, both, route(lambda r, z, q: (r ^ s, z, q)))  13 us
    ppermute x2, waiting for transfers between devices, turned(): lax.ppermute(x, both, route(lambda r, z, q: (z, r ^ z ^ d, q ^ (r == z ==...  9.7 us
    ppermute x8, starting transfers between devices, over_z(): return lax.ppermute(x, both, route(lambda r, z, q: (r, z ^ m, q)))  8.39 us
    ppermute x10, waiting for transfers between devices, over_row(): return lax.ppermute(x, both, route(lambda r, z, q: (r ^ s, z, q)))  8.22 us
    pallas_call x7, Pallas kernels, call(): pl.pallas_call(fetch if far else kernel, out_shape=list(outs), in_specs=[...  7.34 us
    ppermute x8, waiting for transfers between devices, over_z(): return lax.ppermute(x, both, route(lambda r, z, q: (r, z ^ m, q)))  6.85 us
    ppermute x2, starting transfers between devices, turned(): lax.ppermute(x, both, route(lambda r, z, q: (z, r ^ z ^ d, q ^ (r == z ==...  3.6 us
    ppermute x8, waiting for transfers between devices, across_chip(): return lax.ppermute(x, both, route(lambda r, z, q: (r, z, q ^ 1)))  1.58 us
  transfers between devices with their start and end apart: 28, of which 15 were waited for; matrix products, arithmetic and copies ran while one was open for 0% of the time, Pallas kernels for 9%

profile of v7, /device:TPU:0, one launch (start us, length us, event | category | flops | bytes accessed | tf_op | source)
XLA Modules:
  0.0 60.3 jit_solution(18243745712718507218)
XLA Ops:
  0.6 3.0 %collective-permute-start.5 = (bf16[256,768]{1,0:T(8,128)(2,1)}, bf16[256,768]{1,0:T(8,128)(2,1)S(1)}, u32[]{:S(2)}, u32[]{:S(2)}) collective-permute-start(bf16[256,768]{1,0:T(8,128)(2,1)} %refs_11_.1), channel_id=1, source_target_pairs={{0,16},{1,17},{2,18},{3,19},{4,20},{5,21},{6,22},{7,23},{8,24},{9,... | collective-permute-start | bytes 1179656 | tf_op jit(solution)/shard_map/ppermute | solution.py:83
  3.7 1.5 %collective-permute-start.4 = (bf16[256,768]{1,0:T(8,128)(2,1)}, bf16[256,768]{1,0:T(8,128)(2,1)S(1)}, u32[]{:S(2)}, u32[]{:S(2)}) collective-permute-start(bf16[256,768]{1,0:T(8,128)(2,1)} %refs_11_.1), channel_id=1, source_target_pairs={{0,8},{1,9},{2,10},{3,11},{4,12},{5,13},{6,14},{7,15},{8,0},{9,1},... | collective-permute-start | bytes 1179656 | tf_op jit(solution)/shard_map/ppermute | solution.py:83
  5.2 3.6 %collective-permute-start = (bf16[128,768]{1,0:T(8,128)(2,1)}, bf16[128,768]{1,0:T(8,128)(2,1)S(1)}, u32[]{:S(2)}, u32[]{:S(2)}) collective-permute-start(bf16[128,768]{1,0:T(8,128)(2,1)} %refs_0_.5), channel_id=1, source_target_pairs={{0,6},{1,7},{2,12},{3,13},{4,18},{5,19},{6,24},{7,25},{8,4},{9,5},... | collective-permute-start | bytes 589832 | tf_op jit(solution)/shard_map/ppermute | solution.py:89
  8.8 0.0 collective-permute-start.1
  8.8 9.7 %collective-permute-done.refs_0_ = bf16[128,768]{1,0:T(8,128)(2,1)S(1)} collective-permute-done((bf16[128,768]{1,0:T(8,128)(2,1)}, bf16[128,768]{1,0:T(8,128)(2,1)S(1)}, u32[]{:S(2)}, u32[]{:S(2)}) %collective-permute-start) | collective-permute-done | bytes 196640 | tf_op jit(solution)/shard_map/ppermute | solution.py:89
  18.5 0.0 collective-permute-done.1.refs_1_
  18.5 2.0 %collective-permute-start.3 = (bf16[128,768]{1,0:T(8,128)(2,1)S(1)}, bf16[128,768]{1,0:T(8,128)(2,1)S(1)}, u32[]{:S(2)}, u32[]{:S(2)}) collective-permute-start(bf16[128,768]{1,0:T(8,128)(2,1)S(1)} %collective-permute-done.1.refs_1_), channel_id=1, source_target_pairs={{0,2},{1,3},{2,0},{3,1},{4,6},{5,7},{6,4},{7,5},{8,10},{9,11},{10,... | collective-permute-start | bytes 589832 | tf_op jit(solution)/shard_map/ppermute | solution.py:86
  20.5 1.3 %collective-permute-start.6 = (bf16[128,768]{1,0:T(8,128)(2,1)S(1)}, bf16[128,768]{1,0:T(8,128)(2,1)S(1)}, u32[]{:S(2)}, u32[]{:S(2)}) collective-permute-start(bf16[128,768]{1,0:T(8,128)(2,1)S(1)} %slice.8), channel_id=1, source_target_pairs={{0,8},{1,9},{2,10},{3,11},{4,12},{5,13},{6,14},{7,15},{8,0},{9,1},... | collective-permute-start | bytes 589832 | tf_op jit(solution)/shard_map/ppermute | solution.py:83
  21.8 0.0 copy-start.3
  21.8 0.1 collective-permute-start.7
  21.9 2.5 %prepare.1 = (bf16[128,2048]{1,0:T(8,128)(2,1)S(1)}, bf16[2048,256]{1,0:T(8,128)(2,1)S(1)}, bf16[1536,384]{1,0:T(8,128)(2,1)S(1)}, f32[2,128]{1,0:T(2,128)S(1)}) custom-call(bf16[2048,128]{1,0:T(8,128)(2,1)} %refs_0_.3, bf16[2048,128]{1,0:T(8,128)(2,1)} %refs_1_.1, bf16[1536,128]{1,0:T(8,128)(2,1)} %refs_2_.2, bf16[1536,128]{1,0:T(8,128)(2,1)} %refs_3_.1, ...), custom_call_target="tpu_custom_call" | custom-call | tf_op jit(solution)/shard_map/prepare/pallas_call | solution.py:37
  24.4 0.1 collective-permute-start.10
  24.5 1.8 %collective-permute-done.2.refs_0_ = bf16[128,768]{1,0:T(8,128)(2,1)S(1)} collective-permute-done((bf16[128,768]{1,0:T(8,128)(2,1)S(1)}, bf16[128,768]{1,0:T(8,128)(2,1)S(1)}, u32[]{:S(2)}, u32[]{:S(2)}) %collective-permute-start.2) | collective-permute-done | bytes 196640 | tf_op jit(solution)/shard_map/ppermute | solution.py:86
  26.3 2.1 %collective-permute-done.3.refs_1_ = bf16[128,768]{1,0:T(8,128)(2,1)S(1)} collective-permute-done((bf16[128,768]{1,0:T(8,128)(2,1)S(1)}, bf16[128,768]{1,0:T(8,128)(2,1)S(1)}, u32[]{:S(2)}, u32[]{:S(2)}) %collective-permute-start.3) | collective-permute-done | bytes 196640 | tf_op jit(solution)/shard_map/ppermute | solution.py:86
  28.5 0.5 collective-permute-start.9
  29.0 0.6 %project_direct.1.refs_4_ = bf16[256,384]{1,0:T(8,128)(2,1)S(1)} custom-call(bf16[128,768]{1,0:T(8,128)(2,1)S(1)} %collective-permute-done.refs_0_, bf16[128,768]{1,0:T(8,128)(2,1)S(1)} %collective-permute-done.1.refs_1_, bf16[128,768]{1,0:T(8,128)(2,1)S(1)} %collective-permute-done.10.refs_2_, bf16[128,768]{1,0:T(8,128)(2,1)S(1)} %collective-permute-done.11.refs_3_, ...), custom_call_target="tpu_custom_call" | custom-call | tf_op jit(solution)/shard_map/project_direct/pallas_call | solution.py:37
  29.6 0.0 copy-start
  29.6 0.0 copy-start.2
  29.6 0.3 collective-permute-done.8.refs_2_
  29.9 0.3 collective-permute-done.9.refs_3_
  30.2 0.6 %project.1 = (bf16[768,128]{1,0:T(8,128)(2,1)S(1)}, bf16[768,128]{1,0:T(8,128)(2,1)S(1)}, bf16[768,128]{1,0:T(8,128)(2,1)S(1)}, bf16[768,128]{1,0:T(8,128)(2,1)S(1)}) custom-call(bf16[128,768]{1,0:T(8,128)(2,1)S(1)} %collective-permute-done.2.refs_0_, bf16[128,768]{1,0:T(8,128)(2,1)S(1)} %collective-permute-done.3.refs_1_, ...), custom_call_target="tpu_custom_call" | custom-call | tf_op jit(solution)/shard_map/project/pallas_call | solution.py:37
  30.8 0.1 collective-permute-start.12
  30.9 1.7 %collective-permute-start.13 = (bf16[768,128]{1,0:T(8,128)(2,1)S(1)}, bf16[768,128]{1,0:T(8,128)(2,1)S(1)}, u32[]{:S(2)}, u32[]{:S(2)}) collective-permute-start(bf16[768,128]{1,0:T(8,128)(2,1)S(1)} %get-tuple-element.55), channel_id=1, source_target_pairs={{0,16},{1,17},{2,18},{3,19},{4,20},{5,21},{6,22},{7,23},{8,24},{9,... | collective-permute-start | bytes 589832 | tf_op jit(solution)/shard_map/ppermute | solution.py:83
  32.6 1.7 %collective-permute-start.14 = (bf16[768,128]{1,0:T(8,128)(2,1)S(1)}, bf16[768,128]{1,0:T(8,128)(2,1)S(1)}, u32[]{:S(2)}, u32[]{:S(2)}) collective-permute-start(bf16[768,128]{1,0:T(8,128)(2,1)S(1)} %get-tuple-element.56), channel_id=1, source_target_pairs={{0,8},{1,9},{2,10},{3,11},{4,12},{5,13},{6,14},{7,15},{8,0},{9,1},... | collective-permute-start | bytes 589832 | tf_op jit(solution)/shard_map/ppermute | solution.py:83
  34.4 0.7 %gradient.1 = (bf16[256,128]{1,0:T(8,128)(2,1)S(1)}, bf16[256,128]{1,0:T(8,128)(2,1)S(1)}, bf16[256,128]{1,0:T(8,128)(2,1)S(1)}, bf16[256,128]{1,0:T(8,128)(2,1)S(1)}) custom-call(bf16[128,768]{1,0:T(8,128)(2,1)S(1)} %copy-done.2, f32[1,768]{1,0:T(1,128)S(1)} %reshape.13.refs_1_, bf16[256,768]{1,0:T(8,128)(2,1)S(1)} %copy-done, ...), custom_call_target="tpu_custom_call" | custom-call | tf_op jit(solution)/shard_map/gradient/pallas_call | solution.py:37
  35.1 0.4 collective-permute-start.18
  35.5 1.0 %collective-permute-start.19 = (bf16[256,128]{1,0:T(8,128)(2,1)S(1)}, bf16[256,128]{1,0:T(8,128)(2,1)S(1)}, u32[]{:S(2)}, u32[]{:S(2)}) collective-permute-start(bf16[256,128]{1,0:T(8,128)(2,1)S(1)} %get-tuple-element.73), channel_id=1, source_target_pairs={{0,4},{1,5},{2,6},{3,7},{4,0},{5,1},{6,2},{7,3},{8,12},{9,13},{10,... | collective-permute-start | bytes 196616 | tf_op jit(solution)/shard_map/ppermute | solution.py:86
  36.4 3.1 %collective-permute-done.12.refs_3_ = bf16[768,128]{1,0:T(8,128)(2,1)S(1)} collective-permute-done((bf16[768,128]{1,0:T(8,128)(2,1)S(1)}, bf16[768,128]{1,0:T(8,128)(2,1)S(1)}, u32[]{:S(2)}, u32[]{:S(2)}) %collective-permute-start.12) | collective-permute-done | bytes 196640 | tf_op jit(solution)/shard_map/ppermute | solution.py:83
  39.6 0.6 collective-permute-start.20
  40.2 2.0 %collective-permute-done.13.refs_2_ = bf16[768,128]{1,0:T(8,128)(2,1)S(1)} collective-permute-done((bf16[768,128]{1,0:T(8,128)(2,1)S(1)}, bf16[768,128]{1,0:T(8,128)(2,1)S(1)}, u32[]{:S(2)}, u32[]{:S(2)}) %collective-permute-start.13) | collective-permute-done | bytes 196640 | tf_op jit(solution)/shard_map/ppermute | solution.py:83
  42.2 0.8 %collective-permute-done.14.refs_1_ = bf16[768,128]{1,0:T(8,128)(2,1)S(1)} collective-permute-done((bf16[768,128]{1,0:T(8,128)(2,1)S(1)}, bf16[768,128]{1,0:T(8,128)(2,1)S(1)}, u32[]{:S(2)}, u32[]{:S(2)}) %collective-permute-start.14) | collective-permute-done | bytes 196640 | tf_op jit(solution)/shard_map/ppermute | solution.py:83
  43.0 1.7 %attend.1 = (bf16[144,128]{1,0:T(8,128)(2,1)S(1)}, bf16[144,128]{1,0:T(8,128)(2,1)S(1)}, bf16[144,128]{1,0:T(8,128)(2,1)S(1)}, bf16[144,128]{1,0:T(8,128)(2,1)S(1)}) custom-call(bf16[768,128]{1,0:T(8,128)(2,1)S(1)} %get-tuple-element.53.refs_0_, bf16[768,128]{1,0:T(8,128)(2,1)S(1)} %collective-permute-done.14.refs_1_, ...), custom_call_target="tpu_custom_call" | custom-call | tf_op jit(solution)/shard_map/attend/pallas_call | solution.py:37
  44.8 0.4 collective-permute-start.15
  45.2 1.4 %collective-permute-start.16 = (bf16[144,128]{1,0:T(8,128)(2,1)S(1)}, bf16[144,128]{1,0:T(8,128)(2,1)S(1)}, u32[]{:S(2)}, u32[]{:S(2)}) collective-permute-start(bf16[144,128]{1,0:T(8,128)(2,1)S(1)} %get-tuple-element.65), channel_id=1, source_target_pairs={{0,16},{1,17},{2,18},{3,19},{4,20},{5,21},{6,22},{7,23},{8,24},{9,... | collective-permute-start | bytes 110600 | tf_op jit(solution)/shard_map/ppermute | solution.py:83
  46.6 1.7 %collective-permute-start.17 = (bf16[144,128]{1,0:T(8,128)(2,1)S(1)}, bf16[144,128]{1,0:T(8,128)(2,1)S(1)}, u32[]{:S(2)}, u32[]{:S(2)}) collective-permute-start(bf16[144,128]{1,0:T(8,128)(2,1)S(1)} %get-tuple-element.66), channel_id=1, source_target_pairs={{0,8},{1,9},{2,10},{3,11},{4,12},{5,13},{6,14},{7,15},{8,0},{9,1},... | collective-permute-start | bytes 110600 | tf_op jit(solution)/shard_map/ppermute | solution.py:83
  48.3 1.4 %collective-permute-done.15.refs_1_ = bf16[144,128]{1,0:T(8,128)(2,1)S(1)} collective-permute-done((bf16[144,128]{1,0:T(8,128)(2,1)S(1)}, bf16[144,128]{1,0:T(8,128)(2,1)S(1)}, u32[]{:S(2)}, u32[]{:S(2)}) %collective-permute-start.15) | collective-permute-done | bytes 36896 | tf_op jit(solution)/shard_map/ppermute | solution.py:83
  49.7 0.9 %collective-permute-done.17.refs_3_ = bf16[144,128]{1,0:T(8,128)(2,1)S(1)} collective-permute-done((bf16[144,128]{1,0:T(8,128)(2,1)S(1)}, bf16[144,128]{1,0:T(8,128)(2,1)S(1)}, u32[]{:S(2)}, u32[]{:S(2)}) %collective-permute-start.17) | collective-permute-done | bytes 36896 | tf_op jit(solution)/shard_map/ppermute | solution.py:83
  50.5 0.1 finish.1
  50.7 2.2 %collective-permute-start.23 = (bf16[128,128]{1,0:T(8,128)(2,1)S(1)}, bf16[128,128]{1,0:T(8,128)(2,1)S(1)}, u32[]{:S(2)}, u32[]{:S(2)}) collective-permute-start(bf16[128,128]{1,0:T(8,128)(2,1)S(1)} %get-tuple-element.84.refs_3_), channel_id=1, source_target_pairs={{0,6},{1,7},{2,4},{3,5},{4,2},{5,3},{6,0},{7,1},{8,14},{9,15},{10,... | collective-permute-start | bytes 98312 | tf_op jit(solution)/shard_map/ppermute | solution.py:86
  52.8 1.0 %collective-permute-start.22 = (bf16[128,128]{1,0:T(8,128)(2,1)S(1)}, bf16[128,128]{1,0:T(8,128)(2,1)S(1)}, u32[]{:S(2)}, u32[]{:S(2)}) collective-permute-start(bf16[128,128]{1,0:T(8,128)(2,1)S(1)} %get-tuple-element.84.refs_3_), channel_id=1, source_target_pairs={{0,4},{1,5},{2,6},{3,7},{4,0},{5,1},{6,2},{7,3},{8,12},{9,13},{10,... | collective-permute-start | bytes 98312 | tf_op jit(solution)/shard_map/ppermute | solution.py:86
  53.9 1.2 %collective-permute-start.21 = (bf16[128,128]{1,0:T(8,128)(2,1)S(1)}, bf16[128,128]{1,0:T(8,128)(2,1)S(1)}, u32[]{:S(2)}, u32[]{:S(2)}) collective-permute-start(bf16[128,128]{1,0:T(8,128)(2,1)S(1)} %get-tuple-element.84.refs_3_), channel_id=1, source_target_pairs={{0,2},{1,3},{2,0},{3,1},{4,6},{5,7},{6,4},{7,5},{8,10},{9,11},{10,... | collective-permute-start | bytes 98312 | tf_op jit(solution)/shard_map/ppermute | solution.py:86
  55.1 1.6 %collective-permute-done.23.refs_6_ = bf16[128,128]{1,0:T(8,128)(2,1)S(1)} collective-permute-done((bf16[128,128]{1,0:T(8,128)(2,1)S(1)}, bf16[128,128]{1,0:T(8,128)(2,1)S(1)}, u32[]{:S(2)}, u32[]{:S(2)}) %collective-permute-start.23) | collective-permute-done | bytes 32800 | tf_op jit(solution)/shard_map/ppermute | solution.py:86
  56.7 1.0 %collective-permute-done.22.refs_5_ = bf16[128,128]{1,0:T(8,128)(2,1)S(1)} collective-permute-done((bf16[128,128]{1,0:T(8,128)(2,1)S(1)}, bf16[128,128]{1,0:T(8,128)(2,1)S(1)}, u32[]{:S(2)}, u32[]{:S(2)}) %collective-permute-start.22) | collective-permute-done | bytes 32800 | tf_op jit(solution)/shard_map/ppermute | solution.py:86
  57.7 0.3 collective-permute-done.21.refs_4_
  58.0 0.2 collective-permute-start.25
  58.2 0.7 %collective-permute-done.26.refs_9_ = bf16[128,128]{1,0:T(8,128)(2,1)S(1)} collective-permute-done((bf16[128,128]{1,0:T(8,128)(2,1)S(1)}, bf16[128,128]{1,0:T(8,128)(2,1)S(1)}, u32[]{:S(2)}, u32[]{:S(2)}) %collective-permute-start.26) | collective-permute-done | bytes 32800 | tf_op jit(solution)/shard_map/ppermute | solution.py:80
  58.9 0.3 collective-permute-done.25.refs_8_
  59.2 1.1 %output.1 = (bf16[128,768]{1,0:T(8,128)(2,1)}, bf16[128,128]{1,0:T(8,128)(2,1)}) custom-call(bf16[128,768]{1,0:T(8,128)(2,1)S(1)} %copy-done.1, f32[1,768]{1,0:T(1,128)S(1)} %reshape.13.refs_1_, bf16[128,128]{1,0:T(8,128)(2,1)S(1)} %get-tuple-element.83.refs_2_, bf16[128,128]{1,0:T(8,128)(2,1)S(1)} %get-tuple-element.84.refs_3_, ...), custom_call_target="tpu_custom_call" | custom-call | tf_op jit(solution)/shard_map/output/pallas_call | solution.py:37
  (28 shorter events, 0.1 us)
Async XLA Ops:
  0.6 19.9 %collective-permute-start.5 = (bf16[256,768]{1,0:T(8,128)(2,1)}, bf16[256,768]{1,0:T(8,128)(2,1)S(1)}, u32[]{:S(2)}, u32[]{:S(2)}) collective-permute-start(bf16[256,768]{1,0:T(8,128)(2,1)} %refs_11_.1), channel_id=1, source_target_pairs={{0,16},{1,17},{2,18},{3,19},{4,20},{5,21},{6,22},{7,23},{8,24},{9,... | collective-permute-start | bytes 1179656 | tf_op jit(solution)/shard_map/ppermute | solution.py:83
  3.7 18.2 %collective-permute-start.4 = (bf16[256,768]{1,0:T(8,128)(2,1)}, bf16[256,768]{1,0:T(8,128)(2,1)S(1)}, u32[]{:S(2)}, u32[]{:S(2)}) collective-permute-start(bf16[256,768]{1,0:T(8,128)(2,1)} %refs_11_.1), channel_id=1, source_target_pairs={{0,8},{1,9},{2,10},{3,11},{4,12},{5,13},{6,14},{7,15},{8,0},{9,1},... | collective-permute-start | bytes 1179656 | tf_op jit(solution)/shard_map/ppermute | solution.py:83
  5.2 13.3 %collective-permute-start = (bf16[128,768]{1,0:T(8,128)(2,1)}, bf16[128,768]{1,0:T(8,128)(2,1)S(1)}, u32[]{:S(2)}, u32[]{:S(2)}) collective-permute-start(bf16[128,768]{1,0:T(8,128)(2,1)} %refs_0_.5), channel_id=1, source_target_pairs={{0,6},{1,7},{2,12},{3,13},{4,18},{5,19},{6,24},{7,25},{8,4},{9,5},... | collective-permute-start | bytes 589832 | tf_op jit(solution)/shard_map/ppermute | solution.py:89
  8.8 9.7 %collective-permute-start.1 = (bf16[128,768]{1,0:T(8,128)(2,1)}, bf16[128,768]{1,0:T(8,128)(2,1)S(1)}, u32[]{:S(2)}, u32[]{:S(2)}) collective-permute-start(bf16[128,768]{1,0:T(8,128)(2,1)} %refs_0_.5), channel_id=1, source_target_pairs={{0,1},{1,0},{2,10},{3,11},{4,20},{5,21},{6,30},{7,31},{8,2},{9,3},... | collective-permute-start | bytes 589832 | tf_op jit(solution)/shard_map/ppermute | solution.py:89
  18.5 7.8 %collective-permute-start.2 = (bf16[128,768]{1,0:T(8,128)(2,1)S(1)}, bf16[128,768]{1,0:T(8,128)(2,1)S(1)}, u32[]{:S(2)}, u32[]{:S(2)}) collective-permute-start(bf16[128,768]{1,0:T(8,128)(2,1)S(1)} %collective-permute-done.refs_0_), channel_id=1, source_target_pairs={{0,2},{1,3},{2,0},{3,1},{4,6},{5,7},{6,4},{7,5},{8,10},{9,11},{10,... | collective-permute-start | bytes 589832 | tf_op jit(solution)/shard_map/ppermute | solution.py:86
  18.5 10.0 %collective-permute-start.3 = (bf16[128,768]{1,0:T(8,128)(2,1)S(1)}, bf16[128,768]{1,0:T(8,128)(2,1)S(1)}, u32[]{:S(2)}, u32[]{:S(2)}) collective-permute-start(bf16[128,768]{1,0:T(8,128)(2,1)S(1)} %collective-permute-done.1.refs_1_), channel_id=1, source_target_pairs={{0,2},{1,3},{2,0},{3,1},{4,6},{5,7},{6,4},{7,5},{8,10},{9,11},{10,... | collective-permute-start | bytes 589832 | tf_op jit(solution)/shard_map/ppermute | solution.py:86
  20.5 7.9 %collective-permute-start.6 = (bf16[128,768]{1,0:T(8,128)(2,1)S(1)}, bf16[128,768]{1,0:T(8,128)(2,1)S(1)}, u32[]{:S(2)}, u32[]{:S(2)}) collective-permute-start(bf16[128,768]{1,0:T(8,128)(2,1)S(1)} %slice.8), channel_id=1, source_target_pairs={{0,8},{1,9},{2,10},{3,11},{4,12},{5,13},{6,14},{7,15},{8,0},{9,1},... | collective-permute-start | bytes 589832 | tf_op jit(solution)/shard_map/ppermute | solution.py:83
  21.8 7.1 %copy-start.3 = (f32[768]{0:T(1024)S(1)}, f32[768]{0:T(1024)}, u32[]{:S(2)}) copy-start(f32[768]{0:T(1024)} %param.20) | copy-start | bytes 9220
  21.8 6.6 %collective-permute-start.7 = (bf16[128,768]{1,0:T(8,128)(2,1)S(1)}, bf16[128,768]{1,0:T(8,128)(2,1)S(1)}, u32[]{:S(2)}, u32[]{:S(2)}) collective-permute-start(bf16[128,768]{1,0:T(8,128)(2,1)S(1)} %slice.9), channel_id=1, source_target_pairs={{0,16},{1,17},{2,18},{3,19},{4,20},{5,21},{6,22},{7,23},{8,24},{9,... | collective-permute-start | bytes 589832 | tf_op jit(solution)/shard_map/ppermute | solution.py:83
  24.4 4.6 %collective-permute-start.10 = (bf16[128,768]{1,0:T(8,128)(2,1)S(1)}, bf16[128,768]{1,0:T(8,128)(2,1)S(1)}, u32[]{:S(2)}, u32[]{:S(2)}) collective-permute-start(bf16[128,768]{1,0:T(8,128)(2,1)S(1)} %collective-permute-done.refs_0_), channel_id=1, source_target_pairs={{0,1},{1,0},{2,3},{3,2},{4,5},{5,4},{6,7},{7,6},{8,9},{9,8},{10,11... | collective-permute-start | bytes 589832 | tf_op jit(solution)/shard_map/ppermute | solution.py:80
  26.3 2.7 %collective-permute-start.11 = (bf16[128,768]{1,0:T(8,128)(2,1)S(1)}, bf16[128,768]{1,0:T(8,128)(2,1)S(1)}, u32[]{:S(2)}, u32[]{:S(2)}) collective-permute-start(bf16[128,768]{1,0:T(8,128)(2,1)S(1)} %collective-permute-done.1.refs_1_), channel_id=1, source_target_pairs={{0,1},{1,0},{2,3},{3,2},{4,5},{5,4},{6,7},{7,6},{8,9},{9,8},{10,11... | collective-permute-start | bytes 589832 | tf_op jit(solution)/shard_map/ppermute | solution.py:80
  28.4 1.4 %collective-permute-start.8 = (bf16[128,768]{1,0:T(8,128)(2,1)S(1)}, bf16[128,768]{1,0:T(8,128)(2,1)S(1)}, u32[]{:S(2)}, u32[]{:S(2)}) collective-permute-start(bf16[128,768]{1,0:T(8,128)(2,1)S(1)} %collective-permute-done.2.refs_0_), channel_id=1, source_target_pairs={{0,1},{1,0},{2,3},{3,2},{4,5},{5,4},{6,7},{7,6},{8,9},{9,8},{10,11... | collective-permute-start | bytes 589832 | tf_op jit(solution)/shard_map/ppermute | solution.py:80
  28.5 1.7 %collective-permute-start.9 = (bf16[128,768]{1,0:T(8,128)(2,1)S(1)}, bf16[128,768]{1,0:T(8,128)(2,1)S(1)}, u32[]{:S(2)}, u32[]{:S(2)}) collective-permute-start(bf16[128,768]{1,0:T(8,128)(2,1)S(1)} %collective-permute-done.3.refs_1_), channel_id=1, source_target_pairs={{0,1},{1,0},{2,3},{3,2},{4,5},{5,4},{6,7},{7,6},{8,9},{9,8},{10,11... | collective-permute-start | bytes 589832 | tf_op jit(solution)/shard_map/ppermute | solution.py:80
  29.6 4.8 %copy-start = (bf16[256,768]{1,0:T(8,128)(2,1)S(1)}, bf16[256,768]{1,0:T(8,128)(2,1)}, u32[]{:S(2)}) copy-start(bf16[256,768]{1,0:T(8,128)(2,1)} %refs_11_.1) | copy-start | bytes 1179652
  29.6 4.8 %copy-start.2 = (bf16[128,768]{1,0:T(8,128)(2,1)S(1)}, bf16[128,768]{1,0:T(8,128)(2,1)}, u32[]{:S(2)}) copy-start(bf16[128,768]{1,0:T(8,128)(2,1)} %refs_0_.4) | copy-start | bytes 589828
  30.8 8.7 %collective-permute-start.12 = (bf16[768,128]{1,0:T(8,128)(2,1)S(1)}, bf16[768,128]{1,0:T(8,128)(2,1)S(1)}, u32[]{:S(2)}, u32[]{:S(2)}) collective-permute-start(bf16[768,128]{1,0:T(8,128)(2,1)S(1)} %get-tuple-element.54), channel_id=1, source_target_pairs={{0,24},{1,25},{2,26},{3,27},{4,28},{5,29},{6,30},{7,31},{8,16},{9,... | collective-permute-start | bytes 589832 | tf_op jit(solution)/shard_map/ppermute | solution.py:83
  30.9 11.3 %collective-permute-start.13 = (bf16[768,128]{1,0:T(8,128)(2,1)S(1)}, bf16[768,128]{1,0:T(8,128)(2,1)S(1)}, u32[]{:S(2)}, u32[]{:S(2)}) collective-permute-start(bf16[768,128]{1,0:T(8,128)(2,1)S(1)} %get-tuple-element.55), channel_id=1, source_target_pairs={{0,16},{1,17},{2,18},{3,19},{4,20},{5,21},{6,22},{7,23},{8,24},{9,... | collective-permute-start | bytes 589832 | tf_op jit(solution)/shard_map/ppermute | solution.py:83
  32.6 10.4 %collective-permute-start.14 = (bf16[768,128]{1,0:T(8,128)(2,1)S(1)}, bf16[768,128]{1,0:T(8,128)(2,1)S(1)}, u32[]{:S(2)}, u32[]{:S(2)}) collective-permute-start(bf16[768,128]{1,0:T(8,128)(2,1)S(1)} %get-tuple-element.56), channel_id=1, source_target_pairs={{0,8},{1,9},{2,10},{3,11},{4,12},{5,13},{6,14},{7,15},{8,0},{9,1},... | collective-permute-start | bytes 589832 | tf_op jit(solution)/shard_map/ppermute | solution.py:83
  35.1 11.5 %collective-permute-start.18 = (bf16[256,128]{1,0:T(8,128)(2,1)S(1)}, bf16[256,128]{1,0:T(8,128)(2,1)S(1)}, u32[]{:S(2)}, u32[]{:S(2)}) collective-permute-start(bf16[256,128]{1,0:T(8,128)(2,1)S(1)} %get-tuple-element.72), channel_id=1, source_target_pairs={{0,2},{1,3},{2,0},{3,1},{4,6},{5,7},{6,4},{7,5},{8,10},{9,11},{10,... | collective-permute-start | bytes 196616 | tf_op jit(solution)/shard_map/ppermute | solution.py:86
  35.5 12.9 %collective-permute-start.19 = (bf16[256,128]{1,0:T(8,128)(2,1)S(1)}, bf16[256,128]{1,0:T(8,128)(2,1)S(1)}, u32[]{:S(2)}, u32[]{:S(2)}) collective-permute-start(bf16[256,128]{1,0:T(8,128)(2,1)S(1)} %get-tuple-element.73), channel_id=1, source_target_pairs={{0,4},{1,5},{2,6},{3,7},{4,0},{5,1},{6,2},{7,3},{8,12},{9,13},{10,... | collective-permute-start | bytes 196616 | tf_op jit(solution)/shard_map/ppermute | solution.py:86
  39.6 8.8 %collective-permute-start.20 = (bf16[256,128]{1,0:T(8,128)(2,1)S(1)}, bf16[256,128]{1,0:T(8,128)(2,1)S(1)}, u32[]{:S(2)}, u32[]{:S(2)}) collective-permute-start(bf16[256,128]{1,0:T(8,128)(2,1)S(1)} %get-tuple-element.74), channel_id=1, source_target_pairs={{0,6},{1,7},{2,4},{3,5},{4,2},{5,3},{6,0},{7,1},{8,14},{9,15},{10,... | collective-permute-start | bytes 196616 | tf_op jit(solution)/shard_map/ppermute | solution.py:86
  43.0 16.2 %copy-start.1 = (bf16[128,768]{1,0:T(8,128)(2,1)S(1)}, bf16[128,768]{1,0:T(8,128)(2,1)}, u32[]{:S(2)}) copy-start(bf16[128,768]{1,0:T(8,128)(2,1)} %refs_0_.5) | copy-start | bytes 589828
  44.8 4.9 %collective-permute-start.15 = (bf16[144,128]{1,0:T(8,128)(2,1)S(1)}, bf16[144,128]{1,0:T(8,128)(2,1)S(1)}, u32[]{:S(2)}, u32[]{:S(2)}) collective-permute-start(bf16[144,128]{1,0:T(8,128)(2,1)S(1)} %get-tuple-element.64), channel_id=1, source_target_pairs={{0,24},{1,25},{2,26},{3,27},{4,28},{5,29},{6,30},{7,31},{8,16},{9,... | collective-permute-start | bytes 110600 | tf_op jit(solution)/shard_map/ppermute | solution.py:83
  45.2 4.5 %collective-permute-start.16 = (bf16[144,128]{1,0:T(8,128)(2,1)S(1)}, bf16[144,128]{1,0:T(8,128)(2,1)S(1)}, u32[]{:S(2)}, u32[]{:S(2)}) collective-permute-start(bf16[144,128]{1,0:T(8,128)(2,1)S(1)} %get-tuple-element.65), channel_id=1, source_target_pairs={{0,16},{1,17},{2,18},{3,19},{4,20},{5,21},{6,22},{7,23},{8,24},{9,... | collective-permute-start | bytes 110600 | tf_op jit(solution)/shard_map/ppermute | solution.py:83
  46.6 4.0 %collective-permute-start.17 = (bf16[144,128]{1,0:T(8,128)(2,1)S(1)}, bf16[144,128]{1,0:T(8,128)(2,1)S(1)}, u32[]{:S(2)}, u32[]{:S(2)}) collective-permute-start(bf16[144,128]{1,0:T(8,128)(2,1)S(1)} %get-tuple-element.66), channel_id=1, source_target_pairs={{0,8},{1,9},{2,10},{3,11},{4,12},{5,13},{6,14},{7,15},{8,0},{9,1},... | collective-permute-start | bytes 110600 | tf_op jit(solution)/shard_map/ppermute | solution.py:83
  50.7 6.0 %collective-permute-start.23 = (bf16[128,128]{1,0:T(8,128)(2,1)S(1)}, bf16[128,128]{1,0:T(8,128)(2,1)S(1)}, u32[]{:S(2)}, u32[]{:S(2)}) collective-permute-start(bf16[128,128]{1,0:T(8,128)(2,1)S(1)} %get-tuple-element.84.refs_3_), channel_id=1, source_target_pairs={{0,6},{1,7},{2,4},{3,5},{4,2},{5,3},{6,0},{7,1},{8,14},{9,15},{10,... | collective-permute-start | bytes 98312 | tf_op jit(solution)/shard_map/ppermute | solution.py:86
  52.8 4.8 %collective-permute-start.22 = (bf16[128,128]{1,0:T(8,128)(2,1)S(1)}, bf16[128,128]{1,0:T(8,128)(2,1)S(1)}, u32[]{:S(2)}, u32[]{:S(2)}) collective-permute-start(bf16[128,128]{1,0:T(8,128)(2,1)S(1)} %get-tuple-element.84.refs_3_), channel_id=1, source_target_pairs={{0,4},{1,5},{2,6},{3,7},{4,0},{5,1},{6,2},{7,3},{8,12},{9,13},{10,... | collective-permute-start | bytes 98312 | tf_op jit(solution)/shard_map/ppermute | solution.py:86
  53.9 4.1 %collective-permute-start.21 = (bf16[128,128]{1,0:T(8,128)(2,1)S(1)}, bf16[128,128]{1,0:T(8,128)(2,1)S(1)}, u32[]{:S(2)}, u32[]{:S(2)}) collective-permute-start(bf16[128,128]{1,0:T(8,128)(2,1)S(1)} %get-tuple-element.84.refs_3_), channel_id=1, source_target_pairs={{0,2},{1,3},{2,0},{3,1},{4,6},{5,7},{6,4},{7,5},{8,10},{9,11},{10,... | collective-permute-start | bytes 98312 | tf_op jit(solution)/shard_map/ppermute | solution.py:86
  55.1 4.1 %collective-permute-start.24 = (bf16[256,128]{1,0:T(8,128)(2,1)S(1)}, bf16[256,128]{1,0:T(8,128)(2,1)S(1)}, u32[]{:S(2)}, u32[]{:S(2)}) collective-permute-start(bf16[256,128]{1,0:T(8,128)(2,1)S(1)} %get-tuple-element.85), channel_id=1, source_target_pairs={{0,1},{1,0},{2,3},{3,2},{4,5},{5,4},{6,7},{7,6},{8,9},{9,8},{10,11... | collective-permute-start | bytes 196616 | tf_op jit(solution)/shard_map/ppermute | solution.py:80
  56.7 1.5 %collective-permute-start.27 = (bf16[128,128]{1,0:T(8,128)(2,1)S(1)}, bf16[128,128]{1,0:T(8,128)(2,1)S(1)}, u32[]{:S(2)}, u32[]{:S(2)}) collective-permute-start(bf16[128,128]{1,0:T(8,128)(2,1)S(1)} %collective-permute-done.23.refs_6_), channel_id=1, source_target_pairs={{0,1},{1,0},{2,3},{3,2},{4,5},{5,4},{6,7},{7,6},{8,9},{9,8},{10,11... | collective-permute-start | bytes 98312 | tf_op jit(solution)/shard_map/ppermute | solution.py:80
  57.7 1.2 %collective-permute-start.26 = (bf16[128,128]{1,0:T(8,128)(2,1)S(1)}, bf16[128,128]{1,0:T(8,128)(2,1)S(1)}, u32[]{:S(2)}, u32[]{:S(2)}) collective-permute-start(bf16[128,128]{1,0:T(8,128)(2,1)S(1)} %collective-permute-done.22.refs_5_), channel_id=1, source_target_pairs={{0,1},{1,0},{2,3},{3,2},{4,5},{5,4},{6,7},{7,6},{8,9},{9,8},{10,11... | collective-permute-start | bytes 98312 | tf_op jit(solution)/shard_map/ppermute | solution.py:80
  58.0 1.2 %collective-permute-start.25 = (bf16[128,128]{1,0:T(8,128)(2,1)S(1)}, bf16[128,128]{1,0:T(8,128)(2,1)S(1)}, u32[]{:S(2)}, u32[]{:S(2)}) collective-permute-start(bf16[128,128]{1,0:T(8,128)(2,1)S(1)} %collective-permute-done.21.refs_4_), channel_id=1, source_target_pairs={{0,1},{1,0},{2,3},{3,2},{4,5},{5,4},{6,7},{7,6},{8,9},{9,8},{10,11... | collective-permute-start | bytes 98312 | tf_op jit(solution)/shard_map/ppermute | solution.py:80

commit v8 on v7

--- a/solution.py
+++ b/solution.py
@@ -255,7 +255,7 @@
             key_new = normed(total(slice(R * T, (R + 1) * T)), gain_ref[1:2, :]).astype(bf16)
             value_new = total(slice((R + 1) * T, (R + 2) * T)).astype(bf16)
             value_new = jnp.concatenate([value_new, jnp.ones_like(value_new)], axis=1)
-            step = min(512, cached)
+            step = min(2048, cached)
             eye = lax.broadcasted_iota(jnp.int32, (T, H), 0) == lax.broadcasted_iota(
                 jnp.int32, (T, H), 1
             )

time: 60.5 us -> 60.7 us (level)
  no operation moved by 1% of the time
where the time goes in v8:
time: 60.7 us; the launch traced here: 60.5 us
  waiting for transfers between devices  26.3 us (43%)
  starting transfers between devices  25.8 us (43%)
  Pallas kernels  7.53 us (12%)
  between operations  0.79 us (1%)
    ppermute x10, starting transfers between devices, over_row(): return lax.ppermute(x, both, route(lambda r, z, q: (r ^ s, z, q)))  13 us
    ppermute x2, waiting for transfers between devices, turned(): lax.ppermute(x, both, route(lambda r, z, q: (z, r ^ z ^ d, q ^ (r == z ==...  9.7 us
    ppermute x8, starting transfers between devices, over_z(): return lax.ppermute(x, both, route(lambda r, z, q: (r, z ^ m, q)))  8.39 us
    ppermute x10, waiting for transfers between devices, over_row(): return lax.ppermute(x, both, route(lambda r, z, q: (r ^ s, z, q)))  8.22 us
    pallas_call x7, Pallas kernels, call(): pl.pallas_call(fetch if far else kernel, out_shape=list(outs), in_specs=[...  7.53 us
    ppermute x8, waiting for transfers between devices, over_z(): return lax.ppermute(x, both, route(lambda r, z, q: (r, z ^ m, q)))  6.85 us
    ppermute x2, starting transfers between devices, turned(): lax.ppermute(x, both, route(lambda r, z, q: (z, r ^ z ^ d, q ^ (r == z ==...  3.6 us
    ppermute x8, waiting for transfers between devices, across_chip(): return lax.ppermute(x, both, route(lambda r, z, q: (r, z, q ^ 1)))  1.58 us
  transfers between devices with their start and end apart: 28, of which 15 were waited for; matrix products, arithmetic and copies ran while one was open for 0% of the time, Pallas kernels for 9%

profile of v8, /device:TPU:0, one launch (start us, length us, event | category | flops | bytes accessed | tf_op | source)
XLA Modules:
  0.0 60.5 jit_solution(16171437867861225187)
XLA Ops:
  0.6 3.0 %collective-permute-start.5 = (bf16[256,768]{1,0:T(8,128)(2,1)}, bf16[256,768]{1,0:T(8,128)(2,1)S(1)}, u32[]{:S(2)}, u32[]{:S(2)}) collective-permute-start(bf16[256,768]{1,0:T(8,128)(2,1)} %refs_11_.1), channel_id=1, source_target_pairs={{0,16},{1,17},{2,18},{3,19},{4,20},{5,21},{6,22},{7,23},{8,24},{9,... | collective-permute-start | bytes 1179656 | tf_op jit(solution)/shard_map/ppermute | solution.py:83
  3.7 1.5 %collective-permute-start.4 = (bf16[256,768]{1,0:T(8,128)(2,1)}, bf16[256,768]{1,0:T(8,128)(2,1)S(1)}, u32[]{:S(2)}, u32[]{:S(2)}) collective-permute-start(bf16[256,768]{1,0:T(8,128)(2,1)} %refs_11_.1), channel_id=1, source_target_pairs={{0,8},{1,9},{2,10},{3,11},{4,12},{5,13},{6,14},{7,15},{8,0},{9,1},... | collective-permute-start | bytes 1179656 | tf_op jit(solution)/shard_map/ppermute | solution.py:83
  5.2 3.6 %collective-permute-start = (bf16[128,768]{1,0:T(8,128)(2,1)}, bf16[128,768]{1,0:T(8,128)(2,1)S(1)}, u32[]{:S(2)}, u32[]{:S(2)}) collective-permute-start(bf16[128,768]{1,0:T(8,128)(2,1)} %refs_0_.5), channel_id=1, source_target_pairs={{0,6},{1,7},{2,12},{3,13},{4,18},{5,19},{6,24},{7,25},{8,4},{9,5},... | collective-permute-start | bytes 589832 | tf_op jit(solution)/shard_map/ppermute | solution.py:89
  8.8 0.0 collective-permute-start.1
  8.8 9.7 %collective-permute-done.refs_0_ = bf16[128,768]{1,0:T(8,128)(2,1)S(1)} collective-permute-done((bf16[128,768]{1,0:T(8,128)(2,1)}, bf16[128,768]{1,0:T(8,128)(2,1)S(1)}, u32[]{:S(2)}, u32[]{:S(2)}) %collective-permute-start) | collective-permute-done | bytes 196640 | tf_op jit(solution)/shard_map/ppermute | solution.py:89
  18.5 0.0 collective-permute-start.2
  18.5 2.0 %collective-permute-start.3 = (bf16[128,768]{1,0:T(8,128)(2,1)S(1)}, bf16[128,768]{1,0:T(8,128)(2,1)S(1)}, u32[]{:S(2)}, u32[]{:S(2)}) collective-permute-start(bf16[128,768]{1,0:T(8,128)(2,1)S(1)} %collective-permute-done.1.refs_1_), channel_id=1, source_target_pairs={{0,2},{1,3},{2,0},{3,1},{4,6},{5,7},{6,4},{7,5},{8,10},{9,11},{10,... | collective-permute-start | bytes 589832 | tf_op jit(solution)/shard_map/ppermute | solution.py:86
  20.5 1.3 %collective-permute-start.6 = (bf16[128,768]{1,0:T(8,128)(2,1)S(1)}, bf16[128,768]{1,0:T(8,128)(2,1)S(1)}, u32[]{:S(2)}, u32[]{:S(2)}) collective-permute-start(bf16[128,768]{1,0:T(8,128)(2,1)S(1)} %slice.8), channel_id=1, source_target_pairs={{0,8},{1,9},{2,10},{3,11},{4,12},{5,13},{6,14},{7,15},{8,0},{9,1},... | collective-permute-start | bytes 589832 | tf_op jit(solution)/shard_map/ppermute | solution.py:83
  21.8 0.0 copy-start.3
  21.8 0.1 collective-permute-start.7
  21.9 2.5 %prepare.1 = (bf16[128,2048]{1,0:T(8,128)(2,1)S(1)}, bf16[2048,256]{1,0:T(8,128)(2,1)S(1)}, bf16[1536,384]{1,0:T(8,128)(2,1)S(1)}, f32[2,128]{1,0:T(2,128)S(1)}) custom-call(bf16[2048,128]{1,0:T(8,128)(2,1)} %refs_0_.3, bf16[2048,128]{1,0:T(8,128)(2,1)} %refs_1_.1, bf16[1536,128]{1,0:T(8,128)(2,1)} %refs_2_.2, bf16[1536,128]{1,0:T(8,128)(2,1)} %refs_3_.1, ...), custom_call_target="tpu_custom_call" | custom-call | tf_op jit(solution)/shard_map/prepare/pallas_call | solution.py:37
  24.4 0.1 collective-permute-start.10
  24.5 1.8 %collective-permute-done.2.refs_0_ = bf16[128,768]{1,0:T(8,128)(2,1)S(1)} collective-permute-done((bf16[128,768]{1,0:T(8,128)(2,1)S(1)}, bf16[128,768]{1,0:T(8,128)(2,1)S(1)}, u32[]{:S(2)}, u32[]{:S(2)}) %collective-permute-start.2) | collective-permute-done | bytes 196640 | tf_op jit(solution)/shard_map/ppermute | solution.py:86
  26.3 2.1 %collective-permute-done.3.refs_1_ = bf16[128,768]{1,0:T(8,128)(2,1)S(1)} collective-permute-done((bf16[128,768]{1,0:T(8,128)(2,1)S(1)}, bf16[128,768]{1,0:T(8,128)(2,1)S(1)}, u32[]{:S(2)}, u32[]{:S(2)}) %collective-permute-start.3) | collective-permute-done | bytes 196640 | tf_op jit(solution)/shard_map/ppermute | solution.py:86
  28.5 0.5 collective-permute-start.9
  29.0 0.6 project_direct.1.refs_4_
  29.6 0.0 copy-start
  29.6 0.0 copy-start.2
  29.6 0.3 collective-permute-done.8.refs_2_
  29.9 0.3 collective-permute-done.9.refs_3_
  30.2 0.6 %project.1 = (bf16[768,128]{1,0:T(8,128)(2,1)S(1)}, bf16[768,128]{1,0:T(8,128)(2,1)S(1)}, bf16[768,128]{1,0:T(8,128)(2,1)S(1)}, bf16[768,128]{1,0:T(8,128)(2,1)S(1)}) custom-call(bf16[128,768]{1,0:T(8,128)(2,1)S(1)} %collective-permute-done.2.refs_0_, bf16[128,768]{1,0:T(8,128)(2,1)S(1)} %collective-permute-done.3.refs_1_, ...), custom_call_target="tpu_custom_call" | custom-call | tf_op jit(solution)/shard_map/project/pallas_call | solution.py:37
  30.8 0.1 collective-permute-start.12
  30.9 1.7 %collective-permute-start.13 = (bf16[768,128]{1,0:T(8,128)(2,1)S(1)}, bf16[768,128]{1,0:T(8,128)(2,1)S(1)}, u32[]{:S(2)}, u32[]{:S(2)}) collective-permute-start(bf16[768,128]{1,0:T(8,128)(2,1)S(1)} %get-tuple-element.55), channel_id=1, source_target_pairs={{0,16},{1,17},{2,18},{3,19},{4,20},{5,21},{6,22},{7,23},{8,24},{9,... | collective-permute-start | bytes 589832 | tf_op jit(solution)/shard_map/ppermute | solution.py:83
  32.6 1.7 %collective-permute-start.14 = (bf16[768,128]{1,0:T(8,128)(2,1)S(1)}, bf16[768,128]{1,0:T(8,128)(2,1)S(1)}, u32[]{:S(2)}, u32[]{:S(2)}) collective-permute-start(bf16[768,128]{1,0:T(8,128)(2,1)S(1)} %get-tuple-element.56), channel_id=1, source_target_pairs={{0,8},{1,9},{2,10},{3,11},{4,12},{5,13},{6,14},{7,15},{8,0},{9,1},... | collective-permute-start | bytes 589832 | tf_op jit(solution)/shard_map/ppermute | solution.py:83
  34.4 0.7 %gradient.1 = (bf16[256,128]{1,0:T(8,128)(2,1)S(1)}, bf16[256,128]{1,0:T(8,128)(2,1)S(1)}, bf16[256,128]{1,0:T(8,128)(2,1)S(1)}, bf16[256,128]{1,0:T(8,128)(2,1)S(1)}) custom-call(bf16[128,768]{1,0:T(8,128)(2,1)S(1)} %copy-done.2, f32[1,768]{1,0:T(1,128)S(1)} %reshape.13.refs_1_, bf16[256,768]{1,0:T(8,128)(2,1)S(1)} %copy-done, ...), custom_call_target="tpu_custom_call" | custom-call | tf_op jit(solution)/shard_map/gradient/pallas_call | solution.py:37
  35.1 0.4 collective-permute-start.18
  35.5 1.0 %collective-permute-start.19 = (bf16[256,128]{1,0:T(8,128)(2,1)S(1)}, bf16[256,128]{1,0:T(8,128)(2,1)S(1)}, u32[]{:S(2)}, u32[]{:S(2)}) collective-permute-start(bf16[256,128]{1,0:T(8,128)(2,1)S(1)} %get-tuple-element.73), channel_id=1, source_target_pairs={{0,4},{1,5},{2,6},{3,7},{4,0},{5,1},{6,2},{7,3},{8,12},{9,13},{10,... | collective-permute-start | bytes 196616 | tf_op jit(solution)/shard_map/ppermute | solution.py:86
  36.4 3.1 %collective-permute-done.12.refs_3_ = bf16[768,128]{1,0:T(8,128)(2,1)S(1)} collective-permute-done((bf16[768,128]{1,0:T(8,128)(2,1)S(1)}, bf16[768,128]{1,0:T(8,128)(2,1)S(1)}, u32[]{:S(2)}, u32[]{:S(2)}) %collective-permute-start.12) | collective-permute-done | bytes 196640 | tf_op jit(solution)/shard_map/ppermute | solution.py:83
  39.6 0.6 collective-permute-start.20
  40.2 2.0 %collective-permute-done.13.refs_2_ = bf16[768,128]{1,0:T(8,128)(2,1)S(1)} collective-permute-done((bf16[768,128]{1,0:T(8,128)(2,1)S(1)}, bf16[768,128]{1,0:T(8,128)(2,1)S(1)}, u32[]{:S(2)}, u32[]{:S(2)}) %collective-permute-start.13) | collective-permute-done | bytes 196640 | tf_op jit(solution)/shard_map/ppermute | solution.py:83
  42.2 0.8 %collective-permute-done.14.refs_1_ = bf16[768,128]{1,0:T(8,128)(2,1)S(1)} collective-permute-done((bf16[768,128]{1,0:T(8,128)(2,1)S(1)}, bf16[768,128]{1,0:T(8,128)(2,1)S(1)}, u32[]{:S(2)}, u32[]{:S(2)}) %collective-permute-start.14) | collective-permute-done | bytes 196640 | tf_op jit(solution)/shard_map/ppermute | solution.py:83
  43.0 1.9 %attend.1 = (bf16[144,128]{1,0:T(8,128)(2,1)S(1)}, bf16[144,128]{1,0:T(8,128)(2,1)S(1)}, bf16[144,128]{1,0:T(8,128)(2,1)S(1)}, bf16[144,128]{1,0:T(8,128)(2,1)S(1)}) custom-call(bf16[768,128]{1,0:T(8,128)(2,1)S(1)} %get-tuple-element.53.refs_0_, bf16[768,128]{1,0:T(8,128)(2,1)S(1)} %collective-permute-done.14.refs_1_, ...), custom_call_target="tpu_custom_call" | custom-call | tf_op jit(solution)/shard_map/attend/pallas_call | solution.py:37
  45.0 0.4 collective-permute-start.15
  45.4 1.4 %collective-permute-start.16 = (bf16[144,128]{1,0:T(8,128)(2,1)S(1)}, bf16[144,128]{1,0:T(8,128)(2,1)S(1)}, u32[]{:S(2)}, u32[]{:S(2)}) collective-permute-start(bf16[144,128]{1,0:T(8,128)(2,1)S(1)} %get-tuple-element.65), channel_id=1, source_target_pairs={{0,16},{1,17},{2,18},{3,19},{4,20},{5,21},{6,22},{7,23},{8,24},{9,... | collective-permute-start | bytes 110600 | tf_op jit(solution)/shard_map/ppermute | solution.py:83
  46.8 1.7 %collective-permute-start.17 = (bf16[144,128]{1,0:T(8,128)(2,1)S(1)}, bf16[144,128]{1,0:T(8,128)(2,1)S(1)}, u32[]{:S(2)}, u32[]{:S(2)}) collective-permute-start(bf16[144,128]{1,0:T(8,128)(2,1)S(1)} %get-tuple-element.66), channel_id=1, source_target_pairs={{0,8},{1,9},{2,10},{3,11},{4,12},{5,13},{6,14},{7,15},{8,0},{9,1},... | collective-permute-start | bytes 110600 | tf_op jit(solution)/shard_map/ppermute | solution.py:83
  48.5 1.4 %collective-permute-done.15.refs_1_ = bf16[144,128]{1,0:T(8,128)(2,1)S(1)} collective-permute-done((bf16[144,128]{1,0:T(8,128)(2,1)S(1)}, bf16[144,128]{1,0:T(8,128)(2,1)S(1)}, u32[]{:S(2)}, u32[]{:S(2)}) %collective-permute-start.15) | collective-permute-done | bytes 36896 | tf_op jit(solution)/shard_map/ppermute | solution.py:83
  49.9 0.9 %collective-permute-done.17.refs_3_ = bf16[144,128]{1,0:T(8,128)(2,1)S(1)} collective-permute-done((bf16[144,128]{1,0:T(8,128)(2,1)S(1)}, bf16[144,128]{1,0:T(8,128)(2,1)S(1)}, u32[]{:S(2)}, u32[]{:S(2)}) %collective-permute-start.17) | collective-permute-done | bytes 36896 | tf_op jit(solution)/shard_map/ppermute | solution.py:83
  50.8 0.1 finish.1
  50.9 2.2 %collective-permute-start.23 = (bf16[128,128]{1,0:T(8,128)(2,1)S(1)}, bf16[128,128]{1,0:T(8,128)(2,1)S(1)}, u32[]{:S(2)}, u32[]{:S(2)}) collective-permute-start(bf16[128,128]{1,0:T(8,128)(2,1)S(1)} %get-tuple-element.84.refs_3_), channel_id=1, source_target_pairs={{0,6},{1,7},{2,4},{3,5},{4,2},{5,3},{6,0},{7,1},{8,14},{9,15},{10,... | collective-permute-start | bytes 98312 | tf_op jit(solution)/shard_map/ppermute | solution.py:86
  53.0 1.0 %collective-permute-start.22 = (bf16[128,128]{1,0:T(8,128)(2,1)S(1)}, bf16[128,128]{1,0:T(8,128)(2,1)S(1)}, u32[]{:S(2)}, u32[]{:S(2)}) collective-permute-start(bf16[128,128]{1,0:T(8,128)(2,1)S(1)} %get-tuple-element.84.refs_3_), channel_id=1, source_target_pairs={{0,4},{1,5},{2,6},{3,7},{4,0},{5,1},{6,2},{7,3},{8,12},{9,13},{10,... | collective-permute-start | bytes 98312 | tf_op jit(solution)/shard_map/ppermute | solution.py:86
  54.1 1.2 %collective-permute-start.21 = (bf16[128,128]{1,0:T(8,128)(2,1)S(1)}, bf16[128,128]{1,0:T(8,128)(2,1)S(1)}, u32[]{:S(2)}, u32[]{:S(2)}) collective-permute-start(bf16[128,128]{1,0:T(8,128)(2,1)S(1)} %get-tuple-element.84.refs_3_), channel_id=1, source_target_pairs={{0,2},{1,3},{2,0},{3,1},{4,6},{5,7},{6,4},{7,5},{8,10},{9,11},{10,... | collective-permute-start | bytes 98312 | tf_op jit(solution)/shard_map/ppermute | solution.py:86
  55.3 1.6 %collective-permute-done.23.refs_6_ = bf16[128,128]{1,0:T(8,128)(2,1)S(1)} collective-permute-done((bf16[128,128]{1,0:T(8,128)(2,1)S(1)}, bf16[128,128]{1,0:T(8,128)(2,1)S(1)}, u32[]{:S(2)}, u32[]{:S(2)}) %collective-permute-start.23) | collective-permute-done | bytes 32800 | tf_op jit(solution)/shard_map/ppermute | solution.py:86
  56.9 1.0 %collective-permute-done.22.refs_5_ = bf16[128,128]{1,0:T(8,128)(2,1)S(1)} collective-permute-done((bf16[128,128]{1,0:T(8,128)(2,1)S(1)}, bf16[128,128]{1,0:T(8,128)(2,1)S(1)}, u32[]{:S(2)}, u32[]{:S(2)}) %collective-permute-start.22) | collective-permute-done | bytes 32800 | tf_op jit(solution)/shard_map/ppermute | solution.py:86
  57.9 0.3 collective-permute-done.21.refs_4_
  58.2 0.2 collective-permute-start.25
  58.4 0.7 %collective-permute-done.26.refs_9_ = bf16[128,128]{1,0:T(8,128)(2,1)S(1)} collective-permute-done((bf16[128,128]{1,0:T(8,128)(2,1)S(1)}, bf16[128,128]{1,0:T(8,128)(2,1)S(1)}, u32[]{:S(2)}, u32[]{:S(2)}) %collective-permute-start.26) | collective-permute-done | bytes 32800 | tf_op jit(solution)/shard_map/ppermute | solution.py:80
  59.1 0.3 collective-permute-done.25.refs_8_
  59.4 1.1 %output.1 = (bf16[128,768]{1,0:T(8,128)(2,1)}, bf16[128,128]{1,0:T(8,128)(2,1)}) custom-call(bf16[128,768]{1,0:T(8,128)(2,1)S(1)} %copy-done.1, f32[1,768]{1,0:T(1,128)S(1)} %reshape.13.refs_1_, bf16[128,128]{1,0:T(8,128)(2,1)S(1)} %get-tuple-element.83.refs_2_, bf16[128,128]{1,0:T(8,128)(2,1)S(1)} %get-tuple-element.84.refs_3_, ...), custom_call_target="tpu_custom_call" | custom-call | tf_op jit(solution)/shard_map/output/pallas_call | solution.py:37
  (28 shorter events, 0.1 us)
Async XLA Ops:
  0.6 19.9 %collective-permute-start.5 = (bf16[256,768]{1,0:T(8,128)(2,1)}, bf16[256,768]{1,0:T(8,128)(2,1)S(1)}, u32[]{:S(2)}, u32[]{:S(2)}) collective-permute-start(bf16[256,768]{1,0:T(8,128)(2,1)} %refs_11_.1), channel_id=1, source_target_pairs={{0,16},{1,17},{2,18},{3,19},{4,20},{5,21},{6,22},{7,23},{8,24},{9,... | collective-permute-start | bytes 1179656 | tf_op jit(solution)/shard_map/ppermute | solution.py:83
  3.7 18.2 %collective-permute-start.4 = (bf16[256,768]{1,0:T(8,128)(2,1)}, bf16[256,768]{1,0:T(8,128)(2,1)S(1)}, u32[]{:S(2)}, u32[]{:S(2)}) collective-permute-start(bf16[256,768]{1,0:T(8,128)(2,1)} %refs_11_.1), channel_id=1, source_target_pairs={{0,8},{1,9},{2,10},{3,11},{4,12},{5,13},{6,14},{7,15},{8,0},{9,1},... | collective-permute-start | bytes 1179656 | tf_op jit(solution)/shard_map/ppermute | solution.py:83
  5.2 13.3 %collective-permute-start = (bf16[128,768]{1,0:T(8,128)(2,1)}, bf16[128,768]{1,0:T(8,128)(2,1)S(1)}, u32[]{:S(2)}, u32[]{:S(2)}) collective-permute-start(bf16[128,768]{1,0:T(8,128)(2,1)} %refs_0_.5), channel_id=1, source_target_pairs={{0,6},{1,7},{2,12},{3,13},{4,18},{5,19},{6,24},{7,25},{8,4},{9,5},... | collective-permute-start | bytes 589832 | tf_op jit(solution)/shard_map/ppermute | solution.py:89
  8.8 9.7 %collective-permute-start.1 = (bf16[128,768]{1,0:T(8,128)(2,1)}, bf16[128,768]{1,0:T(8,128)(2,1)S(1)}, u32[]{:S(2)}, u32[]{:S(2)}) collective-permute-start(bf16[128,768]{1,0:T(8,128)(2,1)} %refs_0_.5), channel_id=1, source_target_pairs={{0,1},{1,0},{2,10},{3,11},{4,20},{5,21},{6,30},{7,31},{8,2},{9,3},... | collective-permute-start | bytes 589832 | tf_op jit(solution)/shard_map/ppermute | solution.py:89
  18.5 7.8 %collective-permute-start.2 = (bf16[128,768]{1,0:T(8,128)(2,1)S(1)}, bf16[128,768]{1,0:T(8,128)(2,1)S(1)}, u32[]{:S(2)}, u32[]{:S(2)}) collective-permute-start(bf16[128,768]{1,0:T(8,128)(2,1)S(1)} %collective-permute-done.refs_0_), channel_id=1, source_target_pairs={{0,2},{1,3},{2,0},{3,1},{4,6},{5,7},{6,4},{7,5},{8,10},{9,11},{10,... | collective-permute-start | bytes 589832 | tf_op jit(solution)/shard_map/ppermute | solution.py:86
  18.5 10.0 %collective-permute-start.3 = (bf16[128,768]{1,0:T(8,128)(2,1)S(1)}, bf16[128,768]{1,0:T(8,128)(2,1)S(1)}, u32[]{:S(2)}, u32[]{:S(2)}) collective-permute-start(bf16[128,768]{1,0:T(8,128)(2,1)S(1)} %collective-permute-done.1.refs_1_), channel_id=1, source_target_pairs={{0,2},{1,3},{2,0},{3,1},{4,6},{5,7},{6,4},{7,5},{8,10},{9,11},{10,... | collective-permute-start | bytes 589832 | tf_op jit(solution)/shard_map/ppermute | solution.py:86
  20.5 7.9 %collective-permute-start.6 = (bf16[128,768]{1,0:T(8,128)(2,1)S(1)}, bf16[128,768]{1,0:T(8,128)(2,1)S(1)}, u32[]{:S(2)}, u32[]{:S(2)}) collective-permute-start(bf16[128,768]{1,0:T(8,128)(2,1)S(1)} %slice.8), channel_id=1, source_target_pairs={{0,8},{1,9},{2,10},{3,11},{4,12},{5,13},{6,14},{7,15},{8,0},{9,1},... | collective-permute-start | bytes 589832 | tf_op jit(solution)/shard_map/ppermute | solution.py:83
  21.8 7.1 %copy-start.3 = (f32[768]{0:T(1024)S(1)}, f32[768]{0:T(1024)}, u32[]{:S(2)}) copy-start(f32[768]{0:T(1024)} %param.20) | copy-start | bytes 9220
  21.8 6.6 %collective-permute-start.7 = (bf16[128,768]{1,0:T(8,128)(2,1)S(1)}, bf16[128,768]{1,0:T(8,128)(2,1)S(1)}, u32[]{:S(2)}, u32[]{:S(2)}) collective-permute-start(bf16[128,768]{1,0:T(8,128)(2,1)S(1)} %slice.9), channel_id=1, source_target_pairs={{0,16},{1,17},{2,18},{3,19},{4,20},{5,21},{6,22},{7,23},{8,24},{9,... | collective-permute-start | bytes 589832 | tf_op jit(solution)/shard_map/ppermute | solution.py:83
  24.4 4.6 %collective-permute-start.10 = (bf16[128,768]{1,0:T(8,128)(2,1)S(1)}, bf16[128,768]{1,0:T(8,128)(2,1)S(1)}, u32[]{:S(2)}, u32[]{:S(2)}) collective-permute-start(bf16[128,768]{1,0:T(8,128)(2,1)S(1)} %collective-permute-done.refs_0_), channel_id=1, source_target_pairs={{0,1},{1,0},{2,3},{3,2},{4,5},{5,4},{6,7},{7,6},{8,9},{9,8},{10,11... | collective-permute-start | bytes 589832 | tf_op jit(solution)/shard_map/ppermute | solution.py:80
  26.3 2.7 %collective-permute-start.11 = (bf16[128,768]{1,0:T(8,128)(2,1)S(1)}, bf16[128,768]{1,0:T(8,128)(2,1)S(1)}, u32[]{:S(2)}, u32[]{:S(2)}) collective-permute-start(bf16[128,768]{1,0:T(8,128)(2,1)S(1)} %collective-permute-done.1.refs_1_), channel_id=1, source_target_pairs={{0,1},{1,0},{2,3},{3,2},{4,5},{5,4},{6,7},{7,6},{8,9},{9,8},{10,11... | collective-permute-start | bytes 589832 | tf_op jit(solution)/shard_map/ppermute | solution.py:80
  28.4 1.4 %collective-permute-start.8 = (bf16[128,768]{1,0:T(8,128)(2,1)S(1)}, bf16[128,768]{1,0:T(8,128)(2,1)S(1)}, u32[]{:S(2)}, u32[]{:S(2)}) collective-permute-start(bf16[128,768]{1,0:T(8,128)(2,1)S(1)} %collective-permute-done.2.refs_0_), channel_id=1, source_target_pairs={{0,1},{1,0},{2,3},{3,2},{4,5},{5,4},{6,7},{7,6},{8,9},{9,8},{10,11... | collective-permute-start | bytes 589832 | tf_op jit(solution)/shard_map/ppermute | solution.py:80
  28.5 1.7 %collective-permute-start.9 = (bf16[128,768]{1,0:T(8,128)(2,1)S(1)}, bf16[128,768]{1,0:T(8,128)(2,1)S(1)}, u32[]{:S(2)}, u32[]{:S(2)}) collective-permute-start(bf16[128,768]{1,0:T(8,128)(2,1)S(1)} %collective-permute-done.3.refs_1_), channel_id=1, source_target_pairs={{0,1},{1,0},{2,3},{3,2},{4,5},{5,4},{6,7},{7,6},{8,9},{9,8},{10,11... | collective-permute-start | bytes 589832 | tf_op jit(solution)/shard_map/ppermute | solution.py:80
  29.6 4.8 %copy-start = (bf16[256,768]{1,0:T(8,128)(2,1)S(1)}, bf16[256,768]{1,0:T(8,128)(2,1)}, u32[]{:S(2)}) copy-start(bf16[256,768]{1,0:T(8,128)(2,1)} %refs_11_.1) | copy-start | bytes 1179652
  29.6 4.8 %copy-start.2 = (bf16[128,768]{1,0:T(8,128)(2,1)S(1)}, bf16[128,768]{1,0:T(8,128)(2,1)}, u32[]{:S(2)}) copy-start(bf16[128,768]{1,0:T(8,128)(2,1)} %refs_0_.4) | copy-start | bytes 589828
  30.8 8.7 %collective-permute-start.12 = (bf16[768,128]{1,0:T(8,128)(2,1)S(1)}, bf16[768,128]{1,0:T(8,128)(2,1)S(1)}, u32[]{:S(2)}, u32[]{:S(2)}) collective-permute-start(bf16[768,128]{1,0:T(8,128)(2,1)S(1)} %get-tuple-element.54), channel_id=1, source_target_pairs={{0,24},{1,25},{2,26},{3,27},{4,28},{5,29},{6,30},{7,31},{8,16},{9,... | collective-permute-start | bytes 589832 | tf_op jit(solution)/shard_map/ppermute | solution.py:83
  30.9 11.3 %collective-permute-start.13 = (bf16[768,128]{1,0:T(8,128)(2,1)S(1)}, bf16[768,128]{1,0:T(8,128)(2,1)S(1)}, u32[]{:S(2)}, u32[]{:S(2)}) collective-permute-start(bf16[768,128]{1,0:T(8,128)(2,1)S(1)} %get-tuple-element.55), channel_id=1, source_target_pairs={{0,16},{1,17},{2,18},{3,19},{4,20},{5,21},{6,22},{7,23},{8,24},{9,... | collective-permute-start | bytes 589832 | tf_op jit(solution)/shard_map/ppermute | solution.py:83
  32.6 10.4 %collective-permute-start.14 = (bf16[768,128]{1,0:T(8,128)(2,1)S(1)}, bf16[768,128]{1,0:T(8,128)(2,1)S(1)}, u32[]{:S(2)}, u32[]{:S(2)}) collective-permute-start(bf16[768,128]{1,0:T(8,128)(2,1)S(1)} %get-tuple-element.56), channel_id=1, source_target_pairs={{0,8},{1,9},{2,10},{3,11},{4,12},{5,13},{6,14},{7,15},{8,0},{9,1},... | collective-permute-start | bytes 589832 | tf_op jit(solution)/shard_map/ppermute | solution.py:83
  35.1 11.7 %collective-permute-start.18 = (bf16[256,128]{1,0:T(8,128)(2,1)S(1)}, bf16[256,128]{1,0:T(8,128)(2,1)S(1)}, u32[]{:S(2)}, u32[]{:S(2)}) collective-permute-start(bf16[256,128]{1,0:T(8,128)(2,1)S(1)} %get-tuple-element.72), channel_id=1, source_target_pairs={{0,2},{1,3},{2,0},{3,1},{4,6},{5,7},{6,4},{7,5},{8,10},{9,11},{10,... | collective-permute-start | bytes 196616 | tf_op jit(solution)/shard_map/ppermute | solution.py:86
  35.5 13.1 %collective-permute-start.19 = (bf16[256,128]{1,0:T(8,128)(2,1)S(1)}, bf16[256,128]{1,0:T(8,128)(2,1)S(1)}, u32[]{:S(2)}, u32[]{:S(2)}) collective-permute-start(bf16[256,128]{1,0:T(8,128)(2,1)S(1)} %get-tuple-element.73), channel_id=1, source_target_pairs={{0,4},{1,5},{2,6},{3,7},{4,0},{5,1},{6,2},{7,3},{8,12},{9,13},{10,... | collective-permute-start | bytes 196616 | tf_op jit(solution)/shard_map/ppermute | solution.py:86
  39.6 9.0 %collective-permute-start.20 = (bf16[256,128]{1,0:T(8,128)(2,1)S(1)}, bf16[256,128]{1,0:T(8,128)(2,1)S(1)}, u32[]{:S(2)}, u32[]{:S(2)}) collective-permute-start(bf16[256,128]{1,0:T(8,128)(2,1)S(1)} %get-tuple-element.74), channel_id=1, source_target_pairs={{0,6},{1,7},{2,4},{3,5},{4,2},{5,3},{6,0},{7,1},{8,14},{9,15},{10,... | collective-permute-start | bytes 196616 | tf_op jit(solution)/shard_map/ppermute | solution.py:86
  43.0 16.4 %copy-start.1 = (bf16[128,768]{1,0:T(8,128)(2,1)S(1)}, bf16[128,768]{1,0:T(8,128)(2,1)}, u32[]{:S(2)}) copy-start(bf16[128,768]{1,0:T(8,128)(2,1)} %refs_0_.5) | copy-start | bytes 589828
  45.0 4.9 %collective-permute-start.15 = (bf16[144,128]{1,0:T(8,128)(2,1)S(1)}, bf16[144,128]{1,0:T(8,128)(2,1)S(1)}, u32[]{:S(2)}, u32[]{:S(2)}) collective-permute-start(bf16[144,128]{1,0:T(8,128)(2,1)S(1)} %get-tuple-element.64), channel_id=1, source_target_pairs={{0,24},{1,25},{2,26},{3,27},{4,28},{5,29},{6,30},{7,31},{8,16},{9,... | collective-permute-start | bytes 110600 | tf_op jit(solution)/shard_map/ppermute | solution.py:83
  45.4 4.5 %collective-permute-start.16 = (bf16[144,128]{1,0:T(8,128)(2,1)S(1)}, bf16[144,128]{1,0:T(8,128)(2,1)S(1)}, u32[]{:S(2)}, u32[]{:S(2)}) collective-permute-start(bf16[144,128]{1,0:T(8,128)(2,1)S(1)} %get-tuple-element.65), channel_id=1, source_target_pairs={{0,16},{1,17},{2,18},{3,19},{4,20},{5,21},{6,22},{7,23},{8,24},{9,... | collective-permute-start | bytes 110600 | tf_op jit(solution)/shard_map/ppermute | solution.py:83
  46.8 4.0 %collective-permute-start.17 = (bf16[144,128]{1,0:T(8,128)(2,1)S(1)}, bf16[144,128]{1,0:T(8,128)(2,1)S(1)}, u32[]{:S(2)}, u32[]{:S(2)}) collective-permute-start(bf16[144,128]{1,0:T(8,128)(2,1)S(1)} %get-tuple-element.66), channel_id=1, source_target_pairs={{0,8},{1,9},{2,10},{3,11},{4,12},{5,13},{6,14},{7,15},{8,0},{9,1},... | collective-permute-start | bytes 110600 | tf_op jit(solution)/shard_map/ppermute | solution.py:83
  50.9 6.0 %collective-permute-start.23 = (bf16[128,128]{1,0:T(8,128)(2,1)S(1)}, bf16[128,128]{1,0:T(8,128)(2,1)S(1)}, u32[]{:S(2)}, u32[]{:S(2)}) collective-permute-start(bf16[128,128]{1,0:T(8,128)(2,1)S(1)} %get-tuple-element.84.refs_3_), channel_id=1, source_target_pairs={{0,6},{1,7},{2,4},{3,5},{4,2},{5,3},{6,0},{7,1},{8,14},{9,15},{10,... | collective-permute-start | bytes 98312 | tf_op jit(solution)/shard_map/ppermute | solution.py:86
  53.0 4.8 %collective-permute-start.22 = (bf16[128,128]{1,0:T(8,128)(2,1)S(1)}, bf16[128,128]{1,0:T(8,128)(2,1)S(1)}, u32[]{:S(2)}, u32[]{:S(2)}) collective-permute-start(bf16[128,128]{1,0:T(8,128)(2,1)S(1)} %get-tuple-element.84.refs_3_), channel_id=1, source_target_pairs={{0,4},{1,5},{2,6},{3,7},{4,0},{5,1},{6,2},{7,3},{8,12},{9,13},{10,... | collective-permute-start | bytes 98312 | tf_op jit(solution)/shard_map/ppermute | solution.py:86
  54.1 4.1 %collective-permute-start.21 = (bf16[128,128]{1,0:T(8,128)(2,1)S(1)}, bf16[128,128]{1,0:T(8,128)(2,1)S(1)}, u32[]{:S(2)}, u32[]{:S(2)}) collective-permute-start(bf16[128,128]{1,0:T(8,128)(2,1)S(1)} %get-tuple-element.84.refs_3_), channel_id=1, source_target_pairs={{0,2},{1,3},{2,0},{3,1},{4,6},{5,7},{6,4},{7,5},{8,10},{9,11},{10,... | collective-permute-start | bytes 98312 | tf_op jit(solution)/shard_map/ppermute | solution.py:86
  55.3 4.1 %collective-permute-start.24 = (bf16[256,128]{1,0:T(8,128)(2,1)S(1)}, bf16[256,128]{1,0:T(8,128)(2,1)S(1)}, u32[]{:S(2)}, u32[]{:S(2)}) collective-permute-start(bf16[256,128]{1,0:T(8,128)(2,1)S(1)} %get-tuple-element.85), channel_id=1, source_target_pairs={{0,1},{1,0},{2,3},{3,2},{4,5},{5,4},{6,7},{7,6},{8,9},{9,8},{10,11... | collective-permute-start | bytes 196616 | tf_op jit(solution)/shard_map/ppermute | solution.py:80
  56.9 1.5 %collective-permute-start.27 = (bf16[128,128]{1,0:T(8,128)(2,1)S(1)}, bf16[128,128]{1,0:T(8,128)(2,1)S(1)}, u32[]{:S(2)}, u32[]{:S(2)}) collective-permute-start(bf16[128,128]{1,0:T(8,128)(2,1)S(1)} %collective-permute-done.23.refs_6_), channel_id=1, source_target_pairs={{0,1},{1,0},{2,3},{3,2},{4,5},{5,4},{6,7},{7,6},{8,9},{9,8},{10,11... | collective-permute-start | bytes 98312 | tf_op jit(solution)/shard_map/ppermute | solution.py:80
  57.9 1.2 %collective-permute-start.26 = (bf16[128,128]{1,0:T(8,128)(2,1)S(1)}, bf16[128,128]{1,0:T(8,128)(2,1)S(1)}, u32[]{:S(2)}, u32[]{:S(2)}) collective-permute-start(bf16[128,128]{1,0:T(8,128)(2,1)S(1)} %collective-permute-done.22.refs_5_), channel_id=1, source_target_pairs={{0,1},{1,0},{2,3},{3,2},{4,5},{5,4},{6,7},{7,6},{8,9},{9,8},{10,11... | collective-permute-start | bytes 98312 | tf_op jit(solution)/shard_map/ppermute | solution.py:80
  58.2 1.2 %collective-permute-start.25 = (bf16[128,128]{1,0:T(8,128)(2,1)S(1)}, bf16[128,128]{1,0:T(8,128)(2,1)S(1)}, u32[]{:S(2)}, u32[]{:S(2)}) collective-permute-start(bf16[128,128]{1,0:T(8,128)(2,1)S(1)} %collective-permute-done.21.refs_4_), channel_id=1, source_target_pairs={{0,1},{1,0},{2,3},{3,2},{4,5},{5,4},{6,7},{7,6},{8,9},{9,8},{10,11... | collective-permute-start | bytes 98312 | tf_op jit(solution)/shard_map/ppermute | solution.py:80
